TPU v7x, 32 devices: a whole 2x2x4 slice. The times are simulated.
32 devices in a mesh: dp: 8 (over z, x), mp: 4 (over y, core).
Axes of the slice: x: 2, y: 2, z: 4, core: 2. Of those that a mesh axis runs over, the one named last changes fastest.
Arguments:
- tokens: bfloat16 [16384, 768], P('dp'), may hold values from -6 to 6
- w_qkv: bfloat16 [3, 768, 768], P(None, None, 'mp'), may hold values from -0.21875 to 0.21875
- b_qv: float32 [2, 768], P(None, 'mp'), may hold values from -2 to 2
- w_out: bfloat16 [768, 768], P('mp'), may hold values from -0.875 to 0.875
- b_out: float32 [768], replicated, may hold values from -2 to 2
- norm1_gain: float32 [768], replicated, may hold values from 0.5 to 1.5
- norm1_shift: float32 [768], replicated, may hold values from -1.5 to 1.5
- w_in: bfloat16 [768, 3072], P(None, 'mp'), may hold values from -0.21875 to 0.21875
- b_in: float32 [3072], P('mp'), may hold values from -2 to 2
- w_back: bfloat16 [3072, 768], P('mp'), may hold values from -0.15625 to 0.15625
- b_back: float32 [768], replicated, may hold values from -1.5 to 1.5
- norm2_gain: float32 [768], replicated, may hold values from 0.5 to 1.5
- norm2_shift: float32 [768], replicated, may hold values from -0.4 to 0.4
- segment_ids: int32 [32, 512], P('dp'), may hold values from 0 to 15, never falling along the last dimension, each value on 1 to 64 neighbouring positions
- pair_ids: int32 [32, 8], P('dp'), may hold values from 0 to 255
Outputs:
- loss: float32 [], replicated
- layer_out: bfloat16 [16384, 768], P('dp')
- d_tokens: bfloat16 [16384, 768], P('dp')
- d_w_qkv: float32 [3, 768, 768], P(None, None, 'mp')
- d_b_qv: float32 [2, 768], P(None, 'mp')
- d_w_out: float32 [768, 768], P('mp')
- d_b_out: float32 [768], P('mp')
- d_norm1_gain: float32 [768], P('mp')
- d_norm1_shift: float32 [768], P('mp')
- d_w_in: float32 [768, 3072], P(None, 'mp')
- d_b_in: float32 [3072], P('mp')
- d_w_back: float32 [3072, 768], P('mp')
- d_b_back: float32 [768], P('mp')
- d_norm2_gain: float32 [768], P('mp')
- d_norm2_shift: float32 [768], P('mp')
Inputs may be any that keep to these rules, and one draw needn't show every extreme that they name: `segment_ids`: in every row segment numbers never fall and each of the 16 texts has 1 to 64 positions.
All inputs are finite; a program needn't handle non-finite values.
Results may differ from a plain program's by a relative error of at most 0.02865.
Values may be sent and summed in bfloat16 or wider, within the bound.
No kernel may reach another device: no remote copies, remote signals or barrier semaphores. Data moves between devices by JAX's collectives and lax.ppermute only.
A program may use at most 128 MiB of HBM per device.

v0:
```python
import jax
import jax.numpy as jnp
from jax import lax
from jax.sharding import PartitionSpec as P

HEAD_DIM = 64


norm_eps = 1e-06
inv_temp = 50.0
loss_scale = 8.0
highest = lax.Precision.HIGHEST
masked_score = -1000000000.0


def layer_norm(values, gain_vec, shift_vec):
    center = values - jnp.mean(values, axis=-1, keepdims=True)
    spread = jnp.mean(center * center, axis=-1, keepdims=True)
    return center * lax.rsqrt(spread + norm_eps) * gain_vec + shift_vec


def exact_gelu(values):
    return jax.nn.gelu(values, approximate=False)


def product(left_side, right_side):
    return jnp.dot(left_side, right_side, preferred_element_type=jnp.float32)


def product_t(left_side, right_side):
    return lax.dot_general(
        left_side, right_side, (((0,), (0,)), ((), ())), preferred_element_type=jnp.float32
    )


def product_nt(left_side, right_side):
    return lax.dot_general(
        left_side, right_side, (((1,), (1,)), ((), ())), preferred_element_type=jnp.float32
    )


def head_scores(query_heads, key_heads, segment):
    score_scale = HEAD_DIM ** (-0.5)
    scores = (
        jnp.einsum("qhd,khd->hqk", query_heads, key_heads, preferred_element_type=jnp.float32)
        * score_scale
    )
    same_segment = (segment[:, None] == segment[None, :])[None]
    return jnp.where(same_segment, scores, masked_score)


def row_forward(inputs):
    query_rows, key_rows, value_rows, segment = inputs
    length = query_rows.shape[0]
    head_count = query_rows.shape[1] // HEAD_DIM
    query_heads = query_rows.reshape(length, head_count, HEAD_DIM)
    key_heads = key_rows.reshape(length, head_count, HEAD_DIM)
    value_heads = value_rows.reshape(length, head_count, HEAD_DIM)
    scores = head_scores(query_heads, key_heads, segment)
    row_best = jnp.max(scores, axis=-1, keepdims=True)
    weights = jnp.exp(scores - row_best)
    row_total = jnp.sum(weights, axis=-1, keepdims=True)
    weights_low = (weights / row_total).astype(jnp.bfloat16)
    context = jnp.einsum(
        "hqk,khd->qhd", weights_low, value_heads, preferred_element_type=jnp.float32
    )
    log_total = row_best[..., 0] + jnp.log(row_total[..., 0])
    return (context.reshape(length, head_count * HEAD_DIM).astype(jnp.bfloat16), log_total)


def row_backward(inputs):
    query_rows, key_rows, value_rows, segment, log_total, grad_context = inputs
    length = query_rows.shape[0]
    head_count = query_rows.shape[1] // HEAD_DIM
    score_scale = HEAD_DIM ** (-0.5)
    query_heads = query_rows.reshape(length, head_count, HEAD_DIM)
    key_heads = key_rows.reshape(length, head_count, HEAD_DIM)
    value_heads = value_rows.reshape(length, head_count, HEAD_DIM)
    grad_heads = grad_context.reshape(length, head_count, HEAD_DIM)
    scores = head_scores(query_heads, key_heads, segment)
    probability = jnp.exp(scores - log_total[..., None])
    grad_probs = jnp.einsum(
        "qhd,khd->hqk", grad_heads, value_heads, preferred_element_type=jnp.float32
    )
    inner_term = jnp.sum(probability * grad_probs, axis=-1, keepdims=True)
    grad_scores = (probability * (grad_probs - inner_term)).astype(jnp.bfloat16)
    grad_query = (
        jnp.einsum("hqk,khd->qhd", grad_scores, key_heads, preferred_element_type=jnp.float32)
        * score_scale
    )
    grad_key = (
        jnp.einsum("hqk,qhd->khd", grad_scores, query_heads, preferred_element_type=jnp.float32)
        * score_scale
    )
    grad_value = jnp.einsum(
        "hqk,qhd->khd",
        probability.astype(jnp.bfloat16),
        grad_heads,
        preferred_element_type=jnp.float32,
    )
    local_width = head_count * HEAD_DIM
    return (
        grad_query.reshape(length, local_width).astype(jnp.bfloat16),
        grad_key.reshape(length, local_width).astype(jnp.bfloat16),
        grad_value.reshape(length, local_width).astype(jnp.bfloat16),
    )


def shards(
    tokens,
    w_qkv,
    b_qv,
    w_out,
    b_out,
    norm1_gain,
    norm1_shift,
    w_in,
    b_in,
    w_back,
    b_back,
    norm2_gain,
    norm2_shift,
    segment_ids,
    pair_ids,
):
    row_count, row_length = segment_ids.shape
    model_width = tokens.shape[1]
    local_width = w_out.shape[0]
    share_width = model_width // lax.axis_size("mp")

    def own_share(vector):
        return lax.dynamic_slice_in_dim(vector, lax.axis_index("mp") * share_width, share_width)

    def by_rows(flat_array):
        return flat_array.reshape(row_count, row_length, flat_array.shape[-1])

    bias_rows = jnp.stack([b_qv[0], jnp.zeros_like(b_qv[0]), b_qv[1]])[:, None, :]
    qkv_rows = (
        jnp.einsum("td,cde->cte", tokens, w_qkv, preferred_element_type=jnp.float32) + bias_rows
    ).astype(jnp.bfloat16)
    context, log_totals = lax.map(
        row_forward, (by_rows(qkv_rows[0]), by_rows(qkv_rows[1]), by_rows(qkv_rows[2]), segment_ids)
    )
    context = context.reshape(-1, local_width)
    attn_sum = lax.psum(product(context, w_out).astype(jnp.bfloat16), "mp").astype(jnp.float32)
    resid1 = tokens.astype(jnp.float32) + attn_sum + b_out
    normed1, norm1_pull = jax.vjp(layer_norm, resid1, norm1_gain, norm1_shift)
    rounded1 = normed1.astype(jnp.bfloat16)
    before = product(rounded1, w_in) + b_in
    active_full, gelu_pull = jax.vjp(exact_gelu, before)
    active = active_full.astype(jnp.bfloat16)
    ffn_sum = lax.psum(product(active, w_back).astype(jnp.bfloat16), "mp").astype(jnp.float32)
    resid2 = normed1 + ffn_sum + b_back
    normed2, norm2_pull = jax.vjp(layer_norm, resid2, norm2_gain, norm2_shift)
    layer_out = normed2.astype(jnp.bfloat16)
    slot_ids = jnp.arange(2 * pair_ids.shape[1], dtype=jnp.int32)
    member_mask = segment_ids[:, None, :] == slot_ids[None, :, None]
    lengths = jnp.sum(member_mask.astype(jnp.float32), axis=-1)
    pooled = (
        jnp.einsum(
            "rst,rtd->rsd",
            member_mask.astype(jnp.bfloat16),
            layer_out.reshape(row_count, row_length, model_width),
            preferred_element_type=jnp.float32,
        )
        / lengths[..., None]
    )
    inverse = lax.rsqrt(jnp.sum(pooled * pooled, axis=-1, keepdims=True) + norm_eps)
    unit_vecs = (pooled * inverse).astype(jnp.bfloat16)
    query_vecs = unit_vecs[:, 0::2].reshape(-1, model_width)
    passage_vecs = unit_vecs[:, 1::2].reshape(-1, model_width)
    targets = pair_ids.reshape(-1)
    query_count = targets.shape[0]
    passage_count = passage_vecs.shape[0]
    own_ids = lax.axis_index("dp") * passage_count + jnp.arange(passage_count, dtype=jnp.int32)

    def score_block(passages):
        scores = product_nt(query_vecs, passages) * inv_temp
        positive_mask = jnp.arange(passages.shape[0], dtype=jnp.int32)[None, :] == targets[:, None]
        return (scores, positive_mask)

    def score_grads(scores, positive_mask, log_rows):
        return (
            (jnp.exp(scores - log_rows[:, None]) - positive_mask.astype(jnp.float32))
            * (loss_scale * inv_temp)
        ).astype(jnp.bfloat16)

    row_best = jnp.full((query_count,), -1e30, jnp.float32)
    scores, positive_mask = score_block(lax.all_gather(passage_vecs, "dp", axis=0, tiled=True))
    new_best = jnp.maximum(row_best, jnp.max(scores, axis=1))
    row_total = jnp.sum(jnp.exp(scores - new_best[:, None]), axis=1)
    positive = jnp.sum(jnp.where(positive_mask, scores, 0.0), axis=1)
    row_best, row_total, positive = (new_best, row_total, positive)
    log_total = row_best + jnp.log(row_total)
    per_query = log_total - positive
    loss_part = jnp.sum(per_query)
    incoming = lax.all_gather(passage_vecs, "dp", axis=0, tiled=True)
    scores, positive_mask = score_block(incoming)
    grad_query = product(score_grads(scores, positive_mask, log_total), incoming)
    incoming = (
        lax.all_gather(query_vecs.astype(jnp.float32), "dp", axis=0, tiled=True),
        lax.all_gather(log_total, "dp", axis=0, tiled=True),
        lax.all_gather(targets, "dp", axis=0, tiled=True),
    )
    other_queries = incoming[0].astype(jnp.bfloat16)
    scores = product_nt(other_queries, passage_vecs) * inv_temp
    positive_mask = own_ids[None, :] == incoming[2][:, None]
    grad_passage = product_t(score_grads(scores, positive_mask, incoming[1]), other_queries)
    grad_unit = jnp.stack(
        [
            grad_query.reshape(row_count, -1, model_width),
            grad_passage.reshape(row_count, -1, model_width),
        ],
        axis=2,
    ).reshape(row_count, -1, model_width)
    inner_term = jnp.sum(pooled * grad_unit, axis=-1, keepdims=True)
    grad_pooled = inverse * grad_unit - inverse * inverse * inverse * pooled * inner_term
    grad_out = jnp.einsum(
        "rst,rsd->rtd",
        member_mask.astype(jnp.float32),
        grad_pooled / lengths[..., None],
        precision=highest,
    ).reshape(-1, model_width)
    grad_resid2, grad_gain2, grad_shift2 = norm2_pull(grad_out)
    grad_b_back = jnp.sum(grad_resid2, axis=0)
    grad_ffn = grad_resid2.astype(jnp.bfloat16)
    grad_w_back = product_t(active, grad_ffn)
    grad_active = product_nt(grad_ffn, w_back)
    grad_before = gelu_pull(grad_active)[0].astype(jnp.bfloat16)
    grad_b_in = jnp.sum(grad_before.astype(jnp.float32), axis=0)
    grad_w_in = product_t(rounded1, grad_before)
    ffn_summed = (
        grad_w_in,
        grad_b_in,
        grad_w_back,
        own_share(grad_b_back),
        own_share(grad_gain2),
        own_share(grad_shift2),
        loss_part,
    )
    grad_normed1 = grad_resid2 + lax.psum(
        product_nt(grad_before, w_in).astype(jnp.bfloat16), "mp"
    ).astype(jnp.float32)
    grad_resid1, grad_gain1, grad_shift1 = norm1_pull(grad_normed1)
    grad_b_out = jnp.sum(grad_resid1, axis=0)
    grad_attn = grad_resid1.astype(jnp.bfloat16)
    grad_w_out = product_t(context, grad_attn)
    grad_context = product_nt(grad_attn, w_out).astype(jnp.bfloat16)
    grad_q, grad_k, grad_v = lax.map(
        row_backward,
        (
            by_rows(qkv_rows[0]),
            by_rows(qkv_rows[1]),
            by_rows(qkv_rows[2]),
            segment_ids,
            log_totals,
            by_rows(grad_context),
        ),
    )
    grad_qkv = jnp.stack([grad_q, grad_k, grad_v]).reshape(3, -1, local_width)
    grad_w_qkv = jnp.einsum("td,cte->cde", tokens, grad_qkv, preferred_element_type=jnp.float32)
    grad_b_qv = jnp.stack(
        [
            jnp.sum(grad_qkv[0].astype(jnp.float32), axis=0),
            jnp.sum(grad_qkv[2].astype(jnp.float32), axis=0),
        ]
    )
    grad_tokens = grad_resid1 + lax.psum(
        jnp.einsum("cte,cde->td", grad_qkv, w_qkv, preferred_element_type=jnp.float32).astype(
            jnp.bfloat16
        ),
        "mp",
    ).astype(jnp.float32)
    every_sum = lax.psum(
        (
            ffn_summed[0],
            ffn_summed[1],
            ffn_summed[2],
            ffn_summed[3],
            ffn_summed[4],
            ffn_summed[5],
            ffn_summed[6],
            grad_w_qkv,
            grad_b_qv,
            grad_w_out,
            own_share(grad_b_out),
            own_share(grad_gain1),
            own_share(grad_shift1),
        ),
        "dp",
    )
    ffn_summed = every_sum[:7]
    attn_summed = every_sum[7:]
    loss = ffn_summed[6] / (query_count * lax.axis_size("dp"))
    return (
        loss,
        layer_out,
        grad_tokens.astype(jnp.bfloat16),
        attn_summed[0],
        attn_summed[1],
        attn_summed[2],
        attn_summed[3],
        attn_summed[4],
        attn_summed[5],
        ffn_summed[0],
        ffn_summed[1],
        ffn_summed[2],
        ffn_summed[3],
        ffn_summed[4],
        ffn_summed[5],
    )


def solution(mesh):
    return jax.shard_map(
        shards,
        mesh=mesh,
        in_specs=(
            P("dp", None),
            P(None, None, "mp"),
            P(None, "mp"),
            P("mp", None),
            P(),
            P(),
            P(),
            P(None, "mp"),
            P("mp"),
            P("mp", None),
            P(),
            P(),
            P(),
            P("dp", None),
            P("dp", None),
        ),
        out_specs=(
            P(),
            P("dp", None),
            P("dp", None),
            P(None, None, "mp"),
            P(None, "mp"),
            P("mp", None),
            P("mp"),
            P("mp"),
            P("mp"),
            P(None, "mp"),
            P("mp"),
            P("mp", None),
            P("mp"),
            P("mp"),
            P("mp"),
        ),
        check_vma=False,
    )
```

profile of v0, /device:TPU:0, one launch (start us, length us, event | category | flops | bytes accessed | tf_op | source)
XLA Modules:
  0.0 819.5 jit_solution(261729055483690632)
XLA Ops:
  8.2 4.2 fusion.29
  12.6 1.5 reshape_squeeze.12
  14.0 1.3 copy.67
  15.3 1.5 reshape_squeeze.13
  16.7 1.3 copy.68
  18.0 1.5 reshape_squeeze.14
  19.5 1.3 copy.69
  21.7 16.6 %while.26 = (s32[]{:T(128)}, bf16[4,512,192]{1,2,0:T(8,128)(2,1)}, f32[4,3,512]{2,1,0:T(4,128)}, bf16[4,512,192]{1,2,0:T(8,128)(2,1)S(1)}, s32[4,512]{1,0:T(4,12...) while((s32[]{:T(128)}, bf16[4,512,192]{1,2,0:T(8,128)(2,1)}, ...), condition=%wide.region_3.4_spmd, body=%wide.region_0.3_spmd.sunk | while | flops 211122688 | bytes 12903521 | solution.py:141
  38.3 1.2 copy.85
  40.5 3.7 convolution_convert_fusion.2
  44.7 70.8 %all-reduce.10.cloned.1.call-done = bf16[2048,768]{1,0:T(8,128)(2,1)} async-done(((bf16[2048,768]{1,0:T(8,128)(2,1)}), bf16[2048,768]{1,0:T(8,128)(2,1)}) %all-reduce.10.cloned.1.call-update) | async-done | bytes 3145744 | tf_op jit(solution)/shard_map/psum | solution.py:145
  115.5 4.1 fusion.21
  120.1 2.4 multiply_reduce_fusion.5
  123.2 19.4 %multiply_convert_fusion.1 = (bf16[2048,768]{1,0:T(8,128)(2,1)S(1)}, f32[2048,768]{1,0:T(8,128)}, f32[2048,768]{1,0:T(8,128)}) fusion(f32[768]{0:T(1024)} %param.27, bf16[768,768]{1,0:T(8,128)(2,1)S(1)} %copy-done, f32[768]{0:T(1024)} %param.25, f32[768]{0:T(1024)} %param.24, f32[2048]{0:T(1024)S(1)} %fusion.65, f32[2048]{0:T(1024)S(1)} %broadcast_multiply_fusion.1, ...), kind=kOutput, calls=%fused_computation.54 | convolution fusion | flops 2533883904 | bytes 23228416 | tf_op jit(solution)/shard_map/dot_general | solution.py:27
  142.6 1.7 copy-done.51
  144.3 3.9 convolution_convert_fusion.1
  148.3 1.3 reshape.343
  149.6 1.2 dynamic-slice.8
  152.1 1.3 dynamic-update-slice.1
  153.4 12.0 %all-reduce.1 = s32[256]{0:T(256)} all-reduce(s32[256]{0:T(256)} %dynamic-update-slice.1), channel_id=1, replica_groups=mesh['dp'=8,'mp'=4] {'dp'}, use_global_device_ids=true, to_apply=%add.1 | all-reduce | flops 256 | bytes 2048
  166.6 50.4 %all-reduce.12.cloned.1.call-done = bf16[2048,768]{1,0:T(8,128)(2,1)} async-done(((bf16[2048,768]{1,0:T(8,128)(2,1)}), bf16[2048,768]{1,0:T(8,128)(2,1)}) %all-reduce.12.cloned.1.call-update) | async-done | bytes 3145744 | tf_op jit(solution)/shard_map/psum | solution.py:152
  217.0 5.4 fusion.85
  225.1 1.7 copy-done.12
  229.3 1.6 slice.34
  230.8 1.6 slice.33
  232.4 31.3 %all_gather.13 = bf16[256,768]{1,0:T(8,128)(2,1)S(1)} all-gather(bf16[32,768]{1,0:T(8,128)(2,1)} %bitcast.197), channel_id=1, replica_groups=mesh['dp'=8,'mp'=4] {'dp'}, dimensions={0}, use_global_device_ids=true | all-gather | bytes 442368 | tf_op jit(solution)/shard_map/all_gather | solution.py:189
  263.7 1.2 fusion.89
  264.9 1.4 select_reduce_fusion
  268.5 22.1 %all-reduce = f32[256]{0:T(256)} all-reduce(f32[256]{0:T(256)} %copy-done.45), channel_id=1, replica_groups=mesh['dp'=8,'mp'=4] {'dp'}, use_global_device_ids=true, to_apply=%add | all-reduce | flops 256 | bytes 2048
  290.6 33.3 %all_gather.14 = bf16[256,768]{1,0:T(8,128)(2,1)} all-gather(bf16[32,768]{1,0:T(8,128)(2,1)} %bitcast.198), channel_id=1, replica_groups=mesh['dp'=8,'mp'=4] {'dp'}, dimensions={0}, use_global_device_ids=true | all-gather | bytes 442368 | tf_op jit(solution)/shard_map/all_gather | solution.py:201
  324.0 2.3 convolution_bitcast_fusion
  327.3 1.8 pad_maximum_fusion
  329.0 1.7 reshape.337
  330.8 1.3 multiply_reduce_fusion.6
  332.0 5.0 fusion.90
  337.1 3.2 fusion.14
  340.4 3.3 fusion.83
  343.7 9.4 %convert_reduce_fusion = (f32[768]{0:T(1024)}, bf16[2048,768]{1,0:T(8,128)(2,1)S(1)}) fusion(f32[2048,768]{1,0:T(8,128)S(1)} %bitcast.202, bf16[768,768]{1,0:T(8,128)(2,1)S(1)} %copy-done.48, f32[2048,768]{1,0:T(8,128)S(1)} %get-tuple-element.221, f32[2048]{0:T(1024)S(1)} %negate_multiply_fusion.2, f32[2048,768]{1,0:T(8,128)} %get-tuple-element.245, ...), kind=kOutput, calls=%fused_computation.44 | convolution fusion | flops 2445802752 | bytes 23214080 | tf_op jit(solution)/shard_map/dot_general | solution.py:37
  353.2 1.6 copy-done.50
  354.8 4.0 convolution_convert_fusion
  359.1 9.2 %fusion.75 = f32[768,768]{1,0:T(8,128)} fusion(bf16[2048,768]{1,0:T(8,128)(2,1)} %copy-done.50, f32[768]{0:T(1024)} %param.25, f32[768]{0:T(1024)} %param.24, f32[2048]{0:T(1024)} %copy-done.24, bf16[2048,768]{1,0:T(8,128)(2,1)} %all-reduce.10.cloned.1.call-done, bf16[2048,768]{1,0:T(8,128)(2,1)} %param.19, f32[2048]{0:T(1024)S(1)} %broadcast_multiply_fusion.1, ...), kind=kOutput, calls=%fused_computation.165 | convolution fusion | flops 2430074880 | bytes 11822080 | tf_op jit(solution)/shard_map/dot_general | solution.py:31
  368.3 55.5 %all-reduce.14.cloned.1.call-done = bf16[2048,768]{1,0:T(8,128)(2,1)} async-done(((bf16[2048,768]{1,0:T(8,128)(2,1)}), bf16[2048,768]{1,0:T(8,128)(2,1)}) %all-reduce.14.cloned.1.call-update) | async-done | bytes 3145744 | tf_op jit(solution)/shard_map/psum | solution.py:241
  423.8 9.4 %multiply_reduce_fusion.1 = (f32[768]{0:T(1024)S(1)}, f32[2048]{0:T(1024)S(1)}, f32[768]{0:T(1024)S(1)}, f32[768]{0:T(1024)S(1)}) fusion(f32[2048]{0:T(1024)S(1)} %copy-done.25, bf16[2048,768]{1,0:T(8,128)(2,1)} %all-reduce.14.cloned.1.call-done, f32[2048,768]{1,0:T(8,128)} %copy-done.10, f32[2048]{0:T(1024)S(1)} %copy-done.31, ...), kind=kLoop, calls=%fused_computation.45 | loop fusion | flops 25161472 | bytes 15776768 | tf_op jit(solution)/shard_map/transpose(jvp())/reduce_sum | solution.py:19
  433.3 6.0 fusion.82
  439.4 2.6 copy-done.4
  442.0 1.4 convolution_convert_fusion.3
  447.2 30.9 %while.27 = (s32[]{:T(128)}, bf16[4,512,192]{1,2,0:T(8,128)(2,1)}, bf16[4,512,192]{1,2,0:T(8,128)(2,1)}, bf16[4,512,192]{1,2,0:T(8,128)(2,1)}, bf16[4,512,192]{1...) while((s32[]{:T(128)}, bf16[4,512,192]{1,2,0:T(8,128)(2,1)}, ...), condition=%wide.region_25.26_spmd, body=%wide.region_23.25_spmd.sunk | while | flops 511146496 | bytes 28873860 | solution.py:249
  449.8 1.2 multiply_reduce_fusion.9
  457.4 1.2 multiply_reduce_fusion.9
  478.1 1.8 copy.77
  481.4 1.7 copy.78
  486.9 6.2 bitcast_convert_fusion
  493.2 8.0 fusion.72
  501.1 4.7 fusion.74
  505.9 3.2 fusion.32
  511.5 1.4 convert_reduce_fusion.1
  512.9 48.9 %all-reduce.16.cloned.1.call-done = bf16[2048,768]{1,0:T(8,128)(2,1)} async-done(((bf16[2048,768]{1,0:T(8,128)(2,1)}), bf16[2048,768]{1,0:T(8,128)(2,1)}) %all-reduce.16.cloned.1.call-update) | async-done | bytes 3145744 | tf_op jit(solution)/shard_map/psum | solution.py:268
  561.8 5.4 add_convert_fusion
  567.3 39.6 %all-reduce.2 = (f32[]{:T(128)}, f32[2,192]{1,0:T(2,128)}, f32[192]{0:T(256)}, f32[192]{0:T(256)}, f32[192]{0:T(256)}, /*index=5*/f32[768]{0:T(1024)}, f32[192]{0:T(256)}, f32[192]{0:T(256)}, f32[192]{0:T(256)}) all-reduce(f32[]{:T(128)} %subtract_reduce_fusion, ...), channel_id=1, replica_groups=mesh['dp'=8,'mp'=4] {'dp'}, use_global_device_ids=true, to_apply=%region_16.17 | all-reduce | flops 2305 | bytes 18440 | tf_op jit(solution)/shard_map/psum | solution.py:274
  607.6 196.2 %all-reduce.18.cloned.1.call-done = (f32[3,768,192]{1,2,0:T(8,128)}, f32[192,768]{1,0:T(8,128)}, f32[768,768]{1,0:T(8,128)}, f32[768,768]{1,0:T(8,128)}) async-done(((f32[3,768,192]{1,2,0:T(8,128)}, f32[192,768]{1,0:T(8,128)}, f32[768,768]{1,0:T(8,128)}, f32[768,768]{1,0:T(8,128)}), (f32[3,768,192]{1,2,0:T(8,128)}, f32[192,768]{1,0:T(8,128)}, f32[768,768]{1,0:T(8,128)}, ...) | async-done | bytes 7077904 | tf_op jit(solution)/shard_map/psum | solution.py:274
  803.7 2.9 copy.126
  806.7 1.9 copy.127
  808.6 1.4 copy.128
  810.0 1.4 copy.129
  (256 shorter events, 71.4 us)
Async XLA Ops:
  7.2 116.0 %copy-start = (bf16[768,768]{1,0:T(8,128)(2,1)S(1)}, bf16[768,768]{1,0:T(8,128)(2,1)}, u32[]{:S(2)}) copy-start(bf16[768,768]{1,0:T(8,128)(2,1)} %param.26) | copy-start | bytes 3538948
  7.2 108.3 %all-reduce.10.cloned.1.call-start = ((), (), s32[]{:S(2)}) async-start(), calls=%async_computation | async-start | bytes 6291456 | tf_op jit(solution)/shard_map/psum | solution.py:145
  12.6 9.1 %copy-start.21 = (s32[4,512]{1,0:T(4,128)S(1)}, s32[4,512]{1,0:T(4,128)}, u32[]{:S(2)}) copy-start(s32[4,512]{1,0:T(4,128)} %param.32) | copy-start | bytes 24580
  38.3 77.2 %copy-start.28 = (f32[768]{0:T(1024)S(1)}, f32[768]{0:T(1024)}, u32[]{:S(2)}) copy-start(f32[768]{0:T(1024)} %param.23) | copy-start | bytes 9220
  39.5 0.9 copy-start.13
  44.2 172.9 %all-reduce.12.cloned.1.call-start = ((), (), s32[]{:S(2)}) async-start(), calls=%async_computation.1 | async-start | bytes 6291456 | tf_op jit(solution)/shard_map/psum | solution.py:152
  115.4 4.1 copy-start.5
  115.5 4.7 copy-start.8
  122.6 0.6 copy-start.32
  123.2 19.4 %copy-start.24 = (f32[2048]{0:T(1024)}, f32[2048]{0:T(1024)S(1)}, u32[]{:S(2)}) copy-start(f32[2048]{0:T(1024)S(1)} %fusion.65) | copy-start | bytes 24580
  123.2 21.1 %copy-start.47 = (bf16[768,768]{1,0:T(8,128)(2,1)S(1)}, bf16[768,768]{1,0:T(8,128)(2,1)}, u32[]{:S(2)}) copy-start(bf16[768,768]{1,0:T(8,128)(2,1)} %param.28) | copy-start | bytes 3538948
  142.6 1.7 copy-start.51
  148.3 275.5 %all-reduce.14.cloned.1.call-start = ((), (), s32[]{:S(2)}) async-start(), calls=%async_computation.2 | async-start | bytes 6291456 | tf_op jit(solution)/shard_map/psum | solution.py:241
  222.4 2.7 copy-start.2
  222.4 0.9 copy-start.37
  222.4 0.9 copy-start.41
  222.4 2.6 copy-start.22
  223.3 4.0 copy-start.34
  223.3 3.4 copy-start.39
  223.4 4.0 copy-start.26
  225.1 1.7 copy-start.12
  227.3 0.7 copy-start.16
  228.0 0.6 copy-start.40
  266.3 0.6 copy-start.45
  266.9 1.6 copy-start.43
  330.8 6.3 copy-start.3
  330.8 6.3 copy-start.23
  330.8 6.3 copy-start.27
  330.8 6.3 copy-start.38
  337.1 3.2 copy-start.35
  337.1 6.6 slice-start
  340.3 3.4 copy-start.48
  340.3 3.4 copy-start.49
  340.4 3.4 slice-start.1
  343.7 9.5 %copy-start.10 = (f32[2048,768]{1,0:T(8,128)}, f32[2048,768]{1,0:T(8,128)S(1)}, u32[]{:S(2)}) copy-start(f32[2048,768]{1,0:T(8,128)S(1)} %get-tuple-element.221) | copy-start | bytes 18874372
  343.7 9.5 %copy-start.30 = (f32[2048]{0:T(1024)}, f32[2048]{0:T(1024)S(1)}, u32[]{:S(2)}) copy-start(f32[2048]{0:T(1024)S(1)} %negate_multiply_fusion.2) | copy-start | bytes 24580
  353.2 1.6 copy-start.50
  358.8 203.0 %all-reduce.16.cloned.1.call-start = ((), (), s32[]{:S(2)}) async-start(), calls=%async_computation.3 | async-start | bytes 6291456 | tf_op jit(solution)/shard_map/psum | solution.py:268
  359.1 64.7 %copy-start.25 = (f32[2048]{0:T(1024)S(1)}, f32[2048]{0:T(1024)}, u32[]{:S(2)}) copy-start(f32[2048]{0:T(1024)} %copy-done.24) | copy-start | bytes 24580
  359.1 64.7 %copy-start.29 = (f32[768]{0:T(1024)S(1)}, f32[768]{0:T(1024)}, u32[]{:S(2)}) copy-start(f32[768]{0:T(1024)} %param.23) | copy-start | bytes 9220
  359.1 64.7 %copy-start.31 = (f32[2048]{0:T(1024)S(1)}, f32[2048]{0:T(1024)}, u32[]{:S(2)}) copy-start(f32[2048]{0:T(1024)} %copy-done.30) | copy-start | bytes 24580
  359.1 64.7 %copy-start.36 = (f32[768]{0:T(1024)S(1)}, f32[768]{0:T(1024)}, u32[]{:S(2)}) copy-start(f32[768]{0:T(1024)} %param.24) | copy-start | bytes 9220
  368.3 65.0 %copy-start.33 = (f32[2048]{0:T(1024)S(1)}, f32[2048]{0:T(1024)}, u32[]{:S(2)}) copy-start(f32[2048]{0:T(1024)} %copy-done.32) | copy-start | bytes 24580
  423.8 9.5 %copy-start.6 = (bf16[2048,768]{1,0:T(8,128)(2,1)S(1)}, bf16[2048,768]{1,0:T(8,128)(2,1)}, u32[]{:S(2)}) copy-start(bf16[2048,768]{1,0:T(8,128)(2,1)} %param.19) | copy-start | bytes 9437188
  423.8 9.5 %copy-start.9 = (bf16[2048,768]{1,0:T(8,128)(2,1)S(1)}, bf16[2048,768]{1,0:T(8,128)(2,1)}, u32[]{:S(2)}) copy-start(bf16[2048,768]{1,0:T(8,128)(2,1)} %all-reduce.10.cloned.1.call-done) | copy-start | bytes 9437188
  423.8 9.5 %copy-start.11 = (bf16[2048,768]{1,0:T(8,128)(2,1)S(1)}, bf16[2048,768]{1,0:T(8,128)(2,1)}, u32[]{:S(2)}) copy-start(bf16[2048,768]{1,0:T(8,128)(2,1)} %all-reduce.14.cloned.1.call-done) | copy-start | bytes 9437188
  433.3 8.7 %copy-start.19 = (bf16[192,768]{1,0:T(8,128)(2,1)S(1)}, bf16[192,768]{1,0:T(8,128)(2,1)}, u32[]{:S(2)}) copy-start(bf16[192,768]{1,0:T(8,128)(2,1)} %param.22) | copy-start | bytes 884740
  439.4 2.7 copy-start.4
  478.1 5.7 copy-start.15
  493.1 8.0 copy-start.14
  493.1 310.6 %all-reduce.18.cloned.1.call-start = ((), (), s32[]{:S(2)}) async-start(), calls=%async_computation.4 | async-start | bytes 14155776 | tf_op jit(solution)/shard_map/psum | solution.py:274
  501.1 4.7 copy-start.7
  501.1 4.7 copy-start.20
  509.1 1.5 copy-start.44
  509.1 1.5 copy-start.46
  512.9 54.4 %copy-start.42 = (f32[768]{0:T(1024)S(1)}, f32[768]{0:T(1024)}, u32[]{:S(2)}) copy-start(f32[768]{0:T(1024)} %get-tuple-element.250) | copy-start | bytes 9220
  803.7 4.9 copy-start.18
  803.7 6.3 copy-start.17
  803.7 7.7 copy-start.1
Sparse Core Ops, SparseCore 0:
  44.3 71.1 all-reduce.9
  148.4 68.5 all-reduce.11
  359.0 64.8 all-reduce.13
  493.2 68.5 all-reduce.15
  567.2 236.4 all-reduce.17
where the time goes:
time: 826 us; the launch traced here: 820 us
  waiting for transfers between devices  422 us (51%)
  blocking collectives  138 us (17%)
  matrix products  108 us (13%)
  local copies, waits for them, and re-layouts  71.9 us (9%)
  other arithmetic  60.7 us (7%)
  between operations  17.3 us (2%)
    psum x1, waiting for transfers between devices, shards(): lax.psum((ffn_summed[0], ffn_summed[1], ffn_summed[2], ffn_summed[3], ffn...  196 us
    psum x1, waiting for transfers between devices, shards(): lax.psum(product(context, w_out).astype(jnp.bfloat16), 'mp')  70.8 us
    psum x1, waiting for transfers between devices, shards(): lax.psum(product_nt(grad_before, w_in).astype(jnp.bfloat16), 'mp')  55.5 us
    psum x1, waiting for transfers between devices, shards(): lax.psum(product(active, w_back).astype(jnp.bfloat16), 'mp')  50.4 us
    psum x1, waiting for transfers between devices, shards(): lax.psum(jnp.einsum('cte,cde->td', grad_qkv, w_qkv, preferred_element_typ...  48.9 us
    psum x1, blocking collectives, shards(): lax.psum((ffn_summed[0], ffn_summed[1], ffn_summed[2], ffn_summed[3], ffn...  39.6 us
    unnamed x2, blocking collectives  34.1 us
    all_gather x1, blocking collectives, shards(): lax.all_gather(query_vecs.astype(jnp.float32), 'dp', axis=0, tiled=True)  33.3 us
  transfers between devices with their start and end apart: 5, of which 5 were waited for; matrix products, arithmetic and copies ran while one was open for 5% of the time, Pallas kernels for 0%

commit v1 on v0

v1 whole, which is shorter than its diff:
```python
import functools

import jax
import jax.numpy as jnp
from jax import lax
from jax.experimental import pallas as pl
from jax.experimental.pallas import tpu as pltpu
from jax.sharding import PartitionSpec as P

HEAD_DIM = 64
Q_BLOCK = 128
K_WINDOW = 256
LANES = 128
TILE = 256
ROW_TILE = 64
VEC_ROWS = 64
VMEM_BYTES = 56 * 1024 * 1024

norm_eps = 1e-06
inv_temp = 50.0
loss_scale = 8.0
masked_score = -1000000000.0

f32 = jnp.float32
bf16 = jnp.bfloat16


def product(left_side, right_side):
    return jnp.dot(left_side, right_side, preferred_element_type=f32)


def product_t(left_side, right_side):
    return lax.dot_general(
        left_side, right_side, (((0,), (0,)), ((), ())), preferred_element_type=f32
    )


def product_nt(left_side, right_side):
    return lax.dot_general(
        left_side, right_side, (((1,), (1,)), ((), ())), preferred_element_type=f32
    )


def window_start(block, length):
    return min(max(block * Q_BLOCK - HEAD_DIM, 0), length - K_WINDOW)


def gelu_and_slope(values):
    bell = jnp.exp(values * values * -0.5)
    t = 1.0 / (1.0 + (0.3275911 * 0.7071067811865476) * jnp.abs(values))
    poly = 1.061405429 * t - 1.453152027
    poly = poly * t + 1.421413741
    poly = poly * t - 0.284496736
    poly = poly * t + 0.254829592
    tail = (0.5 * t) * (poly * bell)
    phi = jnp.where(values >= 0.0, 1.0 - tail, tail)
    return values * phi, phi + (values * 0.3989422804014327) * bell


def head_lanes(pair, which):
    lane = lax.broadcasted_iota(jnp.int32, pair.shape, 1)
    keep = (lane < HEAD_DIM) if which == 0 else (lane >= HEAD_DIM)
    return jnp.where(keep, pair, jnp.zeros_like(pair))


def columns(array, first, count):
    return array[:, first : first + count]


def head_parts(array, local_width):
    parts = []
    for head in range(local_width // HEAD_DIM):
        first = head // 2 * LANES
        width = min(LANES, local_width - first)
        part = columns(array, first, width)
        parts.append(part if width < LANES else head_lanes(part, head % 2))
    return parts


def merge_heads(results, local_width):
    pieces = []
    for first in range(0, local_width, LANES):
        head = first // HEAD_DIM
        if local_width - first >= LANES:
            lane = lax.broadcasted_iota(jnp.int32, results[head].shape, 1)
            pieces.append((first, jnp.where(lane < HEAD_DIM, results[head], results[head + 1])))
        else:
            pieces.append((first, results[head]))
    return pieces


def attend_forward(m_ref, tok_ref, w_ref, b_ref, seg_ref, win_ref, qkv_ref, prob_ref, ctx_ref):
    length = tok_ref.shape[0]
    width = w_ref.shape[2]
    heads = width // HEAD_DIM
    tok = tok_ref[...]
    q = ((product(tok, w_ref[0]) + b_ref[0:1, :]).astype(bf16) * HEAD_DIM**-0.5).astype(bf16)
    k = product(tok, w_ref[1]).astype(bf16)
    v = (product(tok, w_ref[2]) + b_ref[1:2, :]).astype(bf16)
    qkv_ref[0, 0] = q
    qkv_ref[0, 1] = k
    qkv_ref[0, 2] = v
    q_parts = head_parts(q, width)
    slot = lax.broadcasted_iota(jnp.int32, (16, 1), 0)
    own = (seg_ref[0] == slot).astype(f32).astype(bf16)
    for block in range(length // Q_BLOCK):
        at, start = block * Q_BLOCK, window_start(block, length)
        seen = (win_ref[0, block : block + 1, :] == slot).astype(f32).astype(bf16)
        mask = (product_t(columns(own, at, Q_BLOCK), seen) - 1.0) * -masked_score
        results = []
        for head in range(heads):
            first = head // 2 * LANES
            part = min(LANES, width - first)
            key = k[start : start + K_WINDOW, first : first + part]
            value = v[start : start + K_WINDOW, first : first + part]
            scores = product_nt(q_parts[head][at : at + Q_BLOCK], key) + mask
            weights = jnp.exp(scores - jnp.max(scores, axis=-1, keepdims=True))
            low = (weights * (1.0 / jnp.sum(weights, axis=-1, keepdims=True))).astype(bf16)
            prob_ref[0, head * (length // Q_BLOCK) + block] = low
            results.append(product(low, value))
        for first, merged in merge_heads(results, width):
            ctx_ref[0, at : at + Q_BLOCK, first : first + merged.shape[1]] = merged.astype(bf16)


def attend_backward(
    m_ref, tok_ref, w_ref, qkv_ref, prob_ref, g0_ref, g1_ref, g2_ref, g3_ref,
    dw_ref, o0_ref, o1_ref, o2_ref, o3_ref, gctx, gk_sum, gv_sum, dw_sum, vec_sum,
):
    step = pl.program_id(0)
    length = tok_ref.shape[0]
    width = w_ref.shape[2]
    heads = width // HEAD_DIM
    for piece, g_ref in enumerate((g0_ref, g1_ref, g2_ref, g3_ref)):

        @pl.when(step == piece)
        def _():
            gctx[...] = g_ref[...]

    @pl.when(step == 0)
    def _():
        dw_sum[...] = jnp.zeros_like(dw_sum)
        vec_sum[...] = jnp.zeros_like(vec_sum)

    gk_sum[...] = jnp.zeros_like(gk_sum)
    gv_sum[...] = jnp.zeros_like(gv_sum)
    q, k, v = qkv_ref[0, 0], qkv_ref[0, 1], qkv_ref[0, 2]
    q_parts = head_parts(q, width)
    g_parts = head_parts(gctx[...], width)
    gq_blocks = []
    for block in range(length // Q_BLOCK):
        at, start = block * Q_BLOCK, window_start(block, length)
        rows = slice(start, start + K_WINDOW)
        results, gk, gv = [], {}, {}
        for head in range(heads):
            first = head // 2 * LANES
            part = min(LANES, width - first)
            key, value = k[rows, first : first + part], v[rows, first : first + part]
            grad = g_parts[head][at : at + Q_BLOCK]
            low = prob_ref[0, head * (length // Q_BLOCK) + block]
            prob = low.astype(f32)
            grad_prob = product_nt(grad, value)
            inner = jnp.sum(prob * grad_prob, axis=-1, keepdims=True)
            grad_low = (prob * (grad_prob - inner)).astype(bf16)
            results.append(product(grad_low, key))
            gk_part = product_t(grad_low, q_parts[head][at : at + Q_BLOCK])
            gv_part = product_t(low, grad)
            gk[first] = gk[first] + gk_part if first in gk else gk_part
            gv[first] = gv[first] + gv_part if first in gv else gv_part
        for first in gk:
            lanes = slice(first, first + gk[first].shape[1])
            gk_sum[rows, lanes] += gk[first]
            gv_sum[rows, lanes] += gv[first]
        gq_blocks.append(merge_heads(results, width))
    gq = jnp.concatenate(
        [
            jnp.concatenate(
                [(blocks[i][1] * HEAD_DIM**-0.5).astype(bf16) for blocks in gq_blocks], axis=0
            )
            for i in range(len(gq_blocks[0]))
        ],
        axis=1,
    )
    gk, gv = gk_sum[...].astype(bf16), gv_sum[...].astype(bf16)
    tok = tok_ref[...]
    back = None
    for c, grad in enumerate((gq, gk, gv)):
        dw_sum[c * width : (c + 1) * width, :] += product_t(grad, tok)
        term = product_nt(grad, w_ref[c])
        back = term if back is None else back + term
    vec_sum[0:1, :] += jnp.sum(gq.astype(f32), axis=0, keepdims=True)
    vec_sum[1:2, :] += jnp.sum(gv.astype(f32), axis=0, keepdims=True)
    back = back.astype(bf16)
    for piece, o_ref in enumerate((o0_ref, o1_ref, o2_ref, o3_ref)):

        @pl.when(step == piece)
        def _():
            o_ref[...] = back

    @pl.when(step == pl.num_programs(0) - 1)
    def _():
        dw_ref[0 : 3 * width, :] = dw_sum[...].astype(bf16)
        vec = vec_sum[...]
        top = vec.astype(bf16)
        rest = (vec - top.astype(f32)).astype(bf16)
        dw_ref[3 * width :, :] = jnp.zeros((VEC_ROWS, dw_ref.shape[1]), bf16)
        dw_ref[3 * width : 3 * width + 16, 0:width] = jnp.concatenate([top, rest], axis=0)


def start_all(pairs, sems):
    copies = []
    for i, (source, target) in enumerate(pairs):
        copy = pltpu.make_async_copy(source, target, sems.at[i])
        copy.start()
        copies.append(copy)
    return copies


def middle_forward(
    m_ref, tok_hbm, seg_ref, pair_ref, b_out, gain1, shift1, b_in, b_back, gain2, shift2,
    c0, c1, c2, c3, wo0, wo1, wo2, wo3, wi0, wi1, wi2, wi3, wb0, wb1, wb2, wb3,
    act_hbm, slope_hbm, xhat1_ref, rstd1_ref, low1_ref, xhat2_ref, rstd2_ref, out_ref, pooled_ref, len_ref, msg_ref,
    tok_v, ctx_v, wo_v, wi_v, wb_v, act_v, slope_v, resid, sems, out_sems,
):
    length, width = tok_v.shape
    units = wi_v.shape[2]
    at = pl.multiple_of(m_ref[0] * length, length)
    copies = start_all(
        [(tok_hbm.at[pl.ds(at, length)], tok_v)]
        + [(c, ctx_v.at[r]) for r, c in enumerate((c0, c1, c2, c3))]
        + [(w, wo_v.at[r]) for r, w in enumerate((wo0, wo1, wo2, wo3))]
        + [(w, wi_v.at[r]) for r, w in enumerate((wi0, wi1, wi2, wi3))]
        + [(w, wb_v.at[r]) for r, w in enumerate((wb0, wb1, wb2, wb3))],
        sems,
    )
    for copy in copies[:9]:
        copy.wait()
    for first in range(0, width, TILE):
        cols = slice(first, first + TILE)
        total = tok_v[:, cols].astype(f32) + b_out[:, cols]
        for r in range(4):
            total = total + product(ctx_v[r], wo_v[r, :, cols])
        resid[:, cols] = total

    @pl.loop(0, length // ROW_TILE)
    def _(i):
        rows = pl.ds(pl.multiple_of(i * ROW_TILE, ROW_TILE), ROW_TILE)
        values = resid[rows, :]
        center = values - jnp.mean(values, axis=-1, keepdims=True)
        rate = lax.rsqrt(jnp.mean(center * center, axis=-1, keepdims=True) + norm_eps)
        xhat = center * rate
        xhat1_ref[rows, :] = xhat
        rstd1_ref[rows, :] = jnp.broadcast_to(rate, (ROW_TILE, LANES))
        normed = xhat * gain1[...] + shift1[...]
        resid[rows, :] = normed
        low1_ref[rows, :] = normed.astype(bf16)

    outs = []
    for r in range(4):
        copies[9 + r].wait()
        for first in range(0, units, TILE):
            cols = slice(first, first + TILE)
            before = product(low1_ref[...], wi_v[r, :, cols]) + b_in[r : r + 1, cols]
            active, slope = gelu_and_slope(before)
            act_v[r, :, cols] = active.astype(bf16)
            slope_v[r, :, cols] = slope.astype(bf16)
        outs += start_all(
            [(act_v.at[r], act_hbm.at[r]), (slope_v.at[r], slope_hbm.at[r])],
            out_sems.at[pl.ds(2 * r, 2)],
        )
    for r in range(4):
        copies[13 + r].wait()
    for first in range(0, width, TILE):
        cols = slice(first, first + TILE)
        total = resid[:, cols] + b_back[:, cols]
        for r in range(4):
            total = total + product(act_v[r], wb_v[r, :, cols])
        resid[:, cols] = total

    @pl.loop(0, length // ROW_TILE)
    def _(i):
        rows = pl.ds(pl.multiple_of(i * ROW_TILE, ROW_TILE), ROW_TILE)
        values = resid[rows, :]
        center = values - jnp.mean(values, axis=-1, keepdims=True)
        rate = lax.rsqrt(jnp.mean(center * center, axis=-1, keepdims=True) + norm_eps)
        xhat = center * rate
        xhat2_ref[rows, :] = xhat
        rstd2_ref[rows, :] = jnp.broadcast_to(rate, (ROW_TILE, LANES))
        out_ref[rows, :] = (xhat * gain2[...] + shift2[...]).astype(bf16)

    own = members(seg_ref)
    sums = product(own.astype(bf16), out_ref[...])
    count = jnp.sum(own, axis=-1, keepdims=True)
    pooled = sums / count
    rate = lax.rsqrt(jnp.sum(pooled * pooled, axis=-1, keepdims=True) + norm_eps)
    unit = (pooled * rate).astype(bf16)
    pooled_ref[...] = pooled
    len_ref[...] = jnp.broadcast_to(count, len_ref.shape)
    half = unit.astype(f32)
    msg_ref[:, 0:width] = half[0:8].astype(bf16)
    msg_ref[:, width : 2 * width] = half[8:16].astype(bf16)
    msg_ref[:, 2 * width :] = pair_ref[...].astype(bf16)
    for copy in outs:
        copy.wait()


def members(seg_ref):
    slot = lax.broadcasted_iota(jnp.int32, (16, 1), 0)
    segment = jnp.where(slot < 8, 2 * slot, 2 * slot - 15)
    return (seg_ref[...] == segment).astype(f32)


def contrast(ids_ref, all_ref, own_ref, pooled_ref, len_ref, loss_ref, grad_ref, log_v):
    width = pooled_ref.shape[1]
    count = all_ref.shape[0]
    block = min(count, 256)
    passages = all_ref[:, width : 2 * width]
    number = lax.broadcasted_iota(jnp.int32, (1, count), 1).astype(f32)

    def target(rows):
        coded = rows[:, 2 * width :].astype(f32)
        return coded[:, 0:1] * 64.0 + coded[:, 1:2]

    def statistics(rows, scores):
        best = jnp.max(scores, axis=-1, keepdims=True)
        log_total = best + jnp.log(jnp.sum(jnp.exp(scores - best), axis=-1, keepdims=True))
        return log_total, (number == target(rows)).astype(f32)

    def one_block(i, total):
        rows_at = pl.ds(pl.multiple_of(i * block, block), block)
        rows = all_ref[rows_at, :]
        scores = product_nt(rows[:, 0:width], passages) * inv_temp
        log_total, positive = statistics(rows, scores)
        log_v[rows_at, :] = jnp.broadcast_to(log_total, (block, LANES))
        return total + jnp.sum(log_total - jnp.sum(scores * positive, axis=-1, keepdims=True), keepdims=True)

    total = lax.fori_loop(0, count // block, one_block, jnp.zeros((1, 1), f32))
    loss_ref[...] = jnp.broadcast_to(total * (1.0 / count), loss_ref.shape)
    own = own_ref[...]
    scores = product_nt(own[:, 0:width], passages) * inv_temp
    log_total, positive = statistics(own, scores)
    grad_low = ((jnp.exp(scores - log_total) - positive) * (loss_scale * inv_temp)).astype(bf16)
    grad_query = product(grad_low, passages)

    everyone = all_ref[...]
    queries = everyone[:, 0:width]
    passage = jnp.concatenate(
        [own[:, width : 2 * width].astype(f32), jnp.zeros((LANES - 8, width), f32)], axis=0
    ).astype(bf16)
    lane = lax.broadcasted_iota(jnp.int32, (1, LANES), 1)
    scores = product_nt(queries, passage) * inv_temp
    number = jnp.where(lane < 8, ids_ref[0] * 8 + lane, -1).astype(f32)
    positive = (number == target(everyone)).astype(f32)
    weight = jnp.exp(scores - log_v[...]) - positive
    grad_low = (jnp.where(lane < 8, weight, 0.0) * (loss_scale * inv_temp)).astype(bf16)
    grad_passage = product_t(grad_low, queries)[0:8]

    grad_unit = jnp.concatenate([grad_query, grad_passage], axis=0)
    pooled = pooled_ref[...]
    rate = lax.rsqrt(jnp.sum(pooled * pooled, axis=-1, keepdims=True) + norm_eps)
    inner = jnp.sum(pooled * grad_unit, axis=-1, keepdims=True)
    grad = rate * grad_unit - rate * rate * rate * pooled * inner
    grad_ref[...] = grad / len_ref[:, 0:1]


def column_total(values):
    return jnp.sum(values.reshape(values.shape[0] // 8, 8, values.shape[1]), axis=0)


def back_second(
    gp_ref, seg_ref, xhat_ref, rstd_ref, gain_ref, act_hbm,
    low_ref, grad_ref, vec_ref, d0, d1, d2, d3,
    out_v, act_v, sums, sems,
):
    length, width = xhat_ref.shape
    copies = start_all([(act_hbm.at[r], act_v.at[r]) for r in range(4)], sems)
    own = members(seg_ref).astype(bf16)
    top = gp_ref[...].astype(bf16)
    rest = (gp_ref[...] - top.astype(f32)).astype(bf16)
    out_v[...] = product_t(own, top) + product_t(own, rest)
    sums[...] = jnp.zeros_like(sums)

    @pl.loop(0, length // ROW_TILE)
    def _(i):
        rows = pl.ds(pl.multiple_of(i * ROW_TILE, ROW_TILE), ROW_TILE)
        grad_out, xhat = out_v[rows, :], xhat_ref[rows, :]
        sums[0] += column_total(grad_out * xhat)
        sums[1] += column_total(grad_out)
        grad = grad_out * gain_ref[...]
        first = jnp.mean(grad, axis=-1, keepdims=True)
        second = jnp.mean(grad * xhat, axis=-1, keepdims=True)
        grad = (grad - first - xhat * second) * rstd_ref[rows, 0:1]
        sums[2] += column_total(grad)
        grad_ref[rows, :] = grad
        low_ref[rows, :] = grad.astype(bf16)

    vec_ref[...] = jnp.zeros_like(vec_ref)
    for i in range(3):
        vec_ref[i : i + 1, :] = jnp.sum(sums[i], axis=0, keepdims=True)
    for r, d_ref in ((3, d3), (2, d2), (1, d1), (0, d0)):
        copies[r].wait()
        for first in range(0, width, TILE):
            cols = slice(first, first + TILE)
            d_ref[cols, :] = product_t(act_v[r, :, cols], low_ref[...]).astype(bf16)


def back_first(
    low_ref, resid_ref, xhat_ref, rstd_ref, gain_ref, slope_hbm,
    wo0, wo1, wo2, wo3, wi0, wi1, wi2, wi3, wb0, wb1, wb2, wb3,
    gb_hbm, grad_ref, attn_ref, vec_ref, bin_ref, x0, x1, x2, x3,
    slope_v, wo_v, wi_v, wb_v, gb_v, total_v, sums, sems, out_sems,
):
    length, width = xhat_ref.shape
    units = wi_v.shape[2]
    copies = start_all(
        [p for r, w in enumerate((wb0, wb1, wb2, wb3)) for p in ((w, wb_v.at[r]), (slope_hbm.at[r], slope_v.at[r]))]
        + [(w, wi_v.at[r]) for r, w in enumerate((wi0, wi1, wi2, wi3))]
        + [(w, wo_v.at[r]) for r, w in enumerate((wo0, wo1, wo2, wo3))],
        sems,
    )
    outs = []
    for r in range(4):
        copies[2 * r].wait()
        copies[2 * r + 1].wait()
        for first in range(0, units, TILE):
            cols = slice(first, first + TILE)
            grad = product_nt(low_ref[...], wb_v[r, cols, :])
            low = (grad * slope_v[r, :, cols].astype(f32)).astype(bf16)
            gb_v[r, :, cols] = low
            bin_ref[r : r + 1, cols] = jnp.sum(column_total(low.astype(f32)), axis=0, keepdims=True)
        outs += start_all([(gb_v.at[r], gb_hbm.at[r])], out_sems.at[pl.ds(r, 1)])
    for copy in copies[8:]:
        copy.wait()
    for first in range(0, width, TILE):
        cols = slice(first, first + TILE)
        total = resid_ref[:, cols]
        for r in range(4):
            total = total + product_nt(gb_v[r], wi_v[r, cols, :])
        total_v[:, cols] = total
    sums[...] = jnp.zeros_like(sums)

    @pl.loop(0, length // ROW_TILE)
    def _(i):
        rows = pl.ds(pl.multiple_of(i * ROW_TILE, ROW_TILE), ROW_TILE)
        grad_out, xhat = total_v[rows, :], xhat_ref[rows, :]
        sums[0] += column_total(grad_out * xhat)
        sums[1] += column_total(grad_out)
        grad = grad_out * gain_ref[...]
        first = jnp.mean(grad, axis=-1, keepdims=True)
        second = jnp.mean(grad * xhat, axis=-1, keepdims=True)
        grad = (grad - first - xhat * second) * rstd_ref[rows, 0:1]
        sums[2] += column_total(grad)
        grad_ref[rows, :] = grad
        attn_ref[rows, :] = grad.astype(bf16)

    vec_ref[...] = jnp.zeros_like(vec_ref)
    for i in range(3):
        vec_ref[i : i + 1, :] = jnp.sum(sums[i], axis=0, keepdims=True)
    for r, x_ref in enumerate((x0, x1, x2, x3)):
        x_ref[...] = product_nt(attn_ref[...], wo_v[r]).astype(bf16)
    for copy in outs:
        copy.wait()


def weight_grads(
    low1_ref, attn_ref, vec1_ref, vec2_ref, bin_ref, c0, c1, c2, c3, gb_hbm,
    d0, d1, d2, d3,
    gb_v, sems,
):
    length, width = low1_ref.shape
    units = gb_v.shape[2]
    local = c0.shape[1]
    copies = start_all([(gb_hbm.at[r], gb_v.at[r]) for r in range(4)], sems)
    for r, d_ref, c_ref in ((3, d3, c3), (2, d2, c2), (1, d1, c1), (0, d0, c0)):
        copies[r].wait()
        for first in range(0, width, TILE):
            cols = slice(first, first + TILE)
            d_ref[cols, :] = product_t(low1_ref[:, cols], gb_v[r]).astype(bf16)
        d_ref[width : width + local, :] = product_t(c_ref[...], attn_ref[...]).astype(bf16)
        rows = jnp.concatenate(
            [vec1_ref[0:3, :], vec2_ref[0:3, :], bin_ref[r : r + 1, :], jnp.zeros((1, units), f32)],
            axis=0,
        )
        top = rows.astype(bf16)
        rest = (rows - top.astype(f32)).astype(bf16)
        at = width + local
        d_ref[at : at + 16, :] = jnp.concatenate([top, rest], axis=0)
        d_ref[at + 16 : at + VEC_ROWS, :] = jnp.zeros((VEC_ROWS - 16, units), bf16)


def whole(array, memory=pltpu.VMEM):
    return pl.BlockSpec(memory_space=memory)


def hop(array, axis, flip):
    size = lax.axis_size(axis)
    return lax.ppermute(array, axis, [(i, i ^ flip) for i in range(size)])


def bit_of(axis, flip):
    return (lax.axis_index(axis) // flip) % 2


def ordered(bit, mine, other, axis):
    low_first = jnp.concatenate([mine, other], axis=axis)
    high_first = jnp.concatenate([other, mine], axis=axis)
    return jnp.where(bit == 0, low_first, high_first)


def bits_below(size):
    flips, flip = [], 1
    while flip < size:
        flips.append(flip)
        flip *= 2
    return flips


def gather_parts(mine):
    near = hop(mine, "mp", 1)
    far = hop(mine, "mp", 2)
    return [mine, near, far, hop(far, "mp", 1)]


def add_low(left_side, right_side):
    return (left_side.astype(f32) + right_side.astype(f32)).astype(bf16)


def scatter_parts(parts):
    far = add_low(parts[2], hop(parts[3], "mp", 1))
    near = add_low(parts[0], hop(parts[1], "mp", 1))
    return add_low(near, hop(far, "mp", 2))


def sum_over_rows(array):
    flips = bits_below(lax.axis_size("dp"))
    for flip in flips:
        half = array.shape[0] // 2
        bit = bit_of("dp", flip)
        send = lax.dynamic_slice_in_dim(array, (1 - bit) * half, half)
        keep = lax.dynamic_slice_in_dim(array, bit * half, half)
        array = add_low(keep, hop(send, "dp", flip))
    for flip in reversed(flips):
        array = ordered(bit_of("dp", flip), array, hop(array, "dp", flip), 0)
    return array


def params(cost=None, **more):
    return dict(
        compiler_params=pltpu.CompilerParams(vmem_limit_bytes=VMEM_BYTES, **more), cost_estimate=cost
    )


def cost(flops, moved, exps=0):
    return pl.CostEstimate(flops=int(flops), bytes_accessed=int(moved), transcendentals=int(exps))


def shape(dims, dtype=bf16):
    return jax.ShapeDtypeStruct(dims, dtype)


def shards(
    tokens, w_qkv, b_qv, w_out, b_out, norm1_gain, norm1_shift, w_in, b_in, w_back, b_back,
    norm2_gain, norm2_shift, segment_ids, pair_ids,
):
    row_count, length = segment_ids.shape
    width = tokens.shape[1]
    local = w_out.shape[0]
    units = w_in.shape[1]
    heads = local // HEAD_DIM
    blocks = length // Q_BLOCK
    member = lax.axis_index("mp")
    own_row = lax.axis_index("dp") * row_count + member
    m_arr = member.astype(jnp.int32).reshape(1)
    any_spec = pl.BlockSpec(memory_space=pl.ANY)
    vmem_spec = pl.BlockSpec(memory_space=pltpu.VMEM)
    smem_spec = pl.BlockSpec(memory_space=pltpu.SMEM)
    dma = pltpu.SemaphoreType.DMA

    out_parts = gather_parts(w_out)
    in_parts = gather_parts(w_in)
    back_parts = gather_parts(w_back)
    bias_parts = jnp.concatenate(gather_parts(b_in[None, :]), axis=0)

    windows = jnp.stack(
        [segment_ids[:, window_start(i, length) :][:, :K_WINDOW] for i in range(blocks)], axis=1
    )
    seg_rows = segment_ids[:, None, :]
    pick = lambda r, m: (r ^ m[0], 0, 0)
    qkv, probs, ctx = pl.pallas_call(
        attend_forward,
        grid_spec=pltpu.PrefetchScalarGridSpec(
            num_scalar_prefetch=1,
            grid=(row_count,),
            in_specs=[
                pl.BlockSpec((length, width), lambda r, m: (r ^ m[0], 0)),
                pl.BlockSpec(w_qkv.shape, lambda r, m: (0, 0, 0)),
                pl.BlockSpec(b_qv.shape, lambda r, m: (0, 0)),
                pl.BlockSpec((1, 1, length), pick),
                pl.BlockSpec((1, blocks, K_WINDOW), pick),
            ],
            out_specs=[
                pl.BlockSpec((1, 3, length, local), lambda r, m: (r, 0, 0, 0)),
                pl.BlockSpec((1, heads * blocks, Q_BLOCK, K_WINDOW), lambda r, m: (r, 0, 0, 0)),
                pl.BlockSpec((1, length, local), lambda r, m: (r, 0, 0)),
            ],
        ),
        out_shape=[
            shape((row_count, 3, length, local)),
            shape((row_count, heads * blocks, Q_BLOCK, K_WINDOW)),
            shape((row_count, length, local)),
        ],
        name="attend_forward",
        **params(cost(6 * row_count * length * width * local, 8e6, row_count * heads * length * K_WINDOW)),
    )(m_arr, tokens, w_qkv, b_qv, seg_rows, windows)

    ctx_parts = [ctx[0]] + [hop(ctx[r], "mp", r) for r in range(1, 4)]
    seg_own = lax.dynamic_slice_in_dim(segment_ids, member, 1)
    pair_own = lax.dynamic_slice_in_dim(pair_ids, member, 1).reshape(-1, 1)
    pair_code = jnp.concatenate(
        [pair_own // 64, pair_own % 64, jnp.zeros((pair_own.shape[0], LANES - 2), jnp.int32)], axis=1
    ).astype(f32)
    row = lambda vector: vector[None, :]
    act, slope, xhat1, rstd1, low1, xhat2, rstd2, out_own, pooled, lengths, msg = pl.pallas_call(
        middle_forward,
        in_specs=[smem_spec, any_spec] + [vmem_spec] * 9 + [any_spec] * 16,
        out_specs=[any_spec] * 2 + [vmem_spec] * 9,
        out_shape=[
            shape((4, length, units)), shape((4, length, units)),
            shape((length, width), f32), shape((length, LANES), f32), shape((length, width)),
            shape((length, width), f32), shape((length, LANES), f32), shape((length, width)),
            shape((16, width), f32), shape((16, LANES), f32), shape((8, 2 * width + LANES)),
        ],
        scratch_shapes=[
            pltpu.VMEM((length, width), bf16), pltpu.VMEM((4, length, local), bf16),
            pltpu.VMEM((4, local, width), bf16), pltpu.VMEM((4, width, units), bf16),
            pltpu.VMEM((4, units, width), bf16), pltpu.VMEM((4, length, units), bf16),
            pltpu.VMEM((4, length, units), bf16), pltpu.VMEM((length, width), f32),
            dma((17,)), dma((8,)),
        ],
        name="middle_forward",
        **params(cost(2 * length * width * (width + 8 * units), 25e6, 4 * length * units)),
    )(
        m_arr, tokens, seg_own, pair_code, row(b_out), row(norm1_gain), row(norm1_shift), bias_parts,
        row(b_back), row(norm2_gain), row(norm2_shift), *ctx_parts, *out_parts, *in_parts, *back_parts,
    )

    everyone = msg[None]
    for flip in reversed(bits_below(lax.axis_size("dp"))):
        everyone = both_ways("dp", flip, everyone)
    for flip in reversed(bits_below(lax.axis_size("mp"))):
        everyone = both_ways("mp", flip, everyone)
    everyone = everyone.reshape(-1, msg.shape[1])

    loss, grad_pooled = pl.pallas_call(
        contrast,
        in_specs=[smem_spec] + [vmem_spec] * 4,
        out_specs=[vmem_spec] * 2,
        out_shape=[shape((8, LANES), f32), shape((16, width), f32)],
        scratch_shapes=[pltpu.VMEM((everyone.shape[0], LANES), f32)],
        name="contrast",
        **params(cost(4e8, 2e6, 1e5)),
    )(own_row.astype(jnp.int32).reshape(1), everyone, msg, pooled, lengths)

    grad_low2, grad_resid2, vec2, *d_back = pl.pallas_call(
        back_second,
        in_specs=[vmem_spec] * 5 + [any_spec],
        out_specs=[vmem_spec] * 7,
        out_shape=[
            shape((length, width)), shape((length, width), f32), shape((8, width), f32),
            *[shape((units, width))] * 4,
        ],
        scratch_shapes=[
            pltpu.VMEM((length, width), f32), pltpu.VMEM((4, length, units), bf16),
            pltpu.VMEM((3, 8, width), f32), dma((4,)),
        ],
        name="back_second",
        **params(cost(8 * length * width * units, 14e6)),
    )(grad_pooled, seg_own, xhat2, rstd2, row(norm2_gain), act)

    gb, grad_resid1, attn_low, vec1, d_bin, *ctx_grads = pl.pallas_call(
        back_first,
        in_specs=[vmem_spec] * 5 + [any_spec] * 13,
        out_specs=[any_spec] + [vmem_spec] * 8,
        out_shape=[
            shape((4, length, units)), shape((length, width), f32), shape((length, width)),
            shape((8, width), f32), shape((4, units), f32), *[shape((length, local))] * 4,
        ],
        scratch_shapes=[
            pltpu.VMEM((4, length, units), bf16), pltpu.VMEM((4, local, width), bf16),
            pltpu.VMEM((4, width, units), bf16), pltpu.VMEM((4, units, width), bf16),
            pltpu.VMEM((4, length, units), bf16), pltpu.VMEM((length, width), f32),
            pltpu.VMEM((3, 8, width), f32), dma((16,)), dma((4,)),
        ],
        name="back_first",
        **params(cost(2 * length * width * (width + 8 * units), 25e6)),
    )(
        grad_low2, grad_resid2, xhat1, rstd1, row(norm1_gain), slope, *out_parts, *in_parts, *back_parts,
    )

    grads_here = [ctx_grads[0]] + [hop(ctx_grads[r], "mp", r) for r in range(1, 4)]

    d_first = pl.pallas_call(
        weight_grads,
        in_specs=[vmem_spec] * 9 + [any_spec],
        out_specs=[vmem_spec] * 4,
        out_shape=[shape((width + local + VEC_ROWS, units))] * 4,
        scratch_shapes=[pltpu.VMEM((4, length, units), bf16), dma((4,))],
        name="weight_grads",
        **params(cost(8 * length * width * (units + local), 12e6)),
    )(low1, attn_low, vec1, vec2, d_bin, *ctx_parts, gb)

    same = lambda r, m: (0, 0)
    d_qkv, *backs = pl.pallas_call(
        attend_backward,
        grid_spec=pltpu.PrefetchScalarGridSpec(
            num_scalar_prefetch=1,
            grid=(row_count,),
            in_specs=[
                pl.BlockSpec((length, width), lambda r, m: (r ^ m[0], 0)),
                pl.BlockSpec(w_qkv.shape, lambda r, m: (0, 0, 0)),
                pl.BlockSpec((1, 3, length, local), lambda r, m: (r, 0, 0, 0)),
                pl.BlockSpec((1, heads * blocks, Q_BLOCK, K_WINDOW), lambda r, m: (r, 0, 0, 0)),
            ]
            + [pl.BlockSpec((length, local), same)] * 4,
            out_specs=[pl.BlockSpec((3 * local + VEC_ROWS, width), same)]
            + [pl.BlockSpec((length, width), same)] * 4,
            scratch_shapes=[
                pltpu.VMEM((length, local), bf16), pltpu.VMEM((length, local), f32),
                pltpu.VMEM((length, local), f32), pltpu.VMEM((3 * local, width), f32),
                pltpu.VMEM((8, local), f32),
            ],
        ),
        out_shape=[shape((3 * local + VEC_ROWS, width))] + [shape((length, width))] * 4,
        name="attend_backward",
        **params(cost(12 * row_count * length * width * local, 16e6)),
    )(m_arr, tokens, w_qkv, qkv, probs, *grads_here)

    layer_out = rows_of_all(out_own, row_count)
    near = add_low(backs[0].astype(f32) + grad_resid1, hop(backs[1], "mp", 1))
    far = add_low(backs[2], hop(backs[3], "mp", 1))
    d_tokens = rows_of_all(add_low(near, hop(far, "mp", 2)), row_count)

    sum_back = sum_over_rows(scatter_parts(d_back))
    sum_first = sum_over_rows(scatter_parts(d_first))
    sum_qkv = sum_over_rows(d_qkv)

    at = width + local
    vectors = sum_first[at : at + 8].astype(f32) + sum_first[at + 8 : at + 16].astype(f32)
    shares = lax.dynamic_slice_in_dim(vectors[0:6], member * local, local, axis=1)
    at = 3 * local
    d_bqv = sum_qkv[at : at + 2, 0:local].astype(f32) + sum_qkv[at + 8 : at + 10, 0:local].astype(f32)
    d_wqkv = jnp.swapaxes(sum_qkv[0:at].reshape(3, local, width), 1, 2).astype(f32)
    return (
        loss[0, 0],
        layer_out,
        d_tokens,
        d_wqkv,
        d_bqv,
        sum_first[width : width + local].astype(f32),
        shares[2],
        shares[0],
        shares[1],
        sum_first[0:width].astype(f32),
        vectors[6],
        sum_back.astype(f32),
        shares[5],
        shares[3],
        shares[4],
    )


def both_ways(axis, flip, array):
    other = hop(array, axis, flip)
    low_first = jnp.stack([array, other], axis=1)
    high_first = jnp.stack([other, array], axis=1)
    joined = jnp.where(bit_of(axis, flip) == 0, low_first, high_first)
    return joined.reshape(-1, *array.shape[1:])


def rows_of_all(mine, row_count):
    pair = ordered(bit_of("mp", 2), mine[None], hop(mine, "mp", 2)[None], 0)
    other = hop(pair, "mp", 1)
    low_first = jnp.stack([pair, other], axis=1)
    high_first = jnp.stack([other, pair], axis=1)
    joined = jnp.where(bit_of("mp", 1) == 0, low_first, high_first)
    return joined.reshape(row_count * mine.shape[0], mine.shape[1])


def solution(mesh):
    return jax.shard_map(
        shards,
        mesh=mesh,
        in_specs=(
            P("dp", None),
            P(None, None, "mp"),
            P(None, "mp"),
            P("mp", None),
            P(),
            P(),
            P(),
            P(None, "mp"),
            P("mp"),
            P("mp", None),
            P(),
            P(),
            P(),
            P("dp", None),
            P("dp", None),
        ),
        out_specs=(
            P(),
            P("dp", None),
            P("dp", None),
            P(None, None, "mp"),
            P(None, "mp"),
            P("mp", None),
            P("mp"),
            P("mp"),
            P("mp"),
            P(None, "mp"),
            P("mp"),
            P("mp", None),
            P("mp"),
            P("mp"),
            P("mp"),
        ),
        check_vma=False,
    )
```

time: 826 us -> 417 us (0.50)
  waiting for transfers between devices: 422 us -> 212 us
  blocking collectives: 138 us -> 0 us
  matrix products: 108 us -> 0 us
  Pallas kernels: 0 us -> 97.7 us
  starting transfers between devices: 0.88 us -> 50.2 us
  local copies, waits for them, and re-layouts: 71.9 us -> 23.8 us
  other arithmetic: 60.7 us -> 27.3 us
  between operations: 17.3 us -> 1.48 us
    psum x5 -> x0, waiting for transfers between devices: 422 us -> none  [the longest x1 196 us: shards(): lax.psum((ffn_summed[0], ffn_summed[1], ffn_summed[2], ffn_summed[3], ffn...]
    ppermute x0 -> x54, waiting for transfers between devices: none -> 212 us  [hop(): return lax.ppermute(array, axis, [(i, i ^ flip) for i in range(size)])]
    dot_general x45 -> x0, matrix products: 108 us -> none  [the longest x4 27.9 us: product(): return jnp.dot(left_side, right_side, preferred_element_type=jnp.float32)]
    pallas_call x0 -> x7, Pallas kernels: none -> 97.7 us  [the longest x1 22.1 us: shards(): pl.pallas_call(attend_backward, grid_spec=pltpu.PrefetchScalarGridSpec(nu...]
    all_gather x2 -> x0, blocking collectives: 64.6 us -> none  [the longest x1 33.3 us: shards(): lax.all_gather(query_vecs.astype(jnp.float32), 'dp', axis=0, tiled=True)]
    ppermute x0 -> x54, starting transfers between devices: none -> 50.2 us  [hop(): return lax.ppermute(array, axis, [(i, i ^ flip) for i in range(size)])]
    reduce_sum x17 -> x0, other arithmetic: 42.8 us -> none  [the longest x4 18.8 us: layer_norm(): center = values - jnp.mean(values, axis=-1, keepdims=True)]
    psum x1 -> x0, blocking collectives: 39.6 us -> none  [shards(): lax.psum((ffn_summed[0], ffn_summed[1], ffn_summed[2], ffn_summed[3], ffn...]
  transfers between devices with their start and end apart: 5 -> 54, of which waited for: 5 -> 32; matrix products, arithmetic and copies ran while one was open for 5% -> 10% of each run, Pallas kernels for 0% -> 6%
where the time goes in v1:
time: 417 us; the launch traced here: 412 us
  waiting for transfers between devices  212 us (51%)
  Pallas kernels  97.7 us (23%)
  starting transfers between devices  50.2 us (12%)
  other arithmetic  27.3 us (7%)
  local copies, waits for them, and re-layouts  23.8 us (6%)
    ppermute x54, waiting for transfers between devices, hop(): return lax.ppermute(array, axis, [(i, i ^ flip) for i in range(size)])  212 us
    ppermute x54, starting transfers between devices, hop(): return lax.ppermute(array, axis, [(i, i ^ flip) for i in range(size)])  50.2 us
    pallas_call x1, Pallas kernels, shards(): pl.pallas_call(attend_backward, grid_spec=pltpu.PrefetchScalarGridSpec(nu...  22.1 us
    pallas_call x1, Pallas kernels, shards(): pl.pallas_call(middle_forward, in_specs=[smem_spec, any_spec] + [vmem_spe...  21.4 us
    pallas_call x1, Pallas kernels, shards(): pl.pallas_call(back_first, in_specs=[vmem_spec] * 5 + [any_spec] * 13, ou...  16.3 us
    pallas_call x1, Pallas kernels, shards(): pl.pallas_call(attend_forward, grid_spec=pltpu.PrefetchScalarGridSpec(num...  16.2 us
    convert_element_type x15, other arithmetic, add_low(): return (left_side.astype(f32) + right_side.astype(f32)).astype(bf16)  13.3 us
    pallas_call x1, Pallas kernels, shards(): pl.pallas_call(back_second, in_specs=[vmem_spec] * 5 + [any_spec], out_sp...  9.46 us
  transfers between devices with their start and end apart: 54, of which 32 were waited for; matrix products, arithmetic and copies ran while one was open for 10% of the time, Pallas kernels for 6%

profile of v1, /device:TPU:0, one launch (start us, length us, event | category | flops | bytes accessed | tf_op | source)
XLA Modules:
  0.0 412.3 jit_solution(6593373196141035127)
XLA Ops:
  0.7 3.0 collective-permute-start.10
  6.0 2.4 copy.68.w_ref
  9.0 16.2 %attend_forward.1 = (bf16[4,3,512,192]{3,2,1,0:T(8,128)(2,1)}, bf16[4,12,128,256]{3,2,1,0:T(8,128)(2,1)}, bf16[4,512,192]{2,1,0:T(8,128)(2,1)}) custom-call(s32[1]{0:T(128)} %bitcast.1.m_ref, bf16[2048,768]{1,0:T(8,128)(2,1)} %tok_ref.3, bf16[3,768,192]{2,1,0:T(8,128)(2,1)} %copy.68.w_ref, f32[2,192]{1,0:T(2,128)} %b_ref.1, ...), custom_call_target="tpu_custom_call" | custom-call | flops 1811939328 | bytes 8000000 | tf_op jit(solution)/shard_map/attend_forward/pallas_call | solution.py:588
  25.3 2.1 slice_bitcast_fusion
  27.4 1.9 collective-permute-start.4
  29.4 31.4 %collective-permute-done.1 = f32[1,768]{1,0:T(1,128)S(1)} collective-permute-done((f32[1,768]{1,0:T(1,128)S(1)}, f32[1,768]{1,0:T(1,128)S(1)}, u32[]{:S(2)}, u32[]{:S(2)}) %collective-permute-start.1) | collective-permute-done | bytes 3104 | tf_op jit(solution)/shard_map/ppermute | solution.py:496
  65.8 6.8 %collective-permute-done.5.c3 = bf16[512,192]{1,0:T(8,128)(2,1)S(1)} collective-permute-done((bf16[512,192]{1,0:T(8,128)(2,1)S(1)}, bf16[512,192]{1,0:T(8,128)(2,1)S(1)}, u32[]{:S(2)}, u32[]{:S(2)}) %collective-permute-start.5) | collective-permute-done | bytes 196640 | tf_op jit(solution)/shard_map/ppermute | solution.py:496
  73.4 1.7 collective-permute-start.7
  78.8 3.5 collective-permute-done.7.wo2
  86.3 21.4 %middle_forward.1 = (bf16[4,512,768]{2,1,0:T(8,128)(2,1)}, bf16[4,512,768]{2,1,0:T(8,128)(2,1)}, f32[512,768]{1,0:T(8,128)}, f32[512,128]{1,0:T(8,128)}, bf16[51...) custom-call(s32[1]{0:T(128)} %bitcast.1.m_ref, ...), custom_call_target="tpu_custom_call" | custom-call | flops 5435817984 | bytes 25000000 | tf_op jit(solution)/shard_map/middle_forward/pallas_call | solution.py:622
  107.6 2.9 collective-permute-start.15
  110.5 2.1 collective-permute-done.15
  113.5 1.9 collective-permute-start.16
  117.7 1.8 collective-permute-start.17
  119.5 3.0 collective-permute-done.17
  122.6 1.8 collective-permute-start.18
  124.4 4.1 collective-permute-done.18
  128.7 1.7 collective-permute-done.19
  131.6 2.9 contrast.1
  134.5 9.5 %back_second.1 = (bf16[512,768]{1,0:T(8,128)(2,1)}, f32[512,768]{1,0:T(8,128)}, f32[8,768]{1,0:T(8,128)}, bf16[768,768]{1,0:T(8,128)(2,1)}, bf16[768,768]{1,0:T(...) custom-call(f32[16,768]{1,0:T(8,128)} %get-tuple-element.64.gp_ref, ...), custom_call_target="tpu_custom_call" | custom-call | flops 2415919104 | bytes 14000000 | tf_op jit(solution)/shard_map/back_second/pallas_call | solution.py:663
  144.0 16.3 %back_first.1 = (bf16[4,512,768]{2,1,0:T(8,128)(2,1)}, f32[512,768]{1,0:T(8,128)}, bf16[512,768]{1,0:T(8,128)(2,1)}, f32[8,768]{1,0:T(8,128)}, f32[4,768]{1,0:T(...) custom-call(bf16[512,768]{1,0:T(8,128)(2,1)} %get-tuple-element.68.l, ...), custom_call_target="tpu_custom_call" | custom-call | flops 5435817984 | bytes 25000000 | tf_op jit(solution)/shard_map/back_first/pallas_call | solution.py:679
  160.5 1.8 collective-permute-start.23
  162.3 7.6 %collective-permute-done.23.g2_ref = bf16[512,192]{1,0:T(8,128)(2,1)S(1)} collective-permute-done((bf16[512,192]{1,0:T(8,128)(2,1)}, bf16[512,192]{1,0:T(8,128)(2,1)S(1)}, u32[]{:S(2)}, u32[]{:S(2)}) %collective-permute-start.23) | collective-permute-done | bytes 196640 | tf_op jit(solution)/shard_map/ppermute | solution.py:496
  169.8 4.5 %collective-permute-done.24.g3_ref = bf16[512,192]{1,0:T(8,128)(2,1)S(1)} collective-permute-done((bf16[512,192]{1,0:T(8,128)(2,1)}, bf16[512,192]{1,0:T(8,128)(2,1)S(1)}, u32[]{:S(2)}, u32[]{:S(2)}) %collective-permute-start.24) | collective-permute-done | bytes 196640 | tf_op jit(solution)/shard_map/ppermute | solution.py:496
  175.0 22.1 %attend_backward.1 = (bf16[640,768]{1,0:T(8,128)(2,1)}, bf16[512,768]{1,0:T(8,128)(2,1)}, bf16[512,768]{1,0:T(8,128)(2,1)}, bf16[512,768]{1,0:T(8,128)(2,1)}, bf16[512,768]{1,0:T(8,128)(2,1)}) custom-call(s32[1]{0:T(128)} %bitcast.1.m_ref, bf16[2048,768]{1,0:T(8,128)(2,1)} %tok_ref.3, bf16[3,768,192]{2,1,0:T(8,128)(2,1)} %copy.68.w_ref, ...), custom_call_target="tpu_custom_call" | custom-call | flops 3623878656 | bytes 16000000 | tf_op jit(solution)/shard_map/attend_backward/pallas_call | solution.py:712
  198.2 1.8 collective-permute-start.30
  200.0 9.3 %weight_grads.1 = (bf16[1024,768]{1,0:T(8,128)(2,1)}, bf16[1024,768]{1,0:T(8,128)(2,1)}, bf16[1024,768]{1,0:T(8,128)(2,1)}, bf16[1024,768]{1,0:T(8,128)(2,1)}) custom-call(bf16[512,768]{1,0:T(8,128)(2,1)} %get-tuple-element.83.low1_ref, bf16[512,768]{1,0:T(8,128)(2,1)} %get-tuple-element.84.attn_ref, f32[8,768]{1,0:T(8,128)} %get-tuple-element.85.vec1_ref, ...), custom_call_target="tpu_custom_call" | custom-call | flops 3019898880 | bytes 12000000 | tf_op jit(solution)/shard_map/weight_grads/pallas_call | solution.py:701
  209.9 1.8 collective-permute-done.30
  211.9 1.9 collective-permute-start.31
  213.8 5.8 %collective-permute-done.31 = bf16[160,768]{1,0:T(8,128)(2,1)} collective-permute-done((bf16[160,768]{1,0:T(8,128)(2,1)S(1)}, bf16[160,768]{1,0:T(8,128)(2,1)}, u32[]{:S(2)}, u32[]{:S(2)}) %collective-permute-start.31) | collective-permute-done | bytes 245792 | tf_op jit(solution)/shard_map/ppermute | solution.py:496
  221.2 2.8 collective-permute-start.32
  225.5 3.5 collective-permute-done.32
  231.8 3.0 add_convert_fusion.4
  236.3 1.6 add_convert_fusion.1
  237.9 6.6 %collective-permute-done.20 = bf16[512,768]{1,0:T(8,128)(2,1)S(1)} collective-permute-done((bf16[512,768]{1,0:T(8,128)(2,1)S(1)}, bf16[512,768]{1,0:T(8,128)(2,1)S(1)}, u32[]{:S(2)}, u32[]{:S(2)}) %collective-permute-start.20) | collective-permute-done | bytes 786464 | tf_op jit(solution)/shard_map/ppermute | solution.py:496
  244.5 1.5 collective-permute-start.38
  246.1 1.8 collective-permute-start.34
  249.6 4.6 %collective-permute-done.34 = bf16[160,768]{1,0:T(8,128)(2,1)S(1)} collective-permute-done((bf16[160,768]{1,0:T(8,128)(2,1)S(1)}, bf16[160,768]{1,0:T(8,128)(2,1)S(1)}, u32[]{:S(2)}, u32[]{:S(2)}) %collective-permute-start.34) | collective-permute-done | bytes 245792 | tf_op jit(solution)/shard_map/ppermute | solution.py:496
  256.4 13.4 %collective-permute-done.47 = bf16[768,768]{1,0:T(8,128)(2,1)} collective-permute-done((bf16[768,768]{1,0:T(8,128)(2,1)}, bf16[768,768]{1,0:T(8,128)(2,1)}, u32[]{:S(2)}, u32[]{:S(2)}) %collective-permute-start.47) | collective-permute-done | bytes 1179680 | tf_op jit(solution)/shard_map/ppermute | solution.py:496
  271.4 2.2 add_convert_fusion.3
  273.6 1.6 collective-permute-start.35
  275.2 28.4 %collective-permute-done.38 = bf16[1024,768]{1,0:T(8,128)(2,1)} collective-permute-done((bf16[1024,768]{1,0:T(8,128)(2,1)}, bf16[1024,768]{1,0:T(8,128)(2,1)}, u32[]{:S(2)}, u32[]{:S(2)}) %collective-permute-start.38) | collective-permute-done | bytes 1572896 | tf_op jit(solution)/shard_map/ppermute | solution.py:496
  305.1 2.0 add_convert_fusion
  307.8 9.9 %collective-permute-done.27 = bf16[512,768]{1,0:T(8,128)(2,1)S(1)} collective-permute-done((bf16[512,768]{1,0:T(8,128)(2,1)S(1)}, bf16[512,768]{1,0:T(8,128)(2,1)S(1)}, u32[]{:S(2)}, u32[]{:S(2)}) %collective-permute-start.27) | collective-permute-done | bytes 786464 | tf_op jit(solution)/shard_map/ppermute | solution.py:496
  318.0 1.6 collective-permute-start.28
  320.3 1.9 copy.78
  322.4 1.8 collective-permute-start.49
  324.2 6.3 %collective-permute-done.39 = bf16[512,768]{1,0:T(8,128)(2,1)S(1)} collective-permute-done((bf16[512,768]{1,0:T(8,128)(2,1)S(1)}, bf16[512,768]{1,0:T(8,128)(2,1)S(1)}, u32[]{:S(2)}, u32[]{:S(2)}) %collective-permute-start.39) | collective-permute-done | bytes 786464 | tf_op jit(solution)/shard_map/ppermute | solution.py:496
  330.7 1.8 collective-permute-start.40
  332.5 2.5 collective-permute-done.28
  336.1 2.8 collective-permute-done.40
  339.3 11.1 %collective-permute-done.50 = bf16[96,768]{1,0:T(8,128)(2,1)S(1)} collective-permute-done((bf16[96,768]{1,0:T(8,128)(2,1)S(1)}, bf16[96,768]{1,0:T(8,128)(2,1)S(1)}, u32[]{:S(2)}, u32[]{:S(2)}) %collective-permute-start.50) | collective-permute-done | bytes 147488 | tf_op jit(solution)/shard_map/ppermute | solution.py:496
  350.6 7.3 %collective-permute-done.41 = bf16[128,768]{1,0:T(8,128)(2,1)S(1)} collective-permute-done((bf16[128,768]{1,0:T(8,128)(2,1)S(1)}, bf16[128,768]{1,0:T(8,128)(2,1)S(1)}, u32[]{:S(2)}, u32[]{:S(2)}) %collective-permute-start.41) | collective-permute-done | bytes 196640 | tf_op jit(solution)/shard_map/ppermute | solution.py:496
  358.4 6.8 %collective-permute-done.51 = bf16[96,768]{1,0:T(8,128)(2,1)S(1)} collective-permute-done((bf16[96,768]{1,0:T(8,128)(2,1)S(1)}, bf16[96,768]{1,0:T(8,128)(2,1)S(1)}, u32[]{:S(2)}, u32[]{:S(2)}) %collective-permute-start.51) | collective-permute-done | bytes 147488 | tf_op jit(solution)/shard_map/ppermute | solution.py:496
  365.3 3.8 collective-permute-done.42
  370.6 4.8 %collective-permute-done.52 = bf16[192,768]{1,0:T(8,128)(2,1)S(1)} collective-permute-done((bf16[192,768]{1,0:T(8,128)(2,1)S(1)}, bf16[192,768]{1,0:T(8,128)(2,1)S(1)}, u32[]{:S(2)}, u32[]{:S(2)}) %collective-permute-start.52) | collective-permute-done | bytes 294944 | tf_op jit(solution)/shard_map/ppermute | solution.py:496
  375.6 1.6 collective-permute-start.53
  377.1 6.6 %collective-permute-done.43 = bf16[256,768]{1,0:T(8,128)(2,1)S(1)} collective-permute-done((bf16[256,768]{1,0:T(8,128)(2,1)S(1)}, bf16[256,768]{1,0:T(8,128)(2,1)S(1)}, u32[]{:S(2)}, u32[]{:S(2)}) %collective-permute-start.43) | collective-permute-done | bytes 393248 | tf_op jit(solution)/shard_map/ppermute | solution.py:496
  384.1 1.6 collective-permute-start.44
  387.0 1.9 copy.80
  388.9 3.0 collective-permute-done.53
  391.9 1.6 fusion.1
  393.5 14.2 %collective-permute-done.44 = bf16[512,768]{1,0:T(8,128)(2,1)S(1)} collective-permute-done((bf16[512,768]{1,0:T(8,128)(2,1)S(1)}, bf16[512,768]{1,0:T(8,128)(2,1)S(1)}, u32[]{:S(2)}, u32[]{:S(2)}) %collective-permute-start.44) | collective-permute-done | bytes 786464 | tf_op jit(solution)/shard_map/ppermute | solution.py:496
  408.4 1.6 slice_convert_fusion
  (197 shorter events, 48.6 us)
Async XLA Ops:
  0.6 74.5 %copy-start = (s32[4,8]{1,0:T(4,128)S(1)}, s32[4,8]{1,0:T(4,128)}, u32[]{:S(2)}) copy-start(s32[4,8]{1,0:T(4,128)} %param.29) | copy-start | bytes 388
  0.7 63.1 %collective-permute-start.10 = (bf16[768,768]{1,0:T(8,128)(2,1)}, bf16[768,768]{1,0:T(8,128)(2,1)}, u32[]{:S(2)}, u32[]{:S(2)}) collective-permute-start(bf16[768,768]{1,0:T(8,128)(2,1)} %wi0.3), channel_id=1, source_target_pairs={{0,2},{1,3},{2,0},{3,1},{4,6},{5,7},{6,4},{7,5},{8,10},{9,11},{10,... | collective-permute-start | bytes 3538952 | tf_op jit(solution)/shard_map/ppermute | solution.py:496
  3.7 60.2 %collective-permute-start.13 = (bf16[768,768]{1,0:T(8,128)(2,1)}, bf16[768,768]{1,0:T(8,128)(2,1)}, u32[]{:S(2)}, u32[]{:S(2)}) collective-permute-start(bf16[768,768]{1,0:T(8,128)(2,1)} %wb0.3), channel_id=1, source_target_pairs={{0,2},{1,3},{2,0},{3,1},{4,6},{5,7},{6,4},{7,5},{8,10},{9,11},{10,... | collective-permute-start | bytes 3538952 | tf_op jit(solution)/shard_map/ppermute | solution.py:496
  9.0 54.2 %copy-start.19 = (bf16[768,768]{1,0:T(8,128)(2,1)S(1)}, bf16[768,768]{1,0:T(8,128)(2,1)}, u32[]{:S(2)}) copy-start(bf16[768,768]{1,0:T(8,128)(2,1)} %wb0.3) | copy-start | bytes 3538948
  25.2 38.1 %copy-start.18 = (bf16[768,768]{1,0:T(8,128)(2,1)S(1)}, bf16[768,768]{1,0:T(8,128)(2,1)}, u32[]{:S(2)}) copy-start(bf16[768,768]{1,0:T(8,128)(2,1)} %wi0.3) | copy-start | bytes 3538948
  25.2 48.1 %copy-start.21 = (bf16[192,768]{1,0:T(8,128)(2,1)S(1)}, bf16[192,768]{1,0:T(8,128)(2,1)}, u32[]{:S(2)}) copy-start(bf16[192,768]{1,0:T(8,128)(2,1)} %wo0.3) | copy-start | bytes 884740
  25.2 50.0 %copy-start.12 = (f32[768]{0:T(1024)S(1)}, f32[768]{0:T(1024)}, u32[]{:S(2)}) copy-start(f32[768]{0:T(1024)} %param.20) | copy-start | bytes 9220
  25.3 50.6 %copy-start.13 = (f32[768]{0:T(1024)S(1)}, f32[768]{0:T(1024)}, u32[]{:S(2)}) copy-start(f32[768]{0:T(1024)} %param.26) | copy-start | bytes 9220
  25.3 51.2 %copy-start.14 = (f32[768]{0:T(1024)S(1)}, f32[768]{0:T(1024)}, u32[]{:S(2)}) copy-start(f32[768]{0:T(1024)} %param.19) | copy-start | bytes 9220
  25.3 51.8 %copy-start.15 = (f32[768]{0:T(1024)S(1)}, f32[768]{0:T(1024)}, u32[]{:S(2)}) copy-start(f32[768]{0:T(1024)} %param.21) | copy-start | bytes 9220
  25.3 52.4 %copy-start.16 = (f32[768]{0:T(1024)S(1)}, f32[768]{0:T(1024)}, u32[]{:S(2)}) copy-start(f32[768]{0:T(1024)} %param.25) | copy-start | bytes 9220
  25.3 52.9 %copy-start.17 = (f32[768]{0:T(1024)S(1)}, f32[768]{0:T(1024)}, u32[]{:S(2)}) copy-start(f32[768]{0:T(1024)} %param.27) | copy-start | bytes 9220
  27.4 36.0 %collective-permute-start.3 = (bf16[512,192]{1,0:T(8,128)(2,1)S(1)}, bf16[512,192]{1,0:T(8,128)(2,1)S(1)}, u32[]{:S(2)}, u32[]{:S(2)}) collective-permute-start(bf16[512,192]{1,0:T(8,128)(2,1)S(1)} %get-tuple-element.99), channel_id=1, source_target_pairs={{0,1},{1,0},{2,3},{3,2},{4,5},{5,4},{6,7},{7,6},{8,9},{9,8},{10,11... | collective-permute-start | bytes 589832 | tf_op jit(solution)/shard_map/ppermute | solution.py:496
  27.4 36.9 %collective-permute-start.4 = (bf16[512,192]{1,0:T(8,128)(2,1)S(1)}, bf16[512,192]{1,0:T(8,128)(2,1)S(1)}, u32[]{:S(2)}, u32[]{:S(2)}) collective-permute-start(bf16[512,192]{1,0:T(8,128)(2,1)S(1)} %get-tuple-element.98), channel_id=1, source_target_pairs={{0,2},{1,3},{2,0},{3,1},{4,6},{5,7},{6,4},{7,5},{8,10},{9,11},{10,... | collective-permute-start | bytes 589832 | tf_op jit(solution)/shard_map/ppermute | solution.py:496
  29.3 31.5 %collective-permute-start.1 = (f32[1,768]{1,0:T(1,128)S(1)}, f32[1,768]{1,0:T(1,128)S(1)}, u32[]{:S(2)}, u32[]{:S(2)}) collective-permute-start(f32[1,768]{1,0:T(1,128)S(1)} %broadcast_in_dim.48), channel_id=1, source_target_pairs={{0,2},{1,3},{2,0},{3,1},{4,6},{5,7},{6,4},{7,5},{8,10},{9,11},{10,... | collective-permute-start | bytes 9224 | tf_op jit(solution)/shard_map/ppermute | solution.py:496
  60.8 1.2 collective-permute-start
  62.0 1.2 collective-permute-start.2
  63.2 22.4 %collective-permute-start.12 = (bf16[768,768]{1,0:T(8,128)(2,1)S(1)}, bf16[768,768]{1,0:T(8,128)(2,1)}, u32[]{:S(2)}, u32[]{:S(2)}) collective-permute-start(bf16[768,768]{1,0:T(8,128)(2,1)S(1)} %copy-done.19), channel_id=1, source_target_pairs={{0,1},{1,0},{2,3},{3,2},{4,5},{5,4},{6,7},{7,6},{8,9},{9,8},{10,11... | collective-permute-start | bytes 3538952 | tf_op jit(solution)/shard_map/ppermute | solution.py:496
  63.3 22.2 %collective-permute-start.9 = (bf16[768,768]{1,0:T(8,128)(2,1)S(1)}, bf16[768,768]{1,0:T(8,128)(2,1)}, u32[]{:S(2)}, u32[]{:S(2)}) collective-permute-start(bf16[768,768]{1,0:T(8,128)(2,1)S(1)} %copy-done.18), channel_id=1, source_target_pairs={{0,1},{1,0},{2,3},{3,2},{4,5},{5,4},{6,7},{7,6},{8,9},{9,8},{10,11... | collective-permute-start | bytes 3538952 | tf_op jit(solution)/shard_map/ppermute | solution.py:496
  63.8 21.8 %collective-permute-start.11 = (bf16[768,768]{1,0:T(8,128)(2,1)}, bf16[768,768]{1,0:T(8,128)(2,1)}, u32[]{:S(2)}, u32[]{:S(2)}) collective-permute-start(bf16[768,768]{1,0:T(8,128)(2,1)} %collective-permute-done.10.wi2), channel_id=1, source_target_pairs={{0,1},{1,0},{2,3},{3,2},{4,5},{5,4},{6,7},{7,6},{8,9},{9,8},{10,11... | collective-permute-start | bytes 3538952 | tf_op jit(solution)/shard_map/ppermute | solution.py:496
  63.9 21.7 %collective-permute-start.14 = (bf16[768,768]{1,0:T(8,128)(2,1)}, bf16[768,768]{1,0:T(8,128)(2,1)}, u32[]{:S(2)}, u32[]{:S(2)}) collective-permute-start(bf16[768,768]{1,0:T(8,128)(2,1)} %collective-permute-done.13.wb2), channel_id=1, source_target_pairs={{0,1},{1,0},{2,3},{3,2},{4,5},{5,4},{6,7},{7,6},{8,9},{9,8},{10,11... | collective-permute-start | bytes 3538952 | tf_op jit(solution)/shard_map/ppermute | solution.py:496
  64.3 8.3 %collective-permute-start.5 = (bf16[512,192]{1,0:T(8,128)(2,1)S(1)}, bf16[512,192]{1,0:T(8,128)(2,1)S(1)}, u32[]{:S(2)}, u32[]{:S(2)}) collective-permute-start(bf16[512,192]{1,0:T(8,128)(2,1)S(1)} %get-tuple-element.97), channel_id=1, source_target_pairs={{0,3},{1,2},{2,1},{3,0},{4,7},{5,6},{6,5},{7,4},{8,11},{9,10},{10,... | collective-permute-start | bytes 589832 | tf_op jit(solution)/shard_map/ppermute | solution.py:496
  73.4 9.0 %collective-permute-start.7 = (bf16[192,768]{1,0:T(8,128)(2,1)S(1)}, bf16[192,768]{1,0:T(8,128)(2,1)S(1)}, u32[]{:S(2)}, u32[]{:S(2)}) collective-permute-start(bf16[192,768]{1,0:T(8,128)(2,1)S(1)} %copy-done.21), channel_id=1, source_target_pairs={{0,2},{1,3},{2,0},{3,1},{4,6},{5,7},{6,4},{7,5},{8,10},{9,11},{10,... | collective-permute-start | bytes 884744 | tf_op jit(solution)/shard_map/ppermute | solution.py:496
  82.4 1.6 collective-permute-start.6
  84.0 1.6 collective-permute-start.8
  107.6 5.0 %collective-permute-start.15 = (bf16[1,8,1664]{2,1,0:T(8,128)(2,1)}, bf16[1,8,1664]{2,1,0:T(8,128)(2,1)S(1)}, u32[]{:S(2)}, u32[]{:S(2)}) collective-permute-start(bf16[1,8,1664]{2,1,0:T(8,128)(2,1)} %bitcast.81), channel_id=1, source_target_pairs={{0,16},{4,20},{8,24},{12,28},{16,0},{20,4},{24,8},{28,12},{1,17},{... | collective-permute-start | bytes 79880 | tf_op jit(solution)/shard_map/ppermute | solution.py:496
  113.5 4.2 %collective-permute-start.16 = (bf16[2,8,1664]{2,1,0:T(8,128)(2,1)S(1)}, bf16[2,8,1664]{2,1,0:T(8,128)(2,1)S(1)}, u32[]{:S(2)}, u32[]{:S(2)}) collective-permute-start(bf16[2,8,1664]{2,1,0:T(8,128)(2,1)S(1)} %maximum_select_fusion.19), channel_id=1, source_target_pairs={{0,8},{4,12},{8,0},{12,4},{16,24},{20,28},{24,16},{28,20},{1,9},{5... | collective-permute-start | bytes 159752 | tf_op jit(solution)/shard_map/ppermute | solution.py:496
  117.7 4.8 %collective-permute-start.17 = (bf16[4,8,1664]{2,1,0:T(8,128)(2,1)S(1)}, bf16[4,8,1664]{2,1,0:T(8,128)(2,1)S(1)}, u32[]{:S(2)}, u32[]{:S(2)}) collective-permute-start(bf16[4,8,1664]{2,1,0:T(8,128)(2,1)S(1)} %bitcast.77), channel_id=1, source_target_pairs={{0,4},{4,0},{8,12},{12,8},{16,20},{20,16},{24,28},{28,24},{1,5},{5... | collective-permute-start | bytes 319496 | tf_op jit(solution)/shard_map/ppermute | solution.py:496
  122.6 5.9 %collective-permute-start.18 = (bf16[8,8,1664]{2,1,0:T(8,128)(2,1)S(1)}, bf16[8,8,1664]{2,1,0:T(8,128)(2,1)S(1)}, u32[]{:S(2)}, u32[]{:S(2)}) collective-permute-start(bf16[8,8,1664]{2,1,0:T(8,128)(2,1)S(1)} %bitcast.74), channel_id=1, source_target_pairs={{0,2},{1,3},{2,0},{3,1},{4,6},{5,7},{6,4},{7,5},{8,10},{9,11},{10,... | collective-permute-start | bytes 638984 | tf_op jit(solution)/shard_map/ppermute | solution.py:496
  128.6 1.8 collective-permute-start.19
  160.3 2.0 collective-permute-start.22
  160.5 9.3 %collective-permute-start.23 = (bf16[512,192]{1,0:T(8,128)(2,1)}, bf16[512,192]{1,0:T(8,128)(2,1)S(1)}, u32[]{:S(2)}, u32[]{:S(2)}) collective-permute-start(bf16[512,192]{1,0:T(8,128)(2,1)} %get-tuple-element.75), channel_id=1, source_target_pairs={{0,2},{1,3},{2,0},{3,1},{4,6},{5,7},{6,4},{7,5},{8,10},{9,11},{10,... | collective-permute-start | bytes 589832 | tf_op jit(solution)/shard_map/ppermute | solution.py:496
  162.2 12.1 %collective-permute-start.24 = (bf16[512,192]{1,0:T(8,128)(2,1)}, bf16[512,192]{1,0:T(8,128)(2,1)S(1)}, u32[]{:S(2)}, u32[]{:S(2)}) collective-permute-start(bf16[512,192]{1,0:T(8,128)(2,1)} %get-tuple-element.76), channel_id=1, source_target_pairs={{0,3},{1,2},{2,1},{3,0},{4,7},{5,6},{6,5},{7,4},{8,11},{9,10},{10,... | collective-permute-start | bytes 589832 | tf_op jit(solution)/shard_map/ppermute | solution.py:496
  198.2 13.6 %collective-permute-start.30 = (bf16[320,768]{1,0:T(8,128)(2,1)S(1)}, bf16[320,768]{1,0:T(8,128)(2,1)S(1)}, u32[]{:S(2)}, u32[]{:S(2)}) collective-permute-start(bf16[320,768]{1,0:T(8,128)(2,1)S(1)} %constant_dynamic-slice_fusion.9), channel_id=1, source_target_pairs={{0,4},{4,0},{8,12},{12,8},{16,20},{20,16},{24,28},{28,24},{1,5},{5... | collective-permute-start | bytes 1474568 | tf_op jit(solution)/shard_map/ppermute | solution.py:496
  200.0 30.6 %collective-permute-start.46 = (bf16[768,768]{1,0:T(8,128)(2,1)}, bf16[768,768]{1,0:T(8,128)(2,1)}, u32[]{:S(2)}, u32[]{:S(2)}) collective-permute-start(bf16[768,768]{1,0:T(8,128)(2,1)} %get-tuple-element.96), channel_id=1, source_target_pairs={{0,1},{1,0},{2,3},{3,2},{4,5},{5,4},{6,7},{7,6},{8,9},{9,8},{10,11... | collective-permute-start | bytes 3538952 | tf_op jit(solution)/shard_map/ppermute | solution.py:496
  209.4 25.4 %collective-permute-start.37 = (bf16[1024,768]{1,0:T(8,128)(2,1)}, bf16[1024,768]{1,0:T(8,128)(2,1)S(1)}, u32[]{:S(2)}, u32[]{:S(2)}) collective-permute-start(bf16[1024,768]{1,0:T(8,128)(2,1)} %get-tuple-element.92), channel_id=1, source_target_pairs={{0,1},{1,0},{2,3},{3,2},{4,5},{5,4},{6,7},{7,6},{8,9},{9,8},{10,11... | collective-permute-start | bytes 4718600 | tf_op jit(solution)/shard_map/ppermute | solution.py:496
  211.9 7.6 %collective-permute-start.31 = (bf16[160,768]{1,0:T(8,128)(2,1)S(1)}, bf16[160,768]{1,0:T(8,128)(2,1)}, u32[]{:S(2)}, u32[]{:S(2)}) collective-permute-start(bf16[160,768]{1,0:T(8,128)(2,1)S(1)} %constant_dynamic-slice_fusion.8), channel_id=1, source_target_pairs={{0,8},{4,12},{8,0},{12,4},{16,24},{20,28},{24,16},{28,20},{1,9},{5... | collective-permute-start | bytes 737288 | tf_op jit(solution)/shard_map/ppermute | solution.py:496
  221.2 7.7 %collective-permute-start.32 = (bf16[80,768]{1,0:T(8,128)(2,1)}, bf16[80,768]{1,0:T(8,128)(2,1)S(1)}, u32[]{:S(2)}, u32[]{:S(2)}) collective-permute-start(bf16[80,768]{1,0:T(8,128)(2,1)} %constant_dynamic-slice_fusion.7), channel_id=1, source_target_pairs={{0,16},{4,20},{8,24},{12,28},{16,0},{20,4},{24,8},{28,12},{1,17},{... | collective-permute-start | bytes 368648 | tf_op jit(solution)/shard_map/ppermute | solution.py:496
  224.0 20.5 %collective-permute-start.20 = (bf16[512,768]{1,0:T(8,128)(2,1)S(1)}, bf16[512,768]{1,0:T(8,128)(2,1)S(1)}, u32[]{:S(2)}, u32[]{:S(2)}) collective-permute-start(bf16[512,768]{1,0:T(8,128)(2,1)S(1)} %copy-done.2), channel_id=1, source_target_pairs={{0,2},{1,3},{2,0},{3,1},{4,6},{5,7},{6,4},{7,5},{8,10},{9,11},{10,... | collective-permute-start | bytes 2359304 | tf_op jit(solution)/shard_map/ppermute | solution.py:496
  225.5 30.3 %collective-permute-start.45 = (bf16[768,768]{1,0:T(8,128)(2,1)}, bf16[768,768]{1,0:T(8,128)(2,1)}, u32[]{:S(2)}, u32[]{:S(2)}) collective-permute-start(bf16[768,768]{1,0:T(8,128)(2,1)} %get-tuple-element.94), channel_id=1, source_target_pairs={{0,1},{1,0},{2,3},{3,2},{4,5},{5,4},{6,7},{7,6},{8,9},{9,8},{10,11... | collective-permute-start | bytes 3538952 | tf_op jit(solution)/shard_map/ppermute | solution.py:496
  229.6 16.4 %collective-permute-start.26 = (bf16[512,768]{1,0:T(8,128)(2,1)}, bf16[512,768]{1,0:T(8,128)(2,1)}, u32[]{:S(2)}, u32[]{:S(2)}) collective-permute-start(bf16[512,768]{1,0:T(8,128)(2,1)} %get-tuple-element.81), channel_id=1, source_target_pairs={{0,1},{1,0},{2,3},{3,2},{4,5},{5,4},{6,7},{7,6},{8,9},{9,8},{10,11... | collective-permute-start | bytes 2359304 | tf_op jit(solution)/shard_map/ppermute | solution.py:496
  230.6 13.9 %collective-permute-start.33 = (bf16[80,768]{1,0:T(8,128)(2,1)S(1)}, bf16[80,768]{1,0:T(8,128)(2,1)S(1)}, u32[]{:S(2)}, u32[]{:S(2)}) collective-permute-start(bf16[80,768]{1,0:T(8,128)(2,1)S(1)} %add_convert_fusion.17), channel_id=1, source_target_pairs={{0,16},{4,20},{8,24},{12,28},{16,0},{20,4},{24,8},{28,12},{1,17},{... | collective-permute-start | bytes 368648 | tf_op jit(solution)/shard_map/ppermute | solution.py:496
  234.8 35.1 %collective-permute-start.47 = (bf16[768,768]{1,0:T(8,128)(2,1)}, bf16[768,768]{1,0:T(8,128)(2,1)}, u32[]{:S(2)}, u32[]{:S(2)}) collective-permute-start(bf16[768,768]{1,0:T(8,128)(2,1)} %add_convert_fusion.4), channel_id=1, source_target_pairs={{0,2},{1,3},{2,0},{3,1},{4,6},{5,7},{6,4},{7,5},{8,10},{9,11},{10,... | collective-permute-start | bytes 3538952 | tf_op jit(solution)/shard_map/ppermute | solution.py:496
  244.5 29.1 %collective-permute-start.36 = (bf16[1024,768]{1,0:T(8,128)(2,1)}, bf16[1024,768]{1,0:T(8,128)(2,1)S(1)}, u32[]{:S(2)}, u32[]{:S(2)}) collective-permute-start(bf16[1024,768]{1,0:T(8,128)(2,1)} %get-tuple-element.90), channel_id=1, source_target_pairs={{0,1},{1,0},{2,3},{3,2},{4,5},{5,4},{6,7},{7,6},{8,9},{9,8},{10,11... | collective-permute-start | bytes 4718600 | tf_op jit(solution)/shard_map/ppermute | solution.py:496
  244.5 59.1 %collective-permute-start.38 = (bf16[1024,768]{1,0:T(8,128)(2,1)}, bf16[1024,768]{1,0:T(8,128)(2,1)}, u32[]{:S(2)}, u32[]{:S(2)}) collective-permute-start(bf16[1024,768]{1,0:T(8,128)(2,1)} %add_convert_fusion.1), channel_id=1, source_target_pairs={{0,2},{1,3},{2,0},{3,1},{4,6},{5,7},{6,4},{7,5},{8,10},{9,11},{10,... | collective-permute-start | bytes 4718600 | tf_op jit(solution)/shard_map/ppermute | solution.py:496
  246.1 8.2 %collective-permute-start.34 = (bf16[160,768]{1,0:T(8,128)(2,1)S(1)}, bf16[160,768]{1,0:T(8,128)(2,1)S(1)}, u32[]{:S(2)}, u32[]{:S(2)}) collective-permute-start(bf16[160,768]{1,0:T(8,128)(2,1)S(1)} %maximum_select_fusion.15), channel_id=1, source_target_pairs={{0,8},{4,12},{8,0},{12,4},{16,24},{20,28},{24,16},{28,20},{1,9},{5... | collective-permute-start | bytes 737288 | tf_op jit(solution)/shard_map/ppermute | solution.py:496
  254.2 65.4 %collective-permute-start.21 = (bf16[2,512,768]{2,1,0:T(8,128)(2,1)S(1)}, bf16[2,512,768]{2,1,0:T(8,128)(2,1)S(1)}, u32[]{:S(2)}, u32[]{:S(2)}) collective-permute-start(bf16[2,512,768]{2,1,0:T(8,128)(2,1)S(1)} %maximum_select_fusion.2), channel_id=1, source_target_pairs={{0,1},{1,0},{2,3},{3,2},{4,5},{5,4},{6,7},{7,6},{8,9},{9,8},{10,11... | collective-permute-start | bytes 4718600 | tf_op jit(solution)/shard_map/ppermute | solution.py:496
  255.9 51.3 %collective-permute-start.25 = (bf16[512,768]{1,0:T(8,128)(2,1)S(1)}, bf16[512,768]{1,0:T(8,128)(2,1)S(1)}, u32[]{:S(2)}, u32[]{:S(2)}) collective-permute-start(bf16[512,768]{1,0:T(8,128)(2,1)S(1)} %copy-done.20), channel_id=1, source_target_pairs={{0,1},{1,0},{2,3},{3,2},{4,5},{5,4},{6,7},{7,6},{8,9},{9,8},{10,11... | collective-permute-start | bytes 2359304 | tf_op jit(solution)/shard_map/ppermute | solution.py:496
  269.9 47.8 %collective-permute-start.27 = (bf16[512,768]{1,0:T(8,128)(2,1)S(1)}, bf16[512,768]{1,0:T(8,128)(2,1)S(1)}, u32[]{:S(2)}, u32[]{:S(2)}) collective-permute-start(bf16[512,768]{1,0:T(8,128)(2,1)S(1)} %add_convert_fusion.8), channel_id=1, source_target_pairs={{0,2},{1,3},{2,0},{3,1},{4,6},{5,7},{6,4},{7,5},{8,10},{9,11},{10,... | collective-permute-start | bytes 2359304 | tf_op jit(solution)/shard_map/ppermute | solution.py:496
  273.6 84.3 %collective-permute-start.35 = (bf16[320,768]{1,0:T(8,128)(2,1)S(1)}, bf16[320,768]{1,0:T(8,128)(2,1)S(1)}, u32[]{:S(2)}, u32[]{:S(2)}) collective-permute-start(bf16[320,768]{1,0:T(8,128)(2,1)S(1)} %maximum_select_fusion.11), channel_id=1, source_target_pairs={{0,4},{4,0},{8,12},{12,8},{16,20},{20,16},{24,28},{28,24},{1,5},{5... | collective-permute-start | bytes 1474568 | tf_op jit(solution)/shard_map/ppermute | solution.py:496
  303.6 18.6 %collective-permute-start.48 = (bf16[384,768]{1,0:T(8,128)(2,1)S(1)}, bf16[384,768]{1,0:T(8,128)(2,1)S(1)}, u32[]{:S(2)}, u32[]{:S(2)}) collective-permute-start(bf16[384,768]{1,0:T(8,128)(2,1)S(1)} %constant_dynamic-slice_fusion.3), channel_id=1, source_target_pairs={{0,4},{4,0},{8,12},{12,8},{16,20},{20,16},{24,28},{28,24},{1,5},{5... | collective-permute-start | bytes 1769480 | tf_op jit(solution)/shard_map/ppermute | solution.py:496
  307.2 23.3 %collective-permute-start.39 = (bf16[512,768]{1,0:T(8,128)(2,1)S(1)}, bf16[512,768]{1,0:T(8,128)(2,1)S(1)}, u32[]{:S(2)}, u32[]{:S(2)}) collective-permute-start(bf16[512,768]{1,0:T(8,128)(2,1)S(1)} %constant_dynamic-slice_fusion.6), channel_id=1, source_target_pairs={{0,4},{4,0},{8,12},{12,8},{16,20},{20,16},{24,28},{28,24},{1,5},{5... | collective-permute-start | bytes 2359304 | tf_op jit(solution)/shard_map/ppermute | solution.py:496
  318.0 17.0 %collective-permute-start.28 = (bf16[512,768]{1,0:T(8,128)(2,1)S(1)}, bf16[512,768]{1,0:T(8,128)(2,1)S(1)}, u32[]{:S(2)}, u32[]{:S(2)}) collective-permute-start(bf16[512,768]{1,0:T(8,128)(2,1)S(1)} %add_convert_fusion.7), channel_id=1, source_target_pairs={{0,2},{1,3},{2,0},{3,1},{4,6},{5,7},{6,4},{7,5},{8,10},{9,11},{10,... | collective-permute-start | bytes 2359304 | tf_op jit(solution)/shard_map/ppermute | solution.py:496
  322.4 13.0 %collective-permute-start.49 = (bf16[192,768]{1,0:T(8,128)(2,1)S(1)}, bf16[192,768]{1,0:T(8,128)(2,1)S(1)}, u32[]{:S(2)}, u32[]{:S(2)}) collective-permute-start(bf16[192,768]{1,0:T(8,128)(2,1)S(1)} %constant_dynamic-slice_fusion.2), channel_id=1, source_target_pairs={{0,8},{4,12},{8,0},{12,4},{16,24},{20,28},{24,16},{28,20},{1,9},{5... | collective-permute-start | bytes 884744 | tf_op jit(solution)/shard_map/ppermute | solution.py:496
  330.7 8.1 %collective-permute-start.40 = (bf16[256,768]{1,0:T(8,128)(2,1)S(1)}, bf16[256,768]{1,0:T(8,128)(2,1)S(1)}, u32[]{:S(2)}, u32[]{:S(2)}) collective-permute-start(bf16[256,768]{1,0:T(8,128)(2,1)S(1)} %constant_dynamic-slice_fusion.5), channel_id=1, source_target_pairs={{0,8},{4,12},{8,0},{12,4},{16,24},{20,28},{24,16},{28,20},{1,9},{5... | collective-permute-start | bytes 1179656 | tf_op jit(solution)/shard_map/ppermute | solution.py:496
  335.3 51.2 %collective-permute-start.29 = (bf16[2,512,768]{2,1,0:T(8,128)(2,1)S(1)}, bf16[2,512,768]{2,1,0:T(8,128)(2,1)S(1)}, u32[]{:S(2)}, u32[]{:S(2)}) collective-permute-start(bf16[2,512,768]{2,1,0:T(8,128)(2,1)S(1)} %maximum_select_fusion.4), channel_id=1, source_target_pairs={{0,1},{1,0},{2,3},{3,2},{4,5},{5,4},{6,7},{7,6},{8,9},{9,8},{10,11... | collective-permute-start | bytes 4718600 | tf_op jit(solution)/shard_map/ppermute | solution.py:496
  335.5 15.0 %collective-permute-start.50 = (bf16[96,768]{1,0:T(8,128)(2,1)S(1)}, bf16[96,768]{1,0:T(8,128)(2,1)S(1)}, u32[]{:S(2)}, u32[]{:S(2)}) collective-permute-start(bf16[96,768]{1,0:T(8,128)(2,1)S(1)} %constant_dynamic-slice_fusion.1), channel_id=1, source_target_pairs={{0,16},{4,20},{8,24},{12,28},{16,0},{20,4},{24,8},{28,12},{1,17},{... | collective-permute-start | bytes 442376 | tf_op jit(solution)/shard_map/ppermute | solution.py:496
  339.0 18.8 %collective-permute-start.41 = (bf16[128,768]{1,0:T(8,128)(2,1)S(1)}, bf16[128,768]{1,0:T(8,128)(2,1)S(1)}, u32[]{:S(2)}, u32[]{:S(2)}) collective-permute-start(bf16[128,768]{1,0:T(8,128)(2,1)S(1)} %constant_dynamic-slice_fusion.4), channel_id=1, source_target_pairs={{0,16},{4,20},{8,24},{12,28},{16,0},{20,4},{24,8},{28,12},{1,17},{... | collective-permute-start | bytes 589832 | tf_op jit(solution)/shard_map/ppermute | solution.py:496
  350.5 14.7 %collective-permute-start.51 = (bf16[96,768]{1,0:T(8,128)(2,1)S(1)}, bf16[96,768]{1,0:T(8,128)(2,1)S(1)}, u32[]{:S(2)}, u32[]{:S(2)}) collective-permute-start(bf16[96,768]{1,0:T(8,128)(2,1)S(1)} %add_convert_fusion.16), channel_id=1, source_target_pairs={{0,16},{4,20},{8,24},{12,28},{16,0},{20,4},{24,8},{28,12},{1,17},{... | collective-permute-start | bytes 442376 | tf_op jit(solution)/shard_map/ppermute | solution.py:496
  357.9 11.2 %collective-permute-start.42 = (bf16[128,768]{1,0:T(8,128)(2,1)S(1)}, bf16[128,768]{1,0:T(8,128)(2,1)S(1)}, u32[]{:S(2)}, u32[]{:S(2)}) collective-permute-start(bf16[128,768]{1,0:T(8,128)(2,1)S(1)} %add_convert_fusion.15), channel_id=1, source_target_pairs={{0,16},{4,20},{8,24},{12,28},{16,0},{20,4},{24,8},{28,12},{1,17},{... | collective-permute-start | bytes 589832 | tf_op jit(solution)/shard_map/ppermute | solution.py:496
  365.2 10.2 %collective-permute-start.52 = (bf16[192,768]{1,0:T(8,128)(2,1)S(1)}, bf16[192,768]{1,0:T(8,128)(2,1)S(1)}, u32[]{:S(2)}, u32[]{:S(2)}) collective-permute-start(bf16[192,768]{1,0:T(8,128)(2,1)S(1)} %maximum_select_fusion.14), channel_id=1, source_target_pairs={{0,8},{4,12},{8,0},{12,4},{16,24},{20,28},{24,16},{28,20},{1,9},{5... | collective-permute-start | bytes 884744 | tf_op jit(solution)/shard_map/ppermute | solution.py:496
  369.2 14.6 %collective-permute-start.43 = (bf16[256,768]{1,0:T(8,128)(2,1)S(1)}, bf16[256,768]{1,0:T(8,128)(2,1)S(1)}, u32[]{:S(2)}, u32[]{:S(2)}) collective-permute-start(bf16[256,768]{1,0:T(8,128)(2,1)S(1)} %maximum_select_fusion.13), channel_id=1, source_target_pairs={{0,8},{4,12},{8,0},{12,4},{16,24},{20,28},{24,16},{28,20},{1,9},{5... | collective-permute-start | bytes 1179656 | tf_op jit(solution)/shard_map/ppermute | solution.py:496
  375.6 16.3 %collective-permute-start.53 = (bf16[384,768]{1,0:T(8,128)(2,1)S(1)}, bf16[384,768]{1,0:T(8,128)(2,1)S(1)}, u32[]{:S(2)}, u32[]{:S(2)}) collective-permute-start(bf16[384,768]{1,0:T(8,128)(2,1)S(1)} %maximum_select_fusion.10), channel_id=1, source_target_pairs={{0,4},{4,0},{8,12},{12,8},{16,20},{20,16},{24,28},{28,24},{1,5},{5... | collective-permute-start | bytes 1769480 | tf_op jit(solution)/shard_map/ppermute | solution.py:496
  384.1 23.6 %collective-permute-start.44 = (bf16[512,768]{1,0:T(8,128)(2,1)S(1)}, bf16[512,768]{1,0:T(8,128)(2,1)S(1)}, u32[]{:S(2)}, u32[]{:S(2)}) collective-permute-start(bf16[512,768]{1,0:T(8,128)(2,1)S(1)} %maximum_select_fusion.9), channel_id=1, source_target_pairs={{0,4},{4,0},{8,12},{12,8},{16,20},{20,16},{24,28},{28,24},{1,5},{5... | collective-permute-start | bytes 2359304 | tf_op jit(solution)/shard_map/ppermute | solution.py:496
  (21 other events, 163.0 us)

commit v2 on v1

--- a/solution.py
+++ b/solution.py
@@ -89,14 +89,15 @@
     return pieces
 
 
-def attend_forward(m_ref, tok_ref, w_ref, b_ref, seg_ref, win_ref, qkv_ref, prob_ref, ctx_ref):
+def attend_forward(m_ref, tok_ref, w_ref, b_ref, seg_ref, win_ref, qkv_ref, prob_ref, *refs):
+    ctx_refs, ctx_v = refs[:-1], refs[-1]
     length = tok_ref.shape[0]
-    width = w_ref.shape[2]
+    width = w_ref.shape[1]
     heads = width // HEAD_DIM
     tok = tok_ref[...]
-    q = ((product(tok, w_ref[0]) + b_ref[0:1, :]).astype(bf16) * HEAD_DIM**-0.5).astype(bf16)
-    k = product(tok, w_ref[1]).astype(bf16)
-    v = (product(tok, w_ref[2]) + b_ref[1:2, :]).astype(bf16)
+    q = ((product_nt(tok, w_ref[0]) + b_ref[0:1, :]).astype(bf16) * HEAD_DIM**-0.5).astype(bf16)
+    k = product_nt(tok, w_ref[1]).astype(bf16)
+    v = (product_nt(tok, w_ref[2]) + b_ref[1:2, :]).astype(bf16)
     qkv_ref[0, 0] = q
     qkv_ref[0, 1] = k
     qkv_ref[0, 2] = v
@@ -119,18 +120,28 @@
             prob_ref[0, head * (length // Q_BLOCK) + block] = low
             results.append(product(low, value))
         for first, merged in merge_heads(results, width):
-            ctx_ref[0, at : at + Q_BLOCK, first : first + merged.shape[1]] = merged.astype(bf16)
-
-
-def attend_backward(
-    m_ref, tok_ref, w_ref, qkv_ref, prob_ref, g0_ref, g1_ref, g2_ref, g3_ref,
-    dw_ref, o0_ref, o1_ref, o2_ref, o3_ref, gctx, gk_sum, gv_sum, dw_sum, vec_sum,
-):
+            ctx_v[at : at + Q_BLOCK, first : first + merged.shape[1]] = merged.astype(bf16)
+    for piece, ctx_ref in enumerate(ctx_refs):
+
+        @pl.when(pl.program_id(0) == piece)
+        def _():
+            ctx_ref[...] = ctx_v[...]
+
+
+def attend_backward(count, first, last, m_ref, tok_ref, w_ref, qkv_ref, prob_ref, *refs):
+    g_refs, refs = refs[:count], refs[count:]
+    if not first:
+        before_ref, vec_before_ref, *refs = refs
+    o_refs, refs = refs[:count], refs[count:]
+    if last:
+        dw_ref, gctx, gk_sum, gv_sum, dw_sum, vec_sum = refs
+    else:
+        dw_ref, vec_ref, gctx, gk_sum, gv_sum, dw_sum, vec_sum = refs
     step = pl.program_id(0)
     length = tok_ref.shape[0]
-    width = w_ref.shape[2]
+    width = w_ref.shape[1]
     heads = width // HEAD_DIM
-    for piece, g_ref in enumerate((g0_ref, g1_ref, g2_ref, g3_ref)):
+    for piece, g_ref in enumerate(g_refs):
 
         @pl.when(step == piece)
         def _():
@@ -138,8 +149,8 @@
 
     @pl.when(step == 0)
     def _():
-        dw_sum[...] = jnp.zeros_like(dw_sum)
-        vec_sum[...] = jnp.zeros_like(vec_sum)
+        dw_sum[...] = jnp.zeros_like(dw_sum) if first else before_ref[...]
+        vec_sum[...] = jnp.zeros_like(vec_sum) if first else vec_before_ref[...]
 
     gk_sum[...] = jnp.zeros_like(gk_sum)
     gv_sum[...] = jnp.zeros_like(gv_sum)
@@ -185,25 +196,33 @@
     back = None
     for c, grad in enumerate((gq, gk, gv)):
         dw_sum[c * width : (c + 1) * width, :] += product_t(grad, tok)
-        term = product_nt(grad, w_ref[c])
+        term = product(grad, w_ref[c])
         back = term if back is None else back + term
     vec_sum[0:1, :] += jnp.sum(gq.astype(f32), axis=0, keepdims=True)
     vec_sum[1:2, :] += jnp.sum(gv.astype(f32), axis=0, keepdims=True)
     back = back.astype(bf16)
-    for piece, o_ref in enumerate((o0_ref, o1_ref, o2_ref, o3_ref)):
+    for piece, o_ref in enumerate(o_refs):
 
         @pl.when(step == piece)
         def _():
             o_ref[...] = back
 
-    @pl.when(step == pl.num_programs(0) - 1)
+    @pl.when(step == count - 1)
     def _():
+        if not last:
+            dw_ref[...] = dw_sum[...]
+            vec_ref[...] = vec_sum[...]
+            return
         dw_ref[0 : 3 * width, :] = dw_sum[...].astype(bf16)
         vec = vec_sum[...]
         top = vec.astype(bf16)
         rest = (vec - top.astype(f32)).astype(bf16)
         dw_ref[3 * width :, :] = jnp.zeros((VEC_ROWS, dw_ref.shape[1]), bf16)
         dw_ref[3 * width : 3 * width + 16, 0:width] = jnp.concatenate([top, rest], axis=0)
+
+
+def row_of(ref):
+    return jnp.concatenate([ref[i : i + 1, :] for i in range(ref.shape[0])], axis=1)
 
 
 def start_all(pairs, sems):
@@ -215,21 +234,53 @@
     return copies
 
 
-def middle_forward(
-    m_ref, tok_hbm, seg_ref, pair_ref, b_out, gain1, shift1, b_in, b_back, gain2, shift2,
-    c0, c1, c2, c3, wo0, wo1, wo2, wo3, wi0, wi1, wi2, wi3, wb0, wb1, wb2, wb3,
-    act_hbm, slope_hbm, xhat1_ref, rstd1_ref, low1_ref, xhat2_ref, rstd2_ref, out_ref, pooled_ref, len_ref, msg_ref,
-    tok_v, ctx_v, wo_v, wi_v, wb_v, act_v, slope_v, resid, sems, out_sems,
+def prepare(bits_ref, bias_ref, out_ref, in_hbm, back_hbm, pack_ref, in_ref, back_ref, sems):
+    quarter = in_ref.shape[0]
+    in_at = pl.multiple_of(bits_ref[0] * quarter, quarter)
+    back_at = pl.multiple_of(bits_ref[1] * quarter, quarter)
+    copies = start_all(
+        [(in_hbm.at[pl.ds(in_at, quarter)], in_ref), (back_hbm.at[pl.ds(back_at, quarter)], back_ref)], sems
+    )
+    local = out_ref.shape[0]
+    bias = row_of(bias_ref)
+    high = bias.astype(bf16)
+    rest = bias - high.astype(f32)
+    middle = rest.astype(bf16)
+    low = (rest - middle.astype(f32)).astype(bf16)
+    slot = lax.broadcasted_iota(jnp.int32, (16, 1), 0)
+    rows = jnp.where(slot == 0, high.astype(f32), 0.0)
+    rows = jnp.where(slot == 1, middle.astype(f32), rows)
+    rows = jnp.where(slot == 2, low.astype(f32), rows)
+    pack_ref[0:local, :] = out_ref[...]
+    pack_ref[local : local + 16, :] = rows.astype(bf16)
+    for copy in copies:
+        copy.wait()
+
+
+def feed(r, low_ref, wi_v, b_in, act_v, slope_v):
+    for first in range(0, wi_v.shape[2], TILE):
+        cols = slice(first, first + TILE)
+        before = product(low_ref[...], wi_v[r, :, cols]) + b_in[:, cols]
+        active, slope = gelu_and_slope(before)
+        act_v[r, :, cols] = active.astype(bf16)
+        slope_v[r, :, cols] = slope.astype(bf16)
+
+
+def middle_first(
+    m_ref, tok_hbm, bias_ref, gain_ref, shift_ref, c0, c1, c2, c3, wo0, wo1, wo2, wo3, wi0, wi1, wb0, wb1,
+    act_hbm, slope_hbm, xhat1_ref, rstd1_ref, low1_ref, total_ref,
+    tok_v, ctx_v, wo_v, wi_v, wb_v, act_v, slope_v, sems, out_sems,
 ):
     length, width = tok_v.shape
-    units = wi_v.shape[2]
+    local = ctx_v.shape[2]
+    b_out, gain1, shift1 = row_of(bias_ref), row_of(gain_ref), row_of(shift_ref)
     at = pl.multiple_of(m_ref[0] * length, length)
     copies = start_all(
         [(tok_hbm.at[pl.ds(at, length)], tok_v)]
         + [(c, ctx_v.at[r]) for r, c in enumerate((c0, c1, c2, c3))]
         + [(w, wo_v.at[r]) for r, w in enumerate((wo0, wo1, wo2, wo3))]
-        + [(w, wi_v.at[r]) for r, w in enumerate((wi0, wi1, wi2, wi3))]
-        + [(w, wb_v.at[r]) for r, w in enumerate((wb0, wb1, wb2, wb3))],
+        + [(w, wi_v.at[r]) for r, w in enumerate((wi0, wi1))]
+        + [(w, wb_v.at[r]) for r, w in enumerate((wb0, wb1))],
         sems,
     )
     for copy in copies[:9]:
@@ -238,43 +289,69 @@
         cols = slice(first, first + TILE)
         total = tok_v[:, cols].astype(f32) + b_out[:, cols]
         for r in range(4):
-            total = total + product(ctx_v[r], wo_v[r, :, cols])
-        resid[:, cols] = total
+            total = total + product(ctx_v[r], wo_v[r, 0:local, cols])
+        total_ref[:, cols] = total
 
     @pl.loop(0, length // ROW_TILE)
     def _(i):
         rows = pl.ds(pl.multiple_of(i * ROW_TILE, ROW_TILE), ROW_TILE)
-        values = resid[rows, :]
+        values = total_ref[rows, :]
         center = values - jnp.mean(values, axis=-1, keepdims=True)
         rate = lax.rsqrt(jnp.mean(center * center, axis=-1, keepdims=True) + norm_eps)
         xhat = center * rate
         xhat1_ref[rows, :] = xhat
         rstd1_ref[rows, :] = jnp.broadcast_to(rate, (ROW_TILE, LANES))
-        normed = xhat * gain1[...] + shift1[...]
-        resid[rows, :] = normed
+        normed = xhat * gain1 + shift1
+        total_ref[rows, :] = normed
         low1_ref[rows, :] = normed.astype(bf16)
 
     outs = []
-    for r in range(4):
+    for r in range(2):
         copies[9 + r].wait()
-        for first in range(0, units, TILE):
-            cols = slice(first, first + TILE)
-            before = product(low1_ref[...], wi_v[r, :, cols]) + b_in[r : r + 1, cols]
-            active, slope = gelu_and_slope(before)
-            act_v[r, :, cols] = active.astype(bf16)
-            slope_v[r, :, cols] = slope.astype(bf16)
+        b_in = jnp.sum(wo_v[r, local : local + 16, :].astype(f32), axis=0, keepdims=True)
+        feed(r, low1_ref, wi_v, b_in, act_v, slope_v)
         outs += start_all(
             [(act_v.at[r], act_hbm.at[r]), (slope_v.at[r], slope_hbm.at[r])],
             out_sems.at[pl.ds(2 * r, 2)],
         )
-    for r in range(4):
-        copies[13 + r].wait()
+    for copy in copies[11:]:
+        copy.wait()
+    for first in range(0, width, TILE):
+        cols = slice(first, first + TILE)
+        total_ref[:, cols] += product(act_v[0], wb_v[0, :, cols]) + product(act_v[1], wb_v[1, :, cols])
+    for copy in outs:
+        copy.wait()
+
+
+def middle_second(
+    seg_ref, pair_ref, bias_ref, gain_ref, shift_ref, low1_ref, total_hbm, wo2, wo3, wi2, wi3, wb2, wb3,
+    act_hbm, slope_hbm, xhat2_ref, rstd2_ref, out_ref, pooled_ref, len_ref, msg_ref,
+    wi_v, wb_v, act_v, slope_v, resid, sems, out_sems,
+):
+    length, width = resid.shape
+    local = wo2.shape[0] - 16
+    b_back, gain2, shift2 = row_of(bias_ref), row_of(gain_ref), row_of(shift_ref)
+    copies = start_all(
+        [(w, wi_v.at[r]) for r, w in enumerate((wi2, wi3))]
+        + [(total_hbm, resid)]
+        + [(w, wb_v.at[r]) for r, w in enumerate((wb2, wb3))],
+        sems,
+    )
+    outs = []
+    for r in range(2):
+        copies[r].wait()
+        b_in = jnp.sum((wo2, wo3)[r][local : local + 16, :].astype(f32), axis=0, keepdims=True)
+        feed(r, low1_ref, wi_v, b_in, act_v, slope_v)
+        outs += start_all(
+            [(act_v.at[r], act_hbm.at[r]), (slope_v.at[r], slope_hbm.at[r])],
+            out_sems.at[pl.ds(2 * r, 2)],
+        )
+    for copy in copies[2:]:
+        copy.wait()
     for first in range(0, width, TILE):
         cols = slice(first, first + TILE)
         total = resid[:, cols] + b_back[:, cols]
-        for r in range(4):
-            total = total + product(act_v[r], wb_v[r, :, cols])
-        resid[:, cols] = total
+        resid[:, cols] = total + product(act_v[0], wb_v[0, :, cols]) + product(act_v[1], wb_v[1, :, cols])
 
     @pl.loop(0, length // ROW_TILE)
     def _(i):
@@ -285,7 +362,7 @@
         xhat = center * rate
         xhat2_ref[rows, :] = xhat
         rstd2_ref[rows, :] = jnp.broadcast_to(rate, (ROW_TILE, LANES))
-        out_ref[rows, :] = (xhat * gain2[...] + shift2[...]).astype(bf16)
+        out_ref[rows, :] = (xhat * gain2 + shift2).astype(bf16)
 
     own = members(seg_ref)
     sums = product(own.astype(bf16), out_ref[...])
@@ -367,12 +444,13 @@
 
 
 def back_second(
-    gp_ref, seg_ref, xhat_ref, rstd_ref, gain_ref, act_hbm,
-    low_ref, grad_ref, vec_ref, d0, d1, d2, d3,
+    gp_ref, seg_ref, xhat_ref, rstd_ref, gain_ref, act01_hbm, act23_hbm,
+    low_ref, grad_ref, vec_ref, d_ref,
     out_v, act_v, sums, sems,
 ):
     length, width = xhat_ref.shape
-    copies = start_all([(act_hbm.at[r], act_v.at[r]) for r in range(4)], sems)
+    gain = row_of(gain_ref)
+    copies = start_all([(act23_hbm.at[1], act_v.at[0]), (act01_hbm.at[1], act_v.at[1])], sems)
     own = members(seg_ref).astype(bf16)
     top = gp_ref[...].astype(bf16)
     rest = (gp_ref[...] - top.astype(f32)).astype(bf16)
@@ -385,7 +463,7 @@
         grad_out, xhat = out_v[rows, :], xhat_ref[rows, :]
         sums[0] += column_total(grad_out * xhat)
         sums[1] += column_total(grad_out)
-        grad = grad_out * gain_ref[...]
+        grad = grad_out * gain
         first = jnp.mean(grad, axis=-1, keepdims=True)
         second = jnp.mean(grad * xhat, axis=-1, keepdims=True)
         grad = (grad - first - xhat * second) * rstd_ref[rows, 0:1]
@@ -396,23 +474,33 @@
     vec_ref[...] = jnp.zeros_like(vec_ref)
     for i in range(3):
         vec_ref[i : i + 1, :] = jnp.sum(sums[i], axis=0, keepdims=True)
-    for r, d_ref in ((3, d3), (2, d2), (1, d1), (0, d0)):
-        copies[r].wait()
-        for first in range(0, width, TILE):
+    back_products(copies, act_v, low_ref, d_ref)
+
+
+def back_products(copies, act_v, low_ref, d_ref):
+    for i, copy in enumerate(copies):
+        copy.wait()
+        for first in range(0, act_v.shape[2], TILE):
             cols = slice(first, first + TILE)
-            d_ref[cols, :] = product_t(act_v[r, :, cols], low_ref[...]).astype(bf16)
+            d_ref[i, cols, :] = product_t(act_v[i, :, cols], low_ref[...]).astype(bf16)
+
+
+def back_outer(low_ref, act01_hbm, act23_hbm, d_ref, act_v, sems):
+    copies = start_all([(act23_hbm.at[0], act_v.at[0]), (act01_hbm.at[0], act_v.at[1])], sems)
+    back_products(copies, act_v, low_ref, d_ref)
 
 
 def back_first(
-    low_ref, resid_ref, xhat_ref, rstd_ref, gain_ref, slope_hbm,
+    low_ref, resid_ref, xhat_ref, rstd_ref, gain_ref, slope01_hbm, slope23_hbm,
     wo0, wo1, wo2, wo3, wi0, wi1, wi2, wi3, wb0, wb1, wb2, wb3,
     gb_hbm, grad_ref, attn_ref, vec_ref, bin_ref, x0, x1, x2, x3,
     slope_v, wo_v, wi_v, wb_v, gb_v, total_v, sums, sems, out_sems,
 ):
     length, width = xhat_ref.shape
     units = wi_v.shape[2]
+    gain = row_of(gain_ref)
     copies = start_all(
-        [p for r, w in enumerate((wb0, wb1, wb2, wb3)) for p in ((w, wb_v.at[r]), (slope_hbm.at[r], slope_v.at[r]))]
+        [p for r, w in enumerate((wb0, wb1, wb2, wb3)) for p in ((w, wb_v.at[r]), ((slope01_hbm, slope23_hbm)[r // 2].at[r % 2], slope_v.at[r]))]
         + [(w, wi_v.at[r]) for r, w in enumerate((wi0, wi1, wi2, wi3))]
         + [(w, wo_v.at[r]) for r, w in enumerate((wo0, wo1, wo2, wo3))],
         sems,
@@ -444,7 +532,7 @@
         grad_out, xhat = total_v[rows, :], xhat_ref[rows, :]
         sums[0] += column_total(grad_out * xhat)
         sums[1] += column_total(grad_out)
-        grad = grad_out * gain_ref[...]
+        grad = grad_out * gain
         first = jnp.mean(grad, axis=-1, keepdims=True)
         second = jnp.mean(grad * xhat, axis=-1, keepdims=True)
         grad = (grad - first - xhat * second) * rstd_ref[rows, 0:1]
@@ -456,26 +544,26 @@
     for i in range(3):
         vec_ref[i : i + 1, :] = jnp.sum(sums[i], axis=0, keepdims=True)
     for r, x_ref in enumerate((x0, x1, x2, x3)):
-        x_ref[...] = product_nt(attn_ref[...], wo_v[r]).astype(bf16)
+        x_ref[...] = product_nt(attn_ref[...], wo_v[r, 0 : x_ref.shape[1], :]).astype(bf16)
     for copy in outs:
         copy.wait()
 
 
 def weight_grads(
-    low1_ref, attn_ref, vec1_ref, vec2_ref, bin_ref, c0, c1, c2, c3, gb_hbm,
-    d0, d1, d2, d3,
+    pieces, low1_ref, attn_ref, vec1_ref, vec2_ref, bin_ref, ca, cb, gb_hbm,
+    d_ref,
     gb_v, sems,
 ):
     length, width = low1_ref.shape
     units = gb_v.shape[2]
-    local = c0.shape[1]
-    copies = start_all([(gb_hbm.at[r], gb_v.at[r]) for r in range(4)], sems)
-    for r, d_ref, c_ref in ((3, d3, c3), (2, d2, c2), (1, d1, c1), (0, d0, c0)):
-        copies[r].wait()
+    local = ca.shape[1]
+    copies = start_all([(gb_hbm.at[r], gb_v.at[i]) for i, r in enumerate(pieces)], sems)
+    for i, (r, c_ref) in enumerate(zip(pieces, (ca, cb))):
+        copies[i].wait()
         for first in range(0, width, TILE):
             cols = slice(first, first + TILE)
-            d_ref[cols, :] = product_t(low1_ref[:, cols], gb_v[r]).astype(bf16)
-        d_ref[width : width + local, :] = product_t(c_ref[...], attn_ref[...]).astype(bf16)
+            d_ref[i, cols, :] = product_t(low1_ref[:, cols], gb_v[i]).astype(bf16)
+        d_ref[i, width : width + local, :] = product_t(c_ref[...], attn_ref[...]).astype(bf16)
         rows = jnp.concatenate(
             [vec1_ref[0:3, :], vec2_ref[0:3, :], bin_ref[r : r + 1, :], jnp.zeros((1, units), f32)],
             axis=0,
@@ -483,12 +571,8 @@
         top = rows.astype(bf16)
         rest = (rows - top.astype(f32)).astype(bf16)
         at = width + local
-        d_ref[at : at + 16, :] = jnp.concatenate([top, rest], axis=0)
-        d_ref[at + 16 : at + VEC_ROWS, :] = jnp.zeros((VEC_ROWS - 16, units), bf16)
-
-
-def whole(array, memory=pltpu.VMEM):
-    return pl.BlockSpec(memory_space=memory)
+        d_ref[i, at : at + 16, :] = jnp.concatenate([top, rest], axis=0)
+        d_ref[i, at + 16 : at + VEC_ROWS, :] = jnp.zeros((VEC_ROWS - 16, units), bf16)
 
 
 def hop(array, axis, flip):
@@ -514,33 +598,87 @@
     return flips
 
 
-def gather_parts(mine):
+def together(*arrays):
+    return lax.optimization_barrier(arrays)
+
+
+def late(array, *earlier):
+    return lax.optimization_barrier((array, *earlier))[0]
+
+
+def gather_parts(mine, first=None):
     near = hop(mine, "mp", 1)
-    far = hop(mine, "mp", 2)
+    far = hop(mine, "mp", 2) if first is None else first
     return [mine, near, far, hop(far, "mp", 1)]
+
+
+def join(part, flip):
+    return ordered(bit_of("dp", flip), part, hop(part, "dp", flip), 0)
 
 
 def add_low(left_side, right_side):
     return (left_side.astype(f32) + right_side.astype(f32)).astype(bf16)
 
 
-def scatter_parts(parts):
-    far = add_low(parts[2], hop(parts[3], "mp", 1))
-    near = add_low(parts[0], hop(parts[1], "mp", 1))
-    return add_low(near, hop(far, "mp", 2))
-
-
-def sum_over_rows(array):
-    flips = bits_below(lax.axis_size("dp"))
-    for flip in flips:
-        half = array.shape[0] // 2
-        bit = bit_of("dp", flip)
-        send = lax.dynamic_slice_in_dim(array, (1 - bit) * half, half)
-        keep = lax.dynamic_slice_in_dim(array, bit * half, half)
-        array = add_low(keep, hop(send, "dp", flip))
-    for flip in reversed(flips):
-        array = ordered(bit_of("dp", flip), array, hop(array, "dp", flip), 0)
-    return array
+class Rows:
+    def __init__(self):
+        self.dp, self.mp = lax.axis_size("dp"), lax.axis_size("mp")
+        flips = bits_below(self.dp)
+        self.orders = flips, flips[1:2] + flips[:1] + flips[2:]
+        self.steps = len(flips)
+
+    def swap(self, values, step):
+        pairs = [
+            (i, ((i // self.mp) ^ self.orders[i % self.mp % 2][step]) * self.mp + i % self.mp)
+            for i in range(self.dp * self.mp)
+        ]
+        return lax.ppermute(values, ("dp", "mp"), pairs)
+
+    def bit(self, step):
+        even, odd = (bit_of("dp", order[step]) for order in self.orders)
+        return jnp.where(lax.axis_index("mp") % 2 == 1, odd, even)
+
+    def send(self, array, step):
+        half = array.shape[-2] // 2
+        away = lax.dynamic_slice_in_dim(array, (1 - self.bit(step)) * half, half, axis=-2)
+        return self.swap(away, step)
+
+    def keep(self, array, got, step):
+        half = array.shape[-2] // 2
+        return add_low(lax.dynamic_slice_in_dim(array, self.bit(step) * half, half, axis=-2), got)
+
+    def join(self, array, got, step):
+        return ordered(self.bit(step), array, got, array.ndim - 2)
+
+    def gather(self, array, last):
+        for step in reversed(range(last)):
+            array = self.join(array, self.swap(array, step), step)
+        return array
+
+    def total(self, array):
+        last = self.steps - 1
+        for step in range(last):
+            array = self.keep(array, self.send(array, step), step)
+        array = add_low(array, self.swap(array, last))
+        return self.gather(array, last)
+
+
+class Running:
+    def __init__(self, rows, array, plan):
+        self.rows, self.array, self.plan = rows, array, plan
+
+    def start(self):
+        kind, step = self.plan[0]
+        return self.rows.send(self.array, step) if kind == "send" else self.rows.swap(self.array, step)
+
+    def finish(self, got):
+        kind, step = self.plan.pop(0)
+        if kind == "send":
+            self.array = self.rows.keep(self.array, got, step)
+        elif kind == "full":
+            self.array = add_low(self.array, got)
+        else:
+            self.array = self.rows.join(self.array, got, step)
 
 
 def params(cost=None, **more):
@@ -575,72 +713,122 @@
     smem_spec = pl.BlockSpec(memory_space=pltpu.SMEM)
     dma = pltpu.SemaphoreType.DMA
 
-    out_parts = gather_parts(w_out)
-    in_parts = gather_parts(w_in)
-    back_parts = gather_parts(w_back)
-    bias_parts = jnp.concatenate(gather_parts(b_in[None, :]), axis=0)
+    tall = lambda vector: vector.reshape(-1, LANES)
+    bit_x, bit_z = bit_of("dp", 1), bit_of("dp", 2)
+    bits = jnp.stack([2 * bit_x + bit_z, 2 * bit_z + bit_x]).astype(jnp.int32)
+    out_pack, in_quarter, back_quarter = pl.pallas_call(
+        prepare,
+        in_specs=[smem_spec] + [vmem_spec] * 2 + [any_spec] * 2,
+        out_specs=[vmem_spec] * 3,
+        out_shape=[
+            shape((local + 16, width)), shape((width // 4, units)), shape((units // 4, width)),
+        ],
+        scratch_shapes=[dma((2,))],
+        name="prepare",
+        **params(cost(1e6, 2e6)),
+    )(bits, tall(b_in), w_out, w_in, w_back)
+    near_in, near_back = hop(w_in, "mp", 1), hop(w_back, "mp", 1)
+    near_out = hop(out_pack, "mp", 1)
+    far_out = hop(out_pack, "mp", 2)
+    b_qv, near_in, near_back, near_out = together(b_qv, near_in, near_back, near_out)
+    in_quarter = hop(in_quarter, "mp", 2)
+    back_quarter = hop(back_quarter, "mp", 2)
+    w_t = jnp.swapaxes(w_qkv, 1, 2)
 
     windows = jnp.stack(
         [segment_ids[:, window_start(i, length) :][:, :K_WINDOW] for i in range(blocks)], axis=1
     )
     seg_rows = segment_ids[:, None, :]
-    pick = lambda r, m: (r ^ m[0], 0, 0)
-    qkv, probs, ctx = pl.pallas_call(
-        attend_forward,
-        grid_spec=pltpu.PrefetchScalarGridSpec(
-            num_scalar_prefetch=1,
-            grid=(row_count,),
-            in_specs=[
-                pl.BlockSpec((length, width), lambda r, m: (r ^ m[0], 0)),
-                pl.BlockSpec(w_qkv.shape, lambda r, m: (0, 0, 0)),
-                pl.BlockSpec(b_qv.shape, lambda r, m: (0, 0)),
-                pl.BlockSpec((1, 1, length), pick),
-                pl.BlockSpec((1, blocks, K_WINDOW), pick),
+
+    def attend(count, source):
+        return pl.pallas_call(
+            attend_forward,
+            grid_spec=pltpu.PrefetchScalarGridSpec(
+                num_scalar_prefetch=1,
+                grid=(count,),
+                in_specs=[
+                    pl.BlockSpec((length, width), lambda i, m: (source(i) ^ m[0], 0)),
+                    pl.BlockSpec(w_t.shape, lambda i, m: (0, 0, 0)),
+                    pl.BlockSpec(b_qv.shape, lambda i, m: (0, 0)),
+                    pl.BlockSpec((1, 1, length), lambda i, m: (source(i) ^ m[0], 0, 0)),
+                    pl.BlockSpec((1, blocks, K_WINDOW), lambda i, m: (source(i) ^ m[0], 0, 0)),
+                ],
+                out_specs=[
+                    pl.BlockSpec((1, 3, length, local), lambda i, m: (i, 0, 0, 0)),
+                    pl.BlockSpec((1, heads * blocks, Q_BLOCK, K_WINDOW), lambda i, m: (i, 0, 0, 0)),
+                ]
+                + [pl.BlockSpec((length, local), lambda i, m: (0, 0))] * count,
+                scratch_shapes=[pltpu.VMEM((length, local), bf16)],
+            ),
+            out_shape=[
+                shape((count, 3, length, local)),
+                shape((count, heads * blocks, Q_BLOCK, K_WINDOW)),
+                *[shape((length, local))] * count,
             ],
-            out_specs=[
-                pl.BlockSpec((1, 3, length, local), lambda r, m: (r, 0, 0, 0)),
-                pl.BlockSpec((1, heads * blocks, Q_BLOCK, K_WINDOW), lambda r, m: (r, 0, 0, 0)),
-                pl.BlockSpec((1, length, local), lambda r, m: (r, 0, 0)),
-            ],
-        ),
-        out_shape=[
-            shape((row_count, 3, length, local)),
-            shape((row_count, heads * blocks, Q_BLOCK, K_WINDOW)),
-            shape((row_count, length, local)),
-        ],
-        name="attend_forward",
-        **params(cost(6 * row_count * length * width * local, 8e6, row_count * heads * length * K_WINDOW)),
-    )(m_arr, tokens, w_qkv, b_qv, seg_rows, windows)
-
-    ctx_parts = [ctx[0]] + [hop(ctx[r], "mp", r) for r in range(1, 4)]
+            name="attend_forward",
+            **params(cost(6 * count * length * width * local, 2e6 * count, count * heads * length * K_WINDOW)),
+        )(m_arr, tokens, w_t, b_qv, seg_rows, windows)
+
+    qkv_away, probs_away, ctx3, ctx2, ctx1 = attend(3, lambda i: 3 - i)
+    ctx3, ctx2, ctx1, in_quarter, back_quarter, far_out = together(
+        ctx3, ctx2, ctx1, in_quarter, back_quarter, far_out
+    )
+    in_got, back_got = hop(in_quarter, "dp", 2), hop(back_quarter, "dp", 1)
+    qkv_own, probs_own, ctx0 = attend(1, lambda i: 0)
+    out_parts = [out_pack, near_out, far_out, hop(late(far_out, ctx0), "mp", 1)]
+    in_half = ordered(bit_z, in_quarter, late(in_got, ctx0), 0)
+    back_half = ordered(bit_x, back_quarter, late(back_got, ctx0), 0)
+    ctx_parts = [ctx0, hop(ctx1, "mp", 1), hop(ctx2, "mp", 2), hop(ctx3, "mp", 3)]
     seg_own = lax.dynamic_slice_in_dim(segment_ids, member, 1)
     pair_own = lax.dynamic_slice_in_dim(pair_ids, member, 1).reshape(-1, 1)
     pair_code = jnp.concatenate(
         [pair_own // 64, pair_own % 64, jnp.zeros((pair_own.shape[0], LANES - 2), jnp.int32)], axis=1
     ).astype(f32)
-    row = lambda vector: vector[None, :]
-    act, slope, xhat1, rstd1, low1, xhat2, rstd2, out_own, pooled, lengths, msg = pl.pallas_call(
-        middle_forward,
-        in_specs=[smem_spec, any_spec] + [vmem_spec] * 9 + [any_spec] * 16,
-        out_specs=[any_spec] * 2 + [vmem_spec] * 9,
+    in_got, back_got = hop(in_half, "dp", 1), hop(back_half, "dp", 2)
+    act01, slope01, xhat1, rstd1, low1, total = pl.pallas_call(
+        middle_first,
+        in_specs=[smem_spec, any_spec] + [vmem_spec] * 3 + [any_spec] * 12,
+        out_specs=[any_spec] * 2 + [vmem_spec] * 4,
         out_shape=[
-            shape((4, length, units)), shape((4, length, units)),
+            shape((2, length, units)), shape((2, length, units)),
             shape((length, width), f32), shape((length, LANES), f32), shape((length, width)),
+            shape((length, width), f32),
+        ],
+        scratch_shapes=[
+            pltpu.VMEM((length, width), bf16), pltpu.VMEM((4, length, local), bf16),
+            pltpu.VMEM((4, local + 16, width), bf16), pltpu.VMEM((2, width, units), bf16),
+            pltpu.VMEM((2, units, width), bf16), pltpu.VMEM((2, length, units), bf16),
+            pltpu.VMEM((2, length, units), bf16), dma((13,)), dma((4,)),
+        ],
+        name="middle_first",
+        **params(cost(2 * length * width * (width + 4 * units), 18e6, 2 * length * units)),
+    )(
+        m_arr, tokens, tall(b_out), tall(norm1_gain), tall(norm1_shift), *ctx_parts, *out_parts,
+        w_in, near_in, w_back, near_back,
+    )
+    in_far = ordered(bit_x, in_half, late(in_got, total), 0)
+    back_far = ordered(bit_z, back_half, late(back_got, total), 0)
+    in_parts = [w_in, near_in, in_far, hop(in_far, "mp", 1)]
+    back_parts = [w_back, near_back, back_far, hop(back_far, "mp", 1)]
+    act23, slope23, xhat2, rstd2, out_own, pooled, lengths, msg = pl.pallas_call(
+        middle_second,
+        in_specs=[vmem_spec] * 6 + [any_spec] + [vmem_spec] * 2 + [any_spec] * 4,
+        out_specs=[any_spec] * 2 + [vmem_spec] * 6,
+        out_shape=[
+            shape((2, length, units)), shape((2, length, units)),
             shape((length, width), f32), shape((length, LANES), f32), shape((length, width)),
             shape((16, width), f32), shape((16, LANES), f32), shape((8, 2 * width + LANES)),
         ],
         scratch_shapes=[
-            pltpu.VMEM((length, width), bf16), pltpu.VMEM((4, length, local), bf16),
-            pltpu.VMEM((4, local, width), bf16), pltpu.VMEM((4, width, units), bf16),
-            pltpu.VMEM((4, units, width), bf16), pltpu.VMEM((4, length, units), bf16),
-            pltpu.VMEM((4, length, units), bf16), pltpu.VMEM((length, width), f32),
-            dma((17,)), dma((8,)),
+            pltpu.VMEM((2, width, units), bf16), pltpu.VMEM((2, units, width), bf16),
+            pltpu.VMEM((2, length, units), bf16), pltpu.VMEM((2, length, units), bf16),
+            pltpu.VMEM((length, width), f32), dma((5,)), dma((4,)),
         ],
-        name="middle_forward",
-        **params(cost(2 * length * width * (width + 8 * units), 25e6, 4 * length * units)),
+        name="middle_second",
+        **params(cost(8 * length * width * units, 12e6, 2 * length * units)),
     )(
-        m_arr, tokens, seg_own, pair_code, row(b_out), row(norm1_gain), row(norm1_shift), bias_parts,
-        row(b_back), row(norm2_gain), row(norm2_shift), *ctx_parts, *out_parts, *in_parts, *back_parts,
+        seg_own, pair_code, tall(b_back), tall(norm2_gain), tall(norm2_shift), low1, total,
+        *out_parts[2:], *in_parts[2:], *back_parts[2:],
     )
 
     everyone = msg[None]
@@ -660,32 +848,47 @@
         **params(cost(4e8, 2e6, 1e5)),
     )(own_row.astype(jnp.int32).reshape(1), everyone, msg, pooled, lengths)
 
-    grad_low2, grad_resid2, vec2, *d_back = pl.pallas_call(
+    rows = Rows()
+    grad_low2, grad_resid2, vec2, back_send = pl.pallas_call(
         back_second,
-        in_specs=[vmem_spec] * 5 + [any_spec],
-        out_specs=[vmem_spec] * 7,
+        in_specs=[vmem_spec] * 5 + [any_spec] * 2,
+        out_specs=[vmem_spec] * 4,
         out_shape=[
             shape((length, width)), shape((length, width), f32), shape((8, width), f32),
-            *[shape((units, width))] * 4,
+            shape((2, units, width)),
         ],
         scratch_shapes=[
-            pltpu.VMEM((length, width), f32), pltpu.VMEM((4, length, units), bf16),
-            pltpu.VMEM((3, 8, width), f32), dma((4,)),
+            pltpu.VMEM((length, width), f32), pltpu.VMEM((2, length, units), bf16),
+            pltpu.VMEM((3, 8, width), f32), dma((2,)),
         ],
         name="back_second",
-        **params(cost(8 * length * width * units, 14e6)),
-    )(grad_pooled, seg_own, xhat2, rstd2, row(norm2_gain), act)
+        **params(cost(4 * length * width * units, 14e6)),
+    )(grad_pooled, seg_own, xhat2, rstd2, tall(norm2_gain), act01, act23)
+    back_got = hop(back_send, "mp", 1)
+    back_keep = pl.pallas_call(
+        back_outer,
+        in_specs=[vmem_spec] + [any_spec] * 2,
+        out_specs=vmem_spec,
+        out_shape=shape((2, units, width)),
+        scratch_shapes=[pltpu.VMEM((2, length, units), bf16), dma((2,))],
+        name="back_outer",
+        **params(cost(4 * length * width * units, 8e6)),
+    )(grad_low2, act01, act23)
+    back_sum = add_low(back_keep, back_got)
+    grad_low2, back_sum = together(grad_low2, back_sum)
+    back_got = rows.send(back_sum, 0)
+    out_far = hop(late(out_own, grad_low2), "mp", 2)
 
     gb, grad_resid1, attn_low, vec1, d_bin, *ctx_grads = pl.pallas_call(
         back_first,
-        in_specs=[vmem_spec] * 5 + [any_spec] * 13,
+        in_specs=[vmem_spec] * 5 + [any_spec] * 14,
         out_specs=[any_spec] + [vmem_spec] * 8,
         out_shape=[
             shape((4, length, units)), shape((length, width), f32), shape((length, width)),
             shape((8, width), f32), shape((4, units), f32), *[shape((length, local))] * 4,
         ],
         scratch_shapes=[
-            pltpu.VMEM((4, length, units), bf16), pltpu.VMEM((4, local, width), bf16),
+            pltpu.VMEM((4, length, units), bf16), pltpu.VMEM((4, local + 16, width), bf16),
             pltpu.VMEM((4, width, units), bf16), pltpu.VMEM((4, units, width), bf16),
             pltpu.VMEM((4, length, units), bf16), pltpu.VMEM((length, width), f32),
             pltpu.VMEM((3, 8, width), f32), dma((16,)), dma((4,)),
@@ -693,55 +896,144 @@
         name="back_first",
         **params(cost(2 * length * width * (width + 8 * units), 25e6)),
     )(
-        grad_low2, grad_resid2, xhat1, rstd1, row(norm1_gain), slope, *out_parts, *in_parts, *back_parts,
-    )
-
-    grads_here = [ctx_grads[0]] + [hop(ctx_grads[r], "mp", r) for r in range(1, 4)]
-
-    d_first = pl.pallas_call(
-        weight_grads,
-        in_specs=[vmem_spec] * 9 + [any_spec],
-        out_specs=[vmem_spec] * 4,
-        out_shape=[shape((width + local + VEC_ROWS, units))] * 4,
-        scratch_shapes=[pltpu.VMEM((4, length, units), bf16), dma((4,))],
-        name="weight_grads",
-        **params(cost(8 * length * width * (units + local), 12e6)),
-    )(low1, attn_low, vec1, vec2, d_bin, *ctx_parts, gb)
-
-    same = lambda r, m: (0, 0)
-    d_qkv, *backs = pl.pallas_call(
-        attend_backward,
-        grid_spec=pltpu.PrefetchScalarGridSpec(
-            num_scalar_prefetch=1,
-            grid=(row_count,),
-            in_specs=[
-                pl.BlockSpec((length, width), lambda r, m: (r ^ m[0], 0)),
-                pl.BlockSpec(w_qkv.shape, lambda r, m: (0, 0, 0)),
-                pl.BlockSpec((1, 3, length, local), lambda r, m: (r, 0, 0, 0)),
-                pl.BlockSpec((1, heads * blocks, Q_BLOCK, K_WINDOW), lambda r, m: (r, 0, 0, 0)),
-            ]
-            + [pl.BlockSpec((length, local), same)] * 4,
-            out_specs=[pl.BlockSpec((3 * local + VEC_ROWS, width), same)]
-            + [pl.BlockSpec((length, width), same)] * 4,
-            scratch_shapes=[
-                pltpu.VMEM((length, local), bf16), pltpu.VMEM((length, local), f32),
-                pltpu.VMEM((length, local), f32), pltpu.VMEM((3 * local, width), f32),
-                pltpu.VMEM((8, local), f32),
-            ],
-        ),
-        out_shape=[shape((3 * local + VEC_ROWS, width))] + [shape((length, width))] * 4,
-        name="attend_backward",
-        **params(cost(12 * row_count * length * width * local, 16e6)),
-    )(m_arr, tokens, w_qkv, qkv, probs, *grads_here)
-
-    layer_out = rows_of_all(out_own, row_count)
-    near = add_low(backs[0].astype(f32) + grad_resid1, hop(backs[1], "mp", 1))
-    far = add_low(backs[2], hop(backs[3], "mp", 1))
-    d_tokens = rows_of_all(add_low(near, hop(far, "mp", 2)), row_count)
-
-    sum_back = sum_over_rows(scatter_parts(d_back))
-    sum_first = sum_over_rows(scatter_parts(d_first))
-    sum_qkv = sum_over_rows(d_qkv)
+        grad_low2, grad_resid2, xhat1, rstd1, tall(norm1_gain), slope01, slope23, *out_parts, *in_parts, *back_parts,
+    )
+
+    attn_low, back_got, out_far = together(attn_low, back_got, out_far)
+    out_pair = ordered(bit_of("mp", 2), out_own[None], out_far[None], 0)
+    back_sum = rows.keep(back_sum, back_got, 0)
+    got3 = hop(ctx_grads[3], "mp", 3)
+
+    def first_grads(pieces, low):
+        return pl.pallas_call(
+            functools.partial(weight_grads, pieces),
+            in_specs=[vmem_spec] * 7 + [any_spec],
+            out_specs=vmem_spec,
+            out_shape=shape((2, width + local + VEC_ROWS, units)),
+            scratch_shapes=[pltpu.VMEM((2, length, units), bf16), dma((2,))],
+            name="weight_grads",
+            **params(cost(4 * length * width * (units + local), 7e6)),
+        )(low1, low, vec1, vec2, d_bin, ctx_parts[pieces[0]], ctx_parts[pieces[1]], gb)
+
+    first_send = first_grads((3, 1), attn_low)
+    got3, attn_low, first_send, out_pair = together(got3, attn_low, first_send, out_pair)
+    out_other = hop(out_pair, "mp", 1)
+    first_got = hop(first_send, "mp", 1)
+    got2 = hop(late(ctx_grads[2], first_send), "mp", 2)
+    first_keep = first_grads((2, 0), attn_low)
+    first_sum = add_low(first_keep, first_got)
+    own_grad, first_sum, got2, back_sum, out_other = together(
+        ctx_grads[0], first_sum, got2, back_sum, out_other
+    )
+    first_far, first_near = first_sum[0], first_sum[1]
+    cut = first_far.shape[0] // 4
+    far0 = hop(first_far[:cut], "mp", 2)
+    back_got = rows.send(back_sum, 1)
+    got1 = hop(late(ctx_grads[1], own_grad), "mp", 1)
+
+    def attend_back(count, source, first, qkv, probs, grads, sums):
+        same = lambda i, m: (0, 0)
+        last = source(0) == 1
+        out_specs = [pl.BlockSpec((length, width), same)] * count
+        out_shape = [shape((length, width))] * count
+        if last:
+            out_specs.append(pl.BlockSpec((3 * local + VEC_ROWS, width), same))
+            out_shape.append(shape((3 * local + VEC_ROWS, width)))
+        else:
+            out_specs += [pl.BlockSpec((3 * local, width), same), pl.BlockSpec((8, local), same)]
+            out_shape += [shape((3 * local, width), f32), shape((8, local), f32)]
+        return pl.pallas_call(
+            functools.partial(attend_backward, count, len(sums) == 0, last),
+            grid_spec=pltpu.PrefetchScalarGridSpec(
+                num_scalar_prefetch=1,
+                grid=(count,),
+                in_specs=[
+                    pl.BlockSpec((length, width), lambda i, m: (source(i) ^ m[0], 0)),
+                    pl.BlockSpec(w_t.shape, lambda i, m: (0, 0, 0)),
+                    pl.BlockSpec((1, 3, length, local), lambda i, m: (first + i, 0, 0, 0)),
+                    pl.BlockSpec(
+                        (1, heads * blocks, Q_BLOCK, K_WINDOW), lambda i, m: (first + i, 0, 0, 0)
+                    ),
+                ]
+                + [pl.BlockSpec((length, local), same)] * count
+                + [pl.BlockSpec(part.shape, same) for part in sums],
+                out_specs=out_specs,
+                scratch_shapes=[
+                    pltpu.VMEM((length, local), bf16), pltpu.VMEM((length, local), f32),
+                    pltpu.VMEM((length, local), f32), pltpu.VMEM((3 * local, width), f32),
+                    pltpu.VMEM((8, local), f32),
+                ],
+            ),
+            out_shape=out_shape,
+            name="attend_backward",
+            **params(cost(12 * count * length * width * local, 4e6 * count)),
+        )(m_arr, tokens, w_t, qkv, probs, *grads, *sums)
+
+    back0, *sums = attend_back(1, lambda i: 0, 0, qkv_own, probs_own, [own_grad], [])
+    far0, back_got, got1, *sums = together(far0, back_got, got1, *sums)
+    far1 = hop(first_far[cut : 3 * cut], "mp", 2)
+    back_sum = rows.keep(back_sum, back_got, 1)
+    back_got = rows.send(back_sum, 2)
+    back3, back2, *sums = attend_back(2, lambda i: 3 - i, 0, qkv_away, probs_away, [got3, got2], sums)
+    far1, back_got, *sums = together(far1, back_got, *sums)
+    far2 = hop(first_far[3 * cut :], "mp", 2)
+    back_sum = rows.keep(back_sum, back_got, 2)
+    for step in range(3, rows.steps):
+        back_sum = rows.keep(back_sum, rows.send(back_sum, step), step)
+    back_got = hop(back_sum[0], "mp", 2)
+    far2, first_near, back3, *sums = together(far2, first_near, back3, *sums)
+    first_sum = add_low(first_near, jnp.concatenate([far0, far1, far2], axis=0))
+    first_got = rows.send(first_sum, 0)
+    tok_got3 = hop(back3, "mp", 1)
+    back1, d_qkv = attend_back(1, lambda i: 1, 2, qkv_away, probs_away, [got1], sums)
+    last = rows.steps - 1
+    d_qkv, tok_got3, back_got, first_got = together(d_qkv, tok_got3, back_got, first_got)
+    back_sum = add_low(back_sum[1], back_got)
+    first_sum = rows.keep(first_sum, first_got, 0)
+    tok_got1 = hop(back1, "mp", 1)
+    far = add_low(back2, tok_got3)
+    down = [("send", step) for step in range(last)] + [("full", last)]
+    up = [("join", step) for step in reversed(range(last))]
+    sums = [
+        Running(rows, first_sum, down[1:] + up),
+        Running(rows, d_qkv, down + up),
+        Running(rows, back_sum, [("join", last)] + up),
+    ]
+    sizes = [length // 48 * 16] * 2
+    sizes.append(length - sum(sizes))
+    mine, pieces, tok_totals, at, stage = None, None, [], 0, 0
+    while any(part.plan for part in sums):
+        parts = [part for part in sums if part.plan]
+        hops = [part.start() for part in parts]
+        if stage == 0:
+            hops.append(tok_got1)
+        elif stage <= len(sizes):
+            rows_now = slice(at, at + sizes[stage - 1])
+            at += sizes[stage - 1]
+            hops.append(hop(jnp.stack([mine[rows_now], far[rows_now]]), "mp", 2))
+        elif stage == len(sizes) + 1:
+            tok_pair = jnp.concatenate(tok_totals, axis=1)
+            hops.append(hop(tok_pair, "mp", 1))
+        hops = list(together(*hops))
+        for part in parts:
+            part.finish(hops.pop(0))
+        if stage == 0:
+            mine = add_low(back0.astype(f32) + grad_resid1, hops[0])
+        elif stage <= len(sizes):
+            got = hops[0]
+            tok_totals.append(
+                ordered(
+                    bit_of("mp", 2),
+                    add_low(mine[rows_now], got[1])[None],
+                    add_low(far[rows_now], got[0])[None],
+                    0,
+                )
+            )
+        elif stage == len(sizes) + 1:
+            d_tokens = rows_of_all(tok_pair, hops[0])
+        stage += 1
+    sum_first, sum_qkv, sum_back = (part.array for part in sums)
+    layer_out = rows_of_all(out_pair, out_other)
 
     at = width + local
     vectors = sum_first[at : at + 8].astype(f32) + sum_first[at + 8 : at + 16].astype(f32)
@@ -776,13 +1068,11 @@
     return joined.reshape(-1, *array.shape[1:])
 
 
-def rows_of_all(mine, row_count):
-    pair = ordered(bit_of("mp", 2), mine[None], hop(mine, "mp", 2)[None], 0)
-    other = hop(pair, "mp", 1)
+def rows_of_all(pair, other):
     low_first = jnp.stack([pair, other], axis=1)
     high_first = jnp.stack([other, pair], axis=1)
     joined = jnp.where(bit_of("mp", 1) == 0, low_first, high_first)
-    return joined.reshape(row_count * mine.shape[0], mine.shape[1])
+    return joined.reshape(-1, pair.shape[-1])
 
 
 def solution(mesh):

time: 417 us -> 325 us (0.78)
  waiting for transfers between devices: 212 us -> 88.3 us
  Pallas kernels: 97.7 us -> 121 us
  other arithmetic: 27.3 us -> 38.3 us
  local copies, waits for them, and re-layouts: 23.8 us -> 18.4 us
    ppermute x54 -> x38, waiting for transfers between devices: 212 us -> 50.3 us  [hop(): return lax.ppermute(array, axis, [(i, i ^ flip) for i in range(size)])]
    ppermute x0 -> x16, waiting for transfers between devices: none -> 38 us  [swap(): return lax.ppermute(values, ('dp', 'mp'), pairs)]
    pallas_call x6 -> x13, Pallas kernels: 94.8 us -> 118 us  [the longest x3 29 us: attend_back(): pl.pallas_call(functools.partial(attend_backward, count, len(sums) == 0,...]
    ppermute x0 -> x16, starting transfers between devices: none -> 19.9 us  [swap(): return lax.ppermute(values, ('dp', 'mp'), pairs)]
    ppermute x54 -> x38, starting transfers between devices: 50.2 us -> 31.1 us  [hop(): return lax.ppermute(array, axis, [(i, i ^ flip) for i in range(size)])]
  transfers between devices with their start and end apart: 54 -> 54, of which waited for: 32 -> 22; matrix products, arithmetic and copies ran while one was open for 10% -> 12% of each run, Pallas kernels for 6% -> 31%
where the time goes in v2:
time: 325 us; the launch traced here: 319 us
  Pallas kernels  121 us (37%)
  waiting for transfers between devices  88.3 us (27%)
  starting transfers between devices  50.9 us (16%)
  other arithmetic  38.3 us (12%)
  local copies, waits for them, and re-layouts  18.4 us (6%)
    ppermute x38, waiting for transfers between devices, hop(): return lax.ppermute(array, axis, [(i, i ^ flip) for i in range(size)])  50.3 us
    ppermute x16, waiting for transfers between devices, swap(): return lax.ppermute(values, ('dp', 'mp'), pairs)  38 us
    ppermute x38, starting transfers between devices, hop(): return lax.ppermute(array, axis, [(i, i ^ flip) for i in range(size)])  31.1 us
    pallas_call x3, Pallas kernels, attend_back(): pl.pallas_call(functools.partial(attend_backward, count, len(sums) == 0,...  29 us
    ppermute x16, starting transfers between devices, swap(): return lax.ppermute(values, ('dp', 'mp'), pairs)  19.9 us
    pallas_call x2, Pallas kernels, attend(): pl.pallas_call(attend_forward, grid_spec=pltpu.PrefetchScalarGridSpec(num...  19.2 us
    pallas_call x1, Pallas kernels, shards(): pl.pallas_call(back_first, in_specs=[vmem_spec] * 5 + [any_spec] * 14, ou...  16.5 us
    pallas_call x1, Pallas kernels, shards(): pl.pallas_call(middle_first, in_specs=[smem_spec, any_spec] + [vmem_spec]...  13.5 us
  transfers between devices with their start and end apart: 54, of which 22 were waited for; matrix products, arithmetic and copies ran while one was open for 12% of the time, Pallas kernels for 31%

profile of v2, /device:TPU:0, one launch (start us, length us, event | category | flops | bytes accessed | tf_op | source)
XLA Modules:
  0.0 318.8 jit_solution(7396147731771323632)
XLA Ops:
  1.9 3.0 prepare.1
  5.3 2.6 collective-permute-start.5
  8.0 1.9 collective-permute-start.4
  11.3 13.5 %attend_forward.3 = (bf16[3,3,512,192]{3,2,1,0:T(8,128)(2,1)}, bf16[3,12,128,256]{3,2,1,0:T(8,128)(2,1)}, bf16[512,192]{1,0:T(8,128)(2,1)}, bf16[512,192]{1,0:T(8,128)(2,1)}, bf16[512,192]{1,0:T(8,128)(2,1)}) custom-call(s32[1]{0:T(128)} %bitcast.5.m_ref, bf16[2048,768]{1,0:T(8,128)(2,1)} %tok_ref.9, bf16[3,192,768]{2,1,0:T(8,128)(2,1)} %bitcast.106, ...), custom_call_target="tpu_custom_call" | custom-call | flops 1358954496 | bytes 6000000 | tf_op jit(solution)/shard_map/attend_forward/pallas_call | solution.py:744
  24.8 4.1 %collective-permute-done.4 = bf16[192,768]{1,0:T(8,128)(2,1)S(1)} collective-permute-done((bf16[192,768]{1,0:T(8,128)(2,1)}, bf16[192,768]{1,0:T(8,128)(2,1)S(1)}, u32[]{:S(2)}, u32[]{:S(2)}) %collective-permute-start.4) | collective-permute-done | bytes 294944 | tf_op jit(solution)/shard_map/ppermute | solution.py:580
  28.9 1.8 collective-permute-start.10
  30.7 1.5 collective-permute-start.13
  32.2 5.7 %attend_forward.2 = (bf16[1,3,512,192]{3,2,1,0:T(8,128)(2,1)}, bf16[1,12,128,256]{3,2,1,0:T(8,128)(2,1)}, bf16[512,192]{1,0:T(8,128)(2,1)}) custom-call(s32[1]{0:T(128)} %bitcast.5.m_ref, bf16[2048,768]{1,0:T(8,128)(2,1)} %tok_ref.9, bf16[3,192,768]{2,1,0:T(8,128)(2,1)} %bitcast.107, f32[2,192]{1,0:T(2,128)} %b_ref.1, ...), custom_call_target="tpu_custom_call" | custom-call | flops 452984832 | bytes 2000000 | tf_op jit(solution)/shard_map/attend_forward/pallas_call | solution.py:744
  39.5 1.5 collective-permute-start.7
  41.2 1.6 collective-permute-start.14
  42.8 5.9 %collective-permute-done.7.c2.ca = bf16[512,192]{1,0:T(8,128)(2,1)S(1)} collective-permute-done((bf16[512,192]{1,0:T(8,128)(2,1)S(1)}, bf16[512,192]{1,0:T(8,128)(2,1)S(1)}, u32[]{:S(2)}, u32[]{:S(2)}) %collective-permute-start.7) | collective-permute-done | bytes 196640 | tf_op jit(solution)/shard_map/ppermute | solution.py:580
  48.7 3.1 collective-permute-done.8.c3.ca
  52.6 13.5 %middle_first.1 = (bf16[2,512,768]{2,1,0:T(8,128)(2,1)}, bf16[2,512,768]{2,1,0:T(8,128)(2,1)}, f32[512,768]{1,0:T(8,128)}, f32[512,128]{1,0:T(8,128)}, bf16[512,768]{1,0:T(8,128)(2,1)}, /*index=5*/f32[512,768]{1,0:T(8,128)}) custom-call(s32[1]{0:T(128)} %bitcast.5.m_ref, bf16[2048,768]{1,0:T(8,128)(2,1)} %tok_ref.9, f32[6,128]{1,0:T(8,128)} %bitcast.142, ...), custom_call_target="tpu_custom_call" | custom-call | flops 3019898880 | bytes 18000000 | tf_op jit(solution)/shard_map/middle_first/pallas_call | solution.py:788
  70.4 1.7 collective-permute-done.15.wb3
  72.1 12.0 %middle_second.1 = (bf16[2,512,768]{2,1,0:T(8,128)(2,1)}, bf16[2,512,768]{2,1,0:T(8,128)(2,1)}, f32[512,768]{1,0:T(8,128)}, f32[512,128]{1,0:T(8,128)}, bf16[512...) custom-call(s32[1,512]{1,0:T(1,128)} %constant_dynamic-slice_fusion.9.seg_ref, ...), custom_call_target="tpu_custom_call" | custom-call | flops 2415919104 | bytes 12000000 | tf_op jit(solution)/shard_map/middle_second/pallas_call | solution.py:813
  84.1 2.7 collective-permute-start.16
  86.8 2.7 collective-permute-done.16
  91.5 3.0 collective-permute-done.17
  94.5 1.4 collective-permute-start.18
  96.0 3.3 %collective-permute-done.18 = bf16[4,8,1664]{2,1,0:T(8,128)(2,1)S(1)} collective-permute-done((bf16[4,8,1664]{2,1,0:T(8,128)(2,1)S(1)}, bf16[4,8,1664]{2,1,0:T(8,128)(2,1)S(1)}, u32[]{:S(2)}, u32[]{:S(2)}) %collective-permute-start.18) | collective-permute-done | bytes 106528 | tf_op jit(solution)/shard_map/ppermute | solution.py:580
  99.3 1.6 collective-permute-start.19
  100.9 4.3 %collective-permute-done.19 = bf16[8,8,1664]{2,1,0:T(8,128)(2,1)S(1)} collective-permute-done((bf16[8,8,1664]{2,1,0:T(8,128)(2,1)S(1)}, bf16[8,8,1664]{2,1,0:T(8,128)(2,1)S(1)}, u32[]{:S(2)}, u32[]{:S(2)}) %collective-permute-start.19) | collective-permute-done | bytes 213024 | tf_op jit(solution)/shard_map/ppermute | solution.py:580
  105.5 1.7 collective-permute-done.20
  108.3 2.9 contrast.1
  111.3 6.8 %back_second.1 = (bf16[512,768]{1,0:T(8,128)(2,1)}, f32[512,768]{1,0:T(8,128)}, f32[8,768]{1,0:T(8,128)}, bf16[2,768,768]{2,1,0:T(8,128)(2,1)}) custom-call(f32[16,768]{1,0:T(8,128)} %get-tuple-element.159.gp_ref, s32[1,512]{1,0:T(1,128)} %constant_dynamic-slice_fusion.9.seg_ref, f32[512,768]{1,0:T(8,128)} %get-tuple-element.160.xhat_ref, ...), custom_call_target="tpu_custom_call" | custom-call | flops 1207959552 | bytes 14000000 | tf_op jit(solution)/shard_map/back_second/pallas_call | solution.py:852
  118.3 5.4 %back_outer.1 = bf16[2,768,768]{2,1,0:T(8,128)(2,1)} custom-call(bf16[512,768]{1,0:T(8,128)(2,1)} %get-tuple-element.166.low_ref, bf16[2,512,768]{2,1,0:T(8,128)(2,1)} %get-tuple-element.162.act01_hbm, bf16[2,512,768]{2,1,0:T(8,128)(2,1)} %get-tuple-element.163.act23_hbm), custom_call_target="tpu_custom_call" | custom-call | flops 1207959552 | bytes 8000000 | tf_op jit(solution)/shard_map/back_outer/pallas_call | solution.py:868
  123.7 2.9 add_convert_fusion.1
  126.8 1.4 collective-permute-start.23
  128.2 1.5 collective-permute-start.24
  129.7 16.5 %back_first.1 = (bf16[4,512,768]{2,1,0:T(8,128)(2,1)}, f32[512,768]{1,0:T(8,128)}, bf16[512,768]{1,0:T(8,128)(2,1)}, f32[8,768]{1,0:T(8,128)}, f32[4,768]{1,0:T(...) custom-call(bf16[512,768]{1,0:T(8,128)(2,1)} %get-tuple-element.166., ...), custom_call_target="tpu_custom_call" | custom-call | flops 5435817984 | bytes 25000000 | tf_op jit(solution)/shard_map/back_first/pallas_call | solution.py:882
  147.6 6.3 %weight_grads.2 = bf16[2,1024,768]{2,1,0:T(8,128)(2,1)} custom-call(bf16[512,768]{1,0:T(8,128)(2,1)} %get-tuple-element.147.low1_ref, bf16[512,768]{1,0:T(8,128)(2,1)} %get-tuple-element.185.attn_ref, f32[8,768]{1,0:T(8,128)} %get-tuple-element.178.vec1_ref, f32[8,768]{1,0:T(8,128)} %get-tuple-element.179.vec2_ref, f32[4,768]{1,0:T(4,128)} %get-tuple-element.180.bin_ref, ...), custom_call_target="tpu_custom_call" | custom-call | flops 1509949440 | bytes 7000000 | tf_op jit(solution)/shard_map/weight_grads/pallas_call | solution.py:908
  154.0 1.4 maximum_select_fusion.2
  155.9 1.5 collective-permute-start.26
  157.4 6.3 %weight_grads.3 = bf16[2,1024,768]{2,1,0:T(8,128)(2,1)} custom-call(bf16[512,768]{1,0:T(8,128)(2,1)} %get-tuple-element.147.low1_ref, bf16[512,768]{1,0:T(8,128)(2,1)} %get-tuple-element.185.attn_ref, f32[8,768]{1,0:T(8,128)} %get-tuple-element.178.vec1_ref, f32[8,768]{1,0:T(8,128)} %get-tuple-element.179.vec2_ref, f32[4,768]{1,0:T(4,128)} %get-tuple-element.180.bin_ref, ...), custom_call_target="tpu_custom_call" | custom-call | flops 1509949440 | bytes 7000000 | tf_op jit(solution)/shard_map/weight_grads/pallas_call | solution.py:908
  164.0 2.0 copy-done.2
  166.0 2.8 add_convert_fusion
  172.9 1.5 collective-permute-start.28
  175.0 7.6 %attend_backward.3 = (bf16[512,768]{1,0:T(8,128)(2,1)}, f32[576,768]{1,0:T(8,128)}, f32[8,192]{1,0:T(8,128)}) custom-call(s32[1]{0:T(128)} %bitcast.5.m_ref, bf16[2048,768]{1,0:T(8,128)(2,1)} %tok_ref.9, bf16[3,192,768]{2,1,0:T(8,128)(2,1)} %bitcast.108, bf16[1,3,512,192]{3,2,1,0:T(8,128)(2,1)} %get-tuple-element.191.qkv_ref, ...), custom_call_target="tpu_custom_call" | custom-call | flops 905969664 | bytes 4000000 | tf_op jit(solution)/shard_map/attend_backward/pallas_call | solution.py:945
  185.6 2.3 collective-permute-start.33
  188.1 13.7 %attend_backward.4 = (bf16[512,768]{1,0:T(8,128)(2,1)}, bf16[512,768]{1,0:T(8,128)(2,1)}, f32[576,768]{1,0:T(8,128)}, f32[8,192]{1,0:T(8,128)}) custom-call(s32[1]{0:T(128)} %bitcast.5.m_ref, bf16[2048,768]{1,0:T(8,128)(2,1)} %tok_ref.9, bf16[3,192,768]{2,1,0:T(8,128)(2,1)} %bitcast.109, bf16[3,3,512,192]{3,2,1,0:T(8,128)(2,1)} %get-tuple-element.197.qkv_ref, ...), custom_call_target="tpu_custom_call" | custom-call | flops 1811939328 | bytes 8000000 | tf_op jit(solution)/shard_map/attend_backward/pallas_call | solution.py:945
  201.7 6.3 %collective-permute-done.32 = bf16[512,768]{1,0:T(8,128)(2,1)S(1)} collective-permute-done((bf16[512,768]{1,0:T(8,128)(2,1)S(1)}, bf16[512,768]{1,0:T(8,128)(2,1)S(1)}, u32[]{:S(2)}, u32[]{:S(2)}) %collective-permute-start.32) | collective-permute-done | bytes 786464 | tf_op jit(solution)/shard_map/ppermute | solution.py:580
  211.9 7.8 %attend_backward.5 = (bf16[512,768]{1,0:T(8,128)(2,1)}, bf16[640,768]{1,0:T(8,128)(2,1)}) custom-call(s32[1]{0:T(128)} %bitcast.5.m_ref, bf16[2048,768]{1,0:T(8,128)(2,1)} %tok_ref.9, bf16[3,192,768]{2,1,0:T(8,128)(2,1)} %bitcast.110, bf16[3,3,512,192]{3,2,1,0:T(8,128)(2,1)} %get-tuple-element.197.qkv_ref, ...), custom_call_target="tpu_custom_call" | custom-call | flops 905969664 | bytes 4000000 | tf_op jit(solution)/shard_map/attend_backward/pallas_call | solution.py:945
  219.7 2.2 collective-permute-done.36
  223.8 2.4 collective-permute-start.39
  227.6 8.0 %collective-permute-done.39 = bf16[96,768]{1,0:T(8,128)(2,1)S(1)} collective-permute-done((bf16[96,768]{1,0:T(8,128)(2,1)S(1)}, bf16[96,768]{1,0:T(8,128)(2,1)S(1)}, u32[]{:S(2)}, u32[]{:S(2)}) %collective-permute-start.39) | collective-permute-done | bytes 147488 | tf_op jit(solution)/shard_map/ppermute | solution.py:635
  235.6 1.7 collective-permute-done.37
  237.4 1.8 collective-permute-start.41
  239.2 1.6 collective-permute-start.43
  245.3 1.5 collective-permute-start.48
  246.8 7.3 %collective-permute-done.42 = bf16[160,768]{1,0:T(8,128)(2,1)} collective-permute-done((bf16[160,768]{1,0:T(8,128)(2,1)}, bf16[160,768]{1,0:T(8,128)(2,1)}, u32[]{:S(2)}, u32[]{:S(2)}) %collective-permute-start.42) | collective-permute-done | bytes 245792 | tf_op jit(solution)/shard_map/ppermute | solution.py:635
  254.0 4.3 %collective-permute-done.41 = bf16[256,768]{1,0:T(8,128)(2,1)} collective-permute-done((bf16[256,768]{1,0:T(8,128)(2,1)S(1)}, bf16[256,768]{1,0:T(8,128)(2,1)}, u32[]{:S(2)}, u32[]{:S(2)}) %collective-permute-start.41) | collective-permute-done | bytes 393248 | tf_op jit(solution)/shard_map/ppermute | solution.py:635
  262.7 3.2 %collective-permute-start.46 = (bf16[160,768]{1,0:T(8,128)(2,1)S(1)}, bf16[160,768]{1,0:T(8,128)(2,1)S(1)}, u32[]{:S(2)}, u32[]{:S(2)}) collective-permute-start(bf16[160,768]{1,0:T(8,128)(2,1)S(1)} %add_convert_fusion.13), channel_id=1, source_target_pairs={{0,16},{1,17},{2,18},{3,19},{4,20},{5,21},{6,22},{7,23},{8,24},{9,... | collective-permute-start | bytes 737288 | tf_op jit(solution)/shard_map/ppermute | solution.py:635
  267.0 8.4 %collective-permute-done.46 = bf16[160,768]{1,0:T(8,128)(2,1)S(1)} collective-permute-done((bf16[160,768]{1,0:T(8,128)(2,1)S(1)}, bf16[160,768]{1,0:T(8,128)(2,1)S(1)}, u32[]{:S(2)}, u32[]{:S(2)}) %collective-permute-start.46) | collective-permute-done | bytes 245792 | tf_op jit(solution)/shard_map/ppermute | solution.py:635
  275.5 2.3 collective-permute-done.45
  277.8 1.3 maximum_select_fusion.9
  282.6 1.5 fusion.11
  284.3 11.3 %collective-permute-done.51 = bf16[2,192,768]{2,1,0:T(8,128)(2,1)S(1)} collective-permute-done((bf16[2,192,768]{2,1,0:T(8,128)(2,1)S(1)}, bf16[2,192,768]{2,1,0:T(8,128)(2,1)S(1)}, u32[]{:S(2)}, u32[]{:S(2)}) %collective-permute-start.51) | collective-permute-done | bytes 589856 | tf_op jit(solution)/shard_map/ppermute | solution.py:580
  296.1 3.6 %maximum_select_fusion = bf16[2,2,512,768]{3,2,0,1:T(8,128)(2,1)S(1)} fusion(bf16[2,1,512,768]{3,2,0,1:T(8,128)(2,1)} %bitcast.31, bf16[2,1,512,768]{3,2,0,1:T(8,128)(2,1)} %bitcast.30, pred[]{:T(512)S(6)} %eq.138), kind=kLoop, calls=%fused_computation.2 | loop fusion | flops 4718592 | bytes 6291457 | tf_op jit(solution)/shard_map/jit(_where)/select_n | solution.py:1074
  299.8 1.9 copy.63
  301.6 2.9 fusion
  308.0 1.6 slice_convert_fusion
  309.6 3.9 %collective-permute-done.52 = bf16[320,768]{1,0:T(8,128)(2,1)S(1)} collective-permute-done((bf16[320,768]{1,0:T(8,128)(2,1)S(1)}, bf16[320,768]{1,0:T(8,128)(2,1)S(1)}, u32[]{:S(2)}, u32[]{:S(2)}) %collective-permute-start.52) | collective-permute-done | bytes 491552 | tf_op jit(solution)/shard_map/ppermute | solution.py:635
  315.1 1.9 copy.64
  316.9 1.3 convert_bitcast_fusion
  (201 shorter events, 50.0 us)
Async XLA Ops:
  0.6 67.7 %copy-start = (s32[4,8]{1,0:T(4,128)S(1)}, s32[4,8]{1,0:T(4,128)}, u32[]{:S(2)}) copy-start(s32[4,8]{1,0:T(4,128)} %param.29) | copy-start | bytes 388
  0.7 9.3 %copy-start.22 = (s32[4,512]{1,0:T(4,128)S(1)}, s32[4,512]{1,0:T(4,128)}, u32[]{:S(2)}) copy-start(s32[4,512]{1,0:T(4,128)} %param.28) | copy-start | bytes 24580
  0.7 10.6 %collective-permute-start = (bf16[768,768]{1,0:T(8,128)(2,1)}, bf16[768,768]{1,0:T(8,128)(2,1)S(1)}, u32[]{:S(2)}, u32[]{:S(2)}) collective-permute-start(bf16[768,768]{1,0:T(8,128)(2,1)} %wi0.3), channel_id=1, source_target_pairs={{0,1},{1,0},{2,3},{3,2},{4,5},{5,4},{6,7},{7,6},{8,9},{9,8},{10,11... | collective-permute-start | bytes 3538952 | tf_op jit(solution)/shard_map/ppermute | solution.py:580
  1.2 10.1 %collective-permute-start.1 = (bf16[768,768]{1,0:T(8,128)(2,1)}, bf16[768,768]{1,0:T(8,128)(2,1)}, u32[]{:S(2)}, u32[]{:S(2)}) collective-permute-start(bf16[768,768]{1,0:T(8,128)(2,1)} %wb0.3), channel_id=1, source_target_pairs={{0,1},{1,0},{2,3},{3,2},{4,5},{5,4},{6,7},{7,6},{8,9},{9,8},{10,11... | collective-permute-start | bytes 3538952 | tf_op jit(solution)/shard_map/ppermute | solution.py:580
  4.8 3.2 collective-permute-start.2
  5.3 23.6 %collective-permute-start.5 = (bf16[208,768]{1,0:T(8,128)(2,1)}, bf16[208,768]{1,0:T(8,128)(2,1)}, u32[]{:S(2)}, u32[]{:S(2)}) collective-permute-start(bf16[208,768]{1,0:T(8,128)(2,1)} %get-tuple-element.131.wo0), channel_id=1, source_target_pairs={{0,2},{1,3},{2,0},{3,1},{4,6},{5,7},{6,4},{7,5},{8,10},{9,11},{10,... | collective-permute-start | bytes 958472 | tf_op jit(solution)/shard_map/ppermute | solution.py:580
  7.9 16.9 %collective-permute-start.3 = (bf16[192,768]{1,0:T(8,128)(2,1)}, bf16[192,768]{1,0:T(8,128)(2,1)S(1)}, u32[]{:S(2)}, u32[]{:S(2)}) collective-permute-start(bf16[192,768]{1,0:T(8,128)(2,1)} %get-tuple-element.137), channel_id=1, source_target_pairs={{0,2},{1,3},{2,0},{3,1},{4,6},{5,7},{6,4},{7,5},{8,10},{9,11},{10,... | collective-permute-start | bytes 884744 | tf_op jit(solution)/shard_map/ppermute | solution.py:580
  8.0 16.8 %copy-start.24 = (bf16[208,768]{1,0:T(8,128)(2,1)}, bf16[208,768]{1,0:T(8,128)(2,1)S(1)}, u32[]{:S(2)}) copy-start(bf16[208,768]{1,0:T(8,128)(2,1)S(1)} %collective-permute-done.2.wo1) | copy-start | bytes 958468
  8.0 20.9 %collective-permute-start.4 = (bf16[192,768]{1,0:T(8,128)(2,1)}, bf16[192,768]{1,0:T(8,128)(2,1)S(1)}, u32[]{:S(2)}, u32[]{:S(2)}) collective-permute-start(bf16[192,768]{1,0:T(8,128)(2,1)} %get-tuple-element.138), channel_id=1, source_target_pairs={{0,2},{1,3},{2,0},{3,1},{4,6},{5,7},{6,4},{7,5},{8,10},{9,11},{10,... | collective-permute-start | bytes 884744 | tf_op jit(solution)/shard_map/ppermute | solution.py:580
  11.3 13.5 %copy-start.23 = (bf16[768,768]{1,0:T(8,128)(2,1)}, bf16[768,768]{1,0:T(8,128)(2,1)S(1)}, u32[]{:S(2)}) copy-start(bf16[768,768]{1,0:T(8,128)(2,1)S(1)} %collective-permute-done.wi1) | copy-start | bytes 3538948
  28.9 9.5 %collective-permute-start.10 = (bf16[192,768]{1,0:T(8,128)(2,1)S(1)}, bf16[192,768]{1,0:T(8,128)(2,1)S(1)}, u32[]{:S(2)}, u32[]{:S(2)}) collective-permute-start(bf16[192,768]{1,0:T(8,128)(2,1)S(1)} %collective-permute-done.3), channel_id=1, source_target_pairs={{0,8},{4,12},{8,0},{12,4},{16,24},{20,28},{24,16},{28,20},{1,9},{5... | collective-permute-start | bytes 884744 | tf_op jit(solution)/shard_map/ppermute | solution.py:580
  30.7 10.3 %collective-permute-start.13 = (bf16[192,768]{1,0:T(8,128)(2,1)S(1)}, bf16[192,768]{1,0:T(8,128)(2,1)S(1)}, u32[]{:S(2)}, u32[]{:S(2)}) collective-permute-start(bf16[192,768]{1,0:T(8,128)(2,1)S(1)} %collective-permute-done.4), channel_id=1, source_target_pairs={{0,4},{4,0},{8,12},{12,8},{16,20},{20,16},{24,28},{28,24},{1,5},{5... | collective-permute-start | bytes 884744 | tf_op jit(solution)/shard_map/ppermute | solution.py:580
  32.2 7.2 %copy-start.27 = (bf16[512,192]{1,0:T(8,128)(2,1)S(1)}, bf16[512,192]{1,0:T(8,128)(2,1)}, u32[]{:S(2)}) copy-start(bf16[512,192]{1,0:T(8,128)(2,1)} %get-tuple-element.140) | copy-start | bytes 589828
  32.2 8.8 %copy-start.26 = (bf16[512,192]{1,0:T(8,128)(2,1)S(1)}, bf16[512,192]{1,0:T(8,128)(2,1)}, u32[]{:S(2)}) copy-start(bf16[512,192]{1,0:T(8,128)(2,1)} %get-tuple-element.141) | copy-start | bytes 589828
  32.2 9.0 %collective-permute-start.6 = (bf16[512,192]{1,0:T(8,128)(2,1)}, bf16[512,192]{1,0:T(8,128)(2,1)S(1)}, u32[]{:S(2)}, u32[]{:S(2)}) collective-permute-start(bf16[512,192]{1,0:T(8,128)(2,1)} %get-tuple-element.139), channel_id=1, source_target_pairs={{0,1},{1,0},{2,3},{3,2},{4,5},{5,4},{6,7},{7,6},{8,9},{9,8},{10,11... | collective-permute-start | bytes 589832 | tf_op jit(solution)/shard_map/ppermute | solution.py:580
  37.9 13.9 %collective-permute-start.9 = (bf16[208,768]{1,0:T(8,128)(2,1)}, bf16[208,768]{1,0:T(8,128)(2,1)S(1)}, u32[]{:S(2)}, u32[]{:S(2)}) collective-permute-start(bf16[208,768]{1,0:T(8,128)(2,1)} %collective-permute-done.5.wo2), channel_id=1, source_target_pairs={{0,1},{1,0},{2,3},{3,2},{4,5},{5,4},{6,7},{7,6},{8,9},{9,8},{10,11... | collective-permute-start | bytes 958472 | tf_op jit(solution)/shard_map/ppermute | solution.py:580
  38.6 27.6 %collective-permute-start.11 = (bf16[384,768]{1,0:T(8,128)(2,1)S(1)}, bf16[384,768]{1,0:T(8,128)(2,1)S(1)}, u32[]{:S(2)}, u32[]{:S(2)}) collective-permute-start(bf16[384,768]{1,0:T(8,128)(2,1)S(1)} %maximum_select_fusion.10), channel_id=1, source_target_pairs={{0,4},{4,0},{8,12},{12,8},{16,20},{20,16},{24,28},{28,24},{1,5},{5... | collective-permute-start | bytes 1769480 | tf_op jit(solution)/shard_map/ppermute | solution.py:580
  39.5 9.2 %collective-permute-start.7 = (bf16[512,192]{1,0:T(8,128)(2,1)S(1)}, bf16[512,192]{1,0:T(8,128)(2,1)S(1)}, u32[]{:S(2)}, u32[]{:S(2)}) collective-permute-start(bf16[512,192]{1,0:T(8,128)(2,1)S(1)} %copy-done.27), channel_id=1, source_target_pairs={{0,2},{1,3},{2,0},{3,1},{4,6},{5,7},{6,4},{7,5},{8,10},{9,11},{10,... | collective-permute-start | bytes 589832 | tf_op jit(solution)/shard_map/ppermute | solution.py:580
  41.0 10.8 %collective-permute-start.8 = (bf16[512,192]{1,0:T(8,128)(2,1)S(1)}, bf16[512,192]{1,0:T(8,128)(2,1)S(1)}, u32[]{:S(2)}, u32[]{:S(2)}) collective-permute-start(bf16[512,192]{1,0:T(8,128)(2,1)S(1)} %copy-done.26), channel_id=1, source_target_pairs={{0,3},{1,2},{2,1},{3,0},{4,7},{5,6},{6,5},{7,4},{8,11},{9,10},{10,... | collective-permute-start | bytes 589832 | tf_op jit(solution)/shard_map/ppermute | solution.py:580
  41.2 10.6 %copy-start.18 = (bf16[512,192]{1,0:T(8,128)(2,1)}, bf16[512,192]{1,0:T(8,128)(2,1)S(1)}, u32[]{:S(2)}) copy-start(bf16[512,192]{1,0:T(8,128)(2,1)S(1)} %collective-permute-done.6.c1.cb) | copy-start | bytes 589828
  41.2 26.6 %collective-permute-start.14 = (bf16[384,768]{1,0:T(8,128)(2,1)S(1)}, bf16[384,768]{1,0:T(8,128)(2,1)S(1)}, u32[]{:S(2)}, u32[]{:S(2)}) collective-permute-start(bf16[384,768]{1,0:T(8,128)(2,1)S(1)} %maximum_select_fusion.11), channel_id=1, source_target_pairs={{0,8},{4,12},{8,0},{12,4},{16,24},{20,28},{24,16},{28,20},{1,9},{5... | collective-permute-start | bytes 1769480 | tf_op jit(solution)/shard_map/ppermute | solution.py:580
  66.6 3.7 %collective-permute-start.12 = (bf16[768,768]{1,0:T(8,128)(2,1)S(1)}, bf16[768,768]{1,0:T(8,128)(2,1)}, u32[]{:S(2)}, u32[]{:S(2)}) collective-permute-start(bf16[768,768]{1,0:T(8,128)(2,1)S(1)} %maximum_select_fusion.4.wi2), channel_id=1, source_target_pairs={{0,1},{1,0},{2,3},{3,2},{4,5},{5,4},{6,7},{7,6},{8,9},{9,8},{10,11... | collective-permute-start | bytes 3538952 | tf_op jit(solution)/shard_map/ppermute | solution.py:580
  68.3 3.8 %collective-permute-start.15 = (bf16[768,768]{1,0:T(8,128)(2,1)S(1)}, bf16[768,768]{1,0:T(8,128)(2,1)}, u32[]{:S(2)}, u32[]{:S(2)}) collective-permute-start(bf16[768,768]{1,0:T(8,128)(2,1)S(1)} %maximum_select_fusion.5.wb2), channel_id=1, source_target_pairs={{0,1},{1,0},{2,3},{3,2},{4,5},{5,4},{6,7},{7,6},{8,9},{9,8},{10,11... | collective-permute-start | bytes 3538952 | tf_op jit(solution)/shard_map/ppermute | solution.py:580
  84.1 5.3 %collective-permute-start.16 = (bf16[1,8,1664]{2,1,0:T(8,128)(2,1)}, bf16[1,8,1664]{2,1,0:T(8,128)(2,1)S(1)}, u32[]{:S(2)}, u32[]{:S(2)}) collective-permute-start(bf16[1,8,1664]{2,1,0:T(8,128)(2,1)} %bitcast.127), channel_id=1, source_target_pairs={{0,16},{4,20},{8,24},{12,28},{16,0},{20,4},{24,8},{28,12},{1,17},{... | collective-permute-start | bytes 79880 | tf_op jit(solution)/shard_map/ppermute | solution.py:580
  90.3 4.2 %collective-permute-start.17 = (bf16[2,8,1664]{2,1,0:T(8,128)(2,1)S(1)}, bf16[2,8,1664]{2,1,0:T(8,128)(2,1)S(1)}, u32[]{:S(2)}, u32[]{:S(2)}) collective-permute-start(bf16[2,8,1664]{2,1,0:T(8,128)(2,1)S(1)} %maximum_select_fusion.22), channel_id=1, source_target_pairs={{0,8},{4,12},{8,0},{12,4},{16,24},{20,28},{24,16},{28,20},{1,9},{5... | collective-permute-start | bytes 159752 | tf_op jit(solution)/shard_map/ppermute | solution.py:580
  94.5 4.8 %collective-permute-start.18 = (bf16[4,8,1664]{2,1,0:T(8,128)(2,1)S(1)}, bf16[4,8,1664]{2,1,0:T(8,128)(2,1)S(1)}, u32[]{:S(2)}, u32[]{:S(2)}) collective-permute-start(bf16[4,8,1664]{2,1,0:T(8,128)(2,1)S(1)} %bitcast.123), channel_id=1, source_target_pairs={{0,4},{4,0},{8,12},{12,8},{16,20},{20,16},{24,28},{28,24},{1,5},{5... | collective-permute-start | bytes 319496 | tf_op jit(solution)/shard_map/ppermute | solution.py:580
  99.3 5.9 %collective-permute-start.19 = (bf16[8,8,1664]{2,1,0:T(8,128)(2,1)S(1)}, bf16[8,8,1664]{2,1,0:T(8,128)(2,1)S(1)}, u32[]{:S(2)}, u32[]{:S(2)}) collective-permute-start(bf16[8,8,1664]{2,1,0:T(8,128)(2,1)S(1)} %bitcast.118), channel_id=1, source_target_pairs={{0,2},{1,3},{2,0},{3,1},{4,6},{5,7},{6,4},{7,5},{8,10},{9,11},{10,... | collective-permute-start | bytes 638984 | tf_op jit(solution)/shard_map/ppermute | solution.py:580
  105.4 1.8 collective-permute-start.20
  118.1 5.7 %collective-permute-start.21 = (bf16[2,768,768]{2,1,0:T(8,128)(2,1)}, bf16[2,768,768]{2,1,0:T(8,128)(2,1)}, u32[]{:S(2)}, u32[]{:S(2)}) collective-permute-start(bf16[2,768,768]{2,1,0:T(8,128)(2,1)} %get-tuple-element.165), channel_id=1, source_target_pairs={{0,1},{1,0},{2,3},{3,2},{4,5},{5,4},{6,7},{7,6},{8,9},{9,8},{10,11... | collective-permute-start | bytes 7077896 | tf_op jit(solution)/shard_map/ppermute | solution.py:580
  126.8 20.8 %collective-permute-start.23 = (bf16[2,384,768]{2,1,0:T(8,128)(2,1)S(1)}, bf16[2,384,768]{2,1,0:T(8,128)(2,1)S(1)}, u32[]{:S(2)}, u32[]{:S(2)}) collective-permute-start(bf16[2,384,768]{2,1,0:T(8,128)(2,1)S(1)} %constant_dynamic-slice_fusion.7), channel_id=1, source_target_pairs={{0,4},{1,9},{2,6},{3,11},{4,0},{5,13},{6,2},{7,15},{8,12},{9,1},{1... | collective-permute-start | bytes 3538952 | tf_op jit(solution)/shard_map/ppermute | solution.py:635
  128.2 19.4 %collective-permute-start.24 = (bf16[512,768]{1,0:T(8,128)(2,1)S(1)}, bf16[512,768]{1,0:T(8,128)(2,1)S(1)}, u32[]{:S(2)}, u32[]{:S(2)}) collective-permute-start(bf16[512,768]{1,0:T(8,128)(2,1)S(1)} %copy-done.13), channel_id=1, source_target_pairs={{0,2},{1,3},{2,0},{3,1},{4,6},{5,7},{6,4},{7,5},{8,10},{9,11},{10,... | collective-permute-start | bytes 2359304 | tf_op jit(solution)/shard_map/ppermute | solution.py:580
  146.2 9.1 %collective-permute-start.22 = (bf16[512,192]{1,0:T(8,128)(2,1)}, bf16[512,192]{1,0:T(8,128)(2,1)}, u32[]{:S(2)}, u32[]{:S(2)}) collective-permute-start(bf16[512,192]{1,0:T(8,128)(2,1)} %get-tuple-element.172), channel_id=1, source_target_pairs={{0,3},{1,2},{2,1},{3,0},{4,7},{5,6},{6,5},{7,4},{8,11},{9,10},{10,... | collective-permute-start | bytes 589832 | tf_op jit(solution)/shard_map/ppermute | solution.py:580
  155.4 8.7 %collective-permute-start.25 = (bf16[2,1024,768]{2,1,0:T(8,128)(2,1)}, bf16[2,1024,768]{2,1,0:T(8,128)(2,1)}, u32[]{:S(2)}, u32[]{:S(2)}) collective-permute-start(bf16[2,1024,768]{2,1,0:T(8,128)(2,1)} %weight_grads.2), channel_id=1, source_target_pairs={{0,1},{1,0},{2,3},{3,2},{4,5},{5,4},{6,7},{7,6},{8,9},{9,8},{10,11... | collective-permute-start | bytes 9437192 | tf_op jit(solution)/shard_map/ppermute | solution.py:580
  155.4 13.5 %collective-permute-start.27 = (bf16[2,512,768]{2,1,0:T(8,128)(2,1)}, bf16[2,512,768]{2,1,0:T(8,128)(2,1)}, u32[]{:S(2)}, u32[]{:S(2)}) collective-permute-start(bf16[2,512,768]{2,1,0:T(8,128)(2,1)} %maximum_select_fusion.2), channel_id=1, source_target_pairs={{0,1},{1,0},{2,3},{3,2},{4,5},{5,4},{6,7},{7,6},{8,9},{9,8},{10,11... | collective-permute-start | bytes 4718600 | tf_op jit(solution)/shard_map/ppermute | solution.py:580
  155.9 12.9 %collective-permute-start.26 = (bf16[512,192]{1,0:T(8,128)(2,1)}, bf16[512,192]{1,0:T(8,128)(2,1)S(1)}, u32[]{:S(2)}, u32[]{:S(2)}) collective-permute-start(bf16[512,192]{1,0:T(8,128)(2,1)} %get-tuple-element.188), channel_id=1, source_target_pairs={{0,2},{1,3},{2,0},{3,1},{4,6},{5,7},{6,4},{7,5},{8,10},{9,11},{10,... | collective-permute-start | bytes 589832 | tf_op jit(solution)/shard_map/ppermute | solution.py:580
  169.7 13.9 %collective-permute-start.30 = (bf16[2,192,768]{2,1,0:T(8,128)(2,1)}, bf16[2,192,768]{2,1,0:T(8,128)(2,1)}, u32[]{:S(2)}, u32[]{:S(2)}) collective-permute-start(bf16[2,192,768]{2,1,0:T(8,128)(2,1)} %constant_dynamic-slice_fusion.6), channel_id=1, source_target_pairs={{0,8},{1,5},{2,10},{3,7},{4,12},{5,1},{6,14},{7,3},{8,0},{9,13},{1... | collective-permute-start | bytes 1769480 | tf_op jit(solution)/shard_map/ppermute | solution.py:635
  171.4 12.2 %collective-permute-start.29 = (bf16[256,768]{1,0:T(8,128)(2,1)}, bf16[256,768]{1,0:T(8,128)(2,1)S(1)}, u32[]{:S(2)}, u32[]{:S(2)}) collective-permute-start(bf16[256,768]{1,0:T(8,128)(2,1)} %get-tuple-element.248), channel_id=1, source_target_pairs={{0,2},{1,3},{2,0},{3,1},{4,6},{5,7},{6,4},{7,5},{8,10},{9,11},{10,... | collective-permute-start | bytes 1179656 | tf_op jit(solution)/shard_map/ppermute | solution.py:580
  171.9 10.6 %collective-permute-start.31 = (bf16[512,192]{1,0:T(8,128)(2,1)}, bf16[512,192]{1,0:T(8,128)(2,1)S(1)}, u32[]{:S(2)}, u32[]{:S(2)}) collective-permute-start(bf16[512,192]{1,0:T(8,128)(2,1)} %get-tuple-element.203), channel_id=1, source_target_pairs={{0,1},{1,0},{2,3},{3,2},{4,5},{5,4},{6,7},{7,6},{8,9},{9,8},{10,11... | collective-permute-start | bytes 589832 | tf_op jit(solution)/shard_map/ppermute | solution.py:580
  172.9 35.1 %collective-permute-start.28 = (bf16[256,768]{1,0:T(8,128)(2,1)S(1)}, bf16[256,768]{1,0:T(8,128)(2,1)S(1)}, u32[]{:S(2)}, u32[]{:S(2)}) collective-permute-start(bf16[256,768]{1,0:T(8,128)(2,1)S(1)} %copy-done.15), channel_id=1, source_target_pairs={{0,2},{1,3},{2,0},{3,1},{4,6},{5,7},{6,4},{7,5},{8,10},{9,11},{10,... | collective-permute-start | bytes 1179656 | tf_op jit(solution)/shard_map/ppermute | solution.py:580
  174.4 33.6 %collective-permute-start.32 = (bf16[512,768]{1,0:T(8,128)(2,1)S(1)}, bf16[512,768]{1,0:T(8,128)(2,1)S(1)}, u32[]{:S(2)}, u32[]{:S(2)}) collective-permute-start(bf16[512,768]{1,0:T(8,128)(2,1)S(1)} %slice_bitcast_fusion.1), channel_id=1, source_target_pairs={{0,2},{1,3},{2,0},{3,1},{4,6},{5,7},{6,4},{7,5},{8,10},{9,11},{10,... | collective-permute-start | bytes 2359304 | tf_op jit(solution)/shard_map/ppermute | solution.py:580
  175.0 8.7 %copy-start.4 = (bf16[2,384,768]{2,1,0:T(8,128)(2,1)S(1)}, bf16[2,384,768]{2,1,0:T(8,128)(2,1)}, u32[]{:S(2)}) copy-start(bf16[2,384,768]{2,1,0:T(8,128)(2,1)} %copy-done.3) | copy-start | bytes 3538948
  185.6 22.4 %collective-permute-start.33 = (bf16[2,96,768]{2,1,0:T(8,128)(2,1)S(1)}, bf16[2,96,768]{2,1,0:T(8,128)(2,1)S(1)}, u32[]{:S(2)}, u32[]{:S(2)}) collective-permute-start(bf16[2,96,768]{2,1,0:T(8,128)(2,1)S(1)} %constant_dynamic-slice_fusion.5), channel_id=1, source_target_pairs={{0,16},{1,17},{2,18},{3,19},{4,20},{5,21},{6,22},{7,23},{8,24},{9,... | collective-permute-start | bytes 884744 | tf_op jit(solution)/shard_map/ppermute | solution.py:635
  208.0 11.7 %collective-permute-start.34 = (bf16[512,768]{1,0:T(8,128)(2,1)}, bf16[512,768]{1,0:T(8,128)(2,1)}, u32[]{:S(2)}, u32[]{:S(2)}) collective-permute-start(bf16[512,768]{1,0:T(8,128)(2,1)} %get-tuple-element.222), channel_id=1, source_target_pairs={{0,1},{1,0},{2,3},{3,2},{4,5},{5,4},{6,7},{7,6},{8,9},{9,8},{10,11... | collective-permute-start | bytes 2359304 | tf_op jit(solution)/shard_map/ppermute | solution.py:580
  209.7 12.2 %collective-permute-start.36 = (bf16[512,768]{1,0:T(8,128)(2,1)}, bf16[512,768]{1,0:T(8,128)(2,1)S(1)}, u32[]{:S(2)}, u32[]{:S(2)}) collective-permute-start(bf16[512,768]{1,0:T(8,128)(2,1)} %constant_dynamic-slice_fusion.4), channel_id=1, source_target_pairs={{0,4},{1,9},{2,6},{3,11},{4,0},{5,13},{6,2},{7,15},{8,12},{9,1},{1... | collective-permute-start | bytes 2359304 | tf_op jit(solution)/shard_map/ppermute | solution.py:635
  211.4 8.3 %collective-permute-start.35 = (bf16[96,768]{1,0:T(8,128)(2,1)S(1)}, bf16[96,768]{1,0:T(8,128)(2,1)S(1)}, u32[]{:S(2)}, u32[]{:S(2)}) collective-permute-start(bf16[96,768]{1,0:T(8,128)(2,1)S(1)} %slice_bitcast_fusion.11), channel_id=1, source_target_pairs={{0,2},{1,3},{2,0},{3,1},{4,6},{5,7},{6,4},{7,5},{8,10},{9,11},{10,... | collective-permute-start | bytes 442376 | tf_op jit(solution)/shard_map/ppermute | solution.py:580
  219.7 7.9 %collective-permute-start.40 = (bf16[512,768]{1,0:T(8,128)(2,1)}, bf16[512,768]{1,0:T(8,128)(2,1)S(1)}, u32[]{:S(2)}, u32[]{:S(2)}) collective-permute-start(bf16[512,768]{1,0:T(8,128)(2,1)} %get-tuple-element.227), channel_id=1, source_target_pairs={{0,1},{1,0},{2,3},{3,2},{4,5},{5,4},{6,7},{7,6},{8,9},{9,8},{10,11... | collective-permute-start | bytes 2359304 | tf_op jit(solution)/shard_map/ppermute | solution.py:580
  222.1 15.1 %collective-permute-start.37 = (bf16[256,768]{1,0:T(8,128)(2,1)S(1)}, bf16[256,768]{1,0:T(8,128)(2,1)S(1)}, u32[]{:S(2)}, u32[]{:S(2)}) collective-permute-start(bf16[256,768]{1,0:T(8,128)(2,1)S(1)} %constant_dynamic-slice_fusion.3), channel_id=1, source_target_pairs={{0,8},{1,5},{2,10},{3,7},{4,12},{5,1},{6,14},{7,3},{8,0},{9,13},{1... | collective-permute-start | bytes 1179656 | tf_op jit(solution)/shard_map/ppermute | solution.py:635
  223.1 14.2 %collective-permute-start.38 = (bf16[320,768]{1,0:T(8,128)(2,1)S(1)}, bf16[320,768]{1,0:T(8,128)(2,1)S(1)}, u32[]{:S(2)}, u32[]{:S(2)}) collective-permute-start(bf16[320,768]{1,0:T(8,128)(2,1)S(1)} %constant_dynamic-slice_fusion.2), channel_id=1, source_target_pairs={{0,4},{1,9},{2,6},{3,11},{4,0},{5,13},{6,2},{7,15},{8,12},{9,1},{1... | collective-permute-start | bytes 1474568 | tf_op jit(solution)/shard_map/ppermute | solution.py:635
  223.8 11.7 %collective-permute-start.39 = (bf16[96,768]{1,0:T(8,128)(2,1)S(1)}, bf16[96,768]{1,0:T(8,128)(2,1)S(1)}, u32[]{:S(2)}, u32[]{:S(2)}) collective-permute-start(bf16[96,768]{1,0:T(8,128)(2,1)S(1)} %fusion.9), channel_id=1, source_target_pairs={{0,16},{1,17},{2,18},{3,19},{4,20},{5,21},{6,22},{7,23},{8,24},{9,... | collective-permute-start | bytes 442376 | tf_op jit(solution)/shard_map/ppermute | solution.py:635
  227.5 13.2 %copy-start.7 = (f32[512,768]{1,0:T(8,128)S(1)}, f32[512,768]{1,0:T(8,128)}, u32[]{:S(2)}) copy-start(f32[512,768]{1,0:T(8,128)} %get-tuple-element.195) | copy-start | bytes 4718596
  227.6 13.2 %copy-start.14 = (bf16[512,768]{1,0:T(8,128)(2,1)S(1)}, bf16[512,768]{1,0:T(8,128)(2,1)}, u32[]{:S(2)}) copy-start(bf16[512,768]{1,0:T(8,128)(2,1)} %get-tuple-element.194) | copy-start | bytes 2359300
  237.4 20.9 %collective-permute-start.41 = (bf16[256,768]{1,0:T(8,128)(2,1)S(1)}, bf16[256,768]{1,0:T(8,128)(2,1)}, u32[]{:S(2)}, u32[]{:S(2)}) collective-permute-start(bf16[256,768]{1,0:T(8,128)(2,1)S(1)} %add_convert_fusion.10), channel_id=1, source_target_pairs={{0,16},{1,17},{2,18},{3,19},{4,20},{5,21},{6,22},{7,23},{8,24},{9,... | collective-permute-start | bytes 1179656 | tf_op jit(solution)/shard_map/ppermute | solution.py:635
  239.2 14.9 %collective-permute-start.43 = (bf16[192,768]{1,0:T(8,128)(2,1)S(1)}, bf16[192,768]{1,0:T(8,128)(2,1)}, u32[]{:S(2)}, u32[]{:S(2)}) collective-permute-start(bf16[192,768]{1,0:T(8,128)(2,1)S(1)} %maximum_select_fusion.18), channel_id=1, source_target_pairs={{0,8},{1,5},{2,10},{3,7},{4,12},{5,1},{6,14},{7,3},{8,0},{9,13},{1... | collective-permute-start | bytes 884744 | tf_op jit(solution)/shard_map/ppermute | solution.py:635
  242.6 15.8 %collective-permute-start.44 = (bf16[2,160,768]{2,1,0:T(8,128)(2,1)}, bf16[2,160,768]{2,1,0:T(8,128)(2,1)}, u32[]{:S(2)}, u32[]{:S(2)}) collective-permute-start(bf16[2,160,768]{2,1,0:T(8,128)(2,1)} %pad_maximum_fusion.2), channel_id=1, source_target_pairs={{0,2},{1,3},{2,0},{3,1},{4,6},{5,7},{6,4},{7,5},{8,10},{9,11},{10,... | collective-permute-start | bytes 1474568 | tf_op jit(solution)/shard_map/ppermute | solution.py:580
  243.9 10.1 %collective-permute-start.42 = (bf16[160,768]{1,0:T(8,128)(2,1)}, bf16[160,768]{1,0:T(8,128)(2,1)}, u32[]{:S(2)}, u32[]{:S(2)}) collective-permute-start(bf16[160,768]{1,0:T(8,128)(2,1)} %constant_dynamic-slice_fusion.1), channel_id=1, source_target_pairs={{0,8},{1,5},{2,10},{3,7},{4,12},{5,1},{6,14},{7,3},{8,0},{9,13},{1... | collective-permute-start | bytes 737288 | tf_op jit(solution)/shard_map/ppermute | solution.py:635
  245.3 21.8 %collective-permute-start.48 = (bf16[2,160,768]{2,1,0:T(8,128)(2,1)}, bf16[2,160,768]{2,1,0:T(8,128)(2,1)}, u32[]{:S(2)}, u32[]{:S(2)}) collective-permute-start(bf16[2,160,768]{2,1,0:T(8,128)(2,1)} %pad_maximum_fusion.3), channel_id=1, source_target_pairs={{0,2},{1,3},{2,0},{3,1},{4,6},{5,7},{6,4},{7,5},{8,10},{9,11},{10,... | collective-permute-start | bytes 1474568 | tf_op jit(solution)/shard_map/ppermute | solution.py:580
  259.6 18.2 %collective-permute-start.47 = (bf16[384,768]{1,0:T(8,128)(2,1)S(1)}, bf16[384,768]{1,0:T(8,128)(2,1)}, u32[]{:S(2)}, u32[]{:S(2)}) collective-permute-start(bf16[384,768]{1,0:T(8,128)(2,1)S(1)} %maximum_select_fusion.12), channel_id=1, source_target_pairs={{0,4},{1,9},{2,6},{3,11},{4,0},{5,13},{6,2},{7,15},{8,12},{9,1},{1... | collective-permute-start | bytes 1769480 | tf_op jit(solution)/shard_map/ppermute | solution.py:635
  261.6 16.2 %collective-permute-start.45 = (bf16[256,768]{1,0:T(8,128)(2,1)S(1)}, bf16[256,768]{1,0:T(8,128)(2,1)}, u32[]{:S(2)}, u32[]{:S(2)}) collective-permute-start(bf16[256,768]{1,0:T(8,128)(2,1)S(1)} %add_convert_fusion.9), channel_id=1, source_target_pairs={{0,8},{1,5},{2,10},{3,7},{4,12},{5,1},{6,14},{7,3},{8,0},{9,13},{1... | collective-permute-start | bytes 1179656 | tf_op jit(solution)/shard_map/ppermute | solution.py:635
  262.7 12.8 %collective-permute-start.46 = (bf16[160,768]{1,0:T(8,128)(2,1)S(1)}, bf16[160,768]{1,0:T(8,128)(2,1)S(1)}, u32[]{:S(2)}, u32[]{:S(2)}) collective-permute-start(bf16[160,768]{1,0:T(8,128)(2,1)S(1)} %add_convert_fusion.13), channel_id=1, source_target_pairs={{0,16},{1,17},{2,18},{3,19},{4,20},{5,21},{6,22},{7,23},{8,24},{9,... | collective-permute-start | bytes 737288 | tf_op jit(solution)/shard_map/ppermute | solution.py:635
  279.1 16.5 %collective-permute-start.49 = (bf16[512,768]{1,0:T(8,128)(2,1)S(1)}, bf16[512,768]{1,0:T(8,128)(2,1)S(1)}, u32[]{:S(2)}, u32[]{:S(2)}) collective-permute-start(bf16[512,768]{1,0:T(8,128)(2,1)S(1)} %maximum_select_fusion.9), channel_id=1, source_target_pairs={{0,4},{1,9},{2,6},{3,11},{4,0},{5,13},{6,2},{7,15},{8,12},{9,1},{1... | collective-permute-start | bytes 2359304 | tf_op jit(solution)/shard_map/ppermute | solution.py:635
  280.2 15.3 %collective-permute-start.51 = (bf16[2,192,768]{2,1,0:T(8,128)(2,1)S(1)}, bf16[2,192,768]{2,1,0:T(8,128)(2,1)S(1)}, u32[]{:S(2)}, u32[]{:S(2)}) collective-permute-start(bf16[2,192,768]{2,1,0:T(8,128)(2,1)S(1)} %pad_maximum_fusion.1), channel_id=1, source_target_pairs={{0,2},{1,3},{2,0},{3,1},{4,6},{5,7},{6,4},{7,5},{8,10},{9,11},{10,... | collective-permute-start | bytes 1769480 | tf_op jit(solution)/shard_map/ppermute | solution.py:580
  281.4 14.2 %collective-permute-start.50 = (bf16[160,768]{1,0:T(8,128)(2,1)S(1)}, bf16[160,768]{1,0:T(8,128)(2,1)S(1)}, u32[]{:S(2)}, u32[]{:S(2)}) collective-permute-start(bf16[160,768]{1,0:T(8,128)(2,1)S(1)} %add_convert_fusion.12), channel_id=1, source_target_pairs={{0,8},{1,5},{2,10},{3,7},{4,12},{5,1},{6,14},{7,3},{8,0},{9,13},{1... | collective-permute-start | bytes 737288 | tf_op jit(solution)/shard_map/ppermute | solution.py:635
  296.1 17.5 %collective-permute-start.53 = (bf16[2,512,768]{2,1,0:T(8,128)(2,1)S(1)}, bf16[2,512,768]{2,1,0:T(8,128)(2,1)S(1)}, u32[]{:S(2)}, u32[]{:S(2)}) collective-permute-start(bf16[2,512,768]{2,1,0:T(8,128)(2,1)S(1)} %get-tuple-element.250), channel_id=1, source_target_pairs={{0,1},{1,0},{2,3},{3,2},{4,5},{5,4},{6,7},{7,6},{8,9},{9,8},{10,11... | collective-permute-start | bytes 4718600 | tf_op jit(solution)/shard_map/ppermute | solution.py:580
  304.6 8.9 %collective-permute-start.52 = (bf16[320,768]{1,0:T(8,128)(2,1)S(1)}, bf16[320,768]{1,0:T(8,128)(2,1)S(1)}, u32[]{:S(2)}, u32[]{:S(2)}) collective-permute-start(bf16[320,768]{1,0:T(8,128)(2,1)S(1)} %maximum_select_fusion.16), channel_id=1, source_target_pairs={{0,4},{1,9},{2,6},{3,11},{4,0},{5,13},{6,2},{7,15},{8,12},{9,1},{1... | collective-permute-start | bytes 1474568 | tf_op jit(solution)/shard_map/ppermute | solution.py:635
  (18 other events, 40.9 us)

commit v3 on v2

--- a/solution.py
+++ b/solution.py
@@ -14,7 +14,7 @@
 TILE = 256
 ROW_TILE = 64
 VEC_ROWS = 64
-VMEM_BYTES = 56 * 1024 * 1024
+VMEM_BYTES = 52 * 1024 * 1024
 
 norm_eps = 1e-06
 inv_temp = 50.0
@@ -776,9 +776,11 @@
     in_got, back_got = hop(in_quarter, "dp", 2), hop(back_quarter, "dp", 1)
     qkv_own, probs_own, ctx0 = attend(1, lambda i: 0)
     out_parts = [out_pack, near_out, far_out, hop(late(far_out, ctx0), "mp", 1)]
+    ctx_got2, ctx_got3 = hop(ctx2, "mp", 2), hop(ctx3, "mp", 3)
     in_half = ordered(bit_z, in_quarter, late(in_got, ctx0), 0)
     back_half = ordered(bit_x, back_quarter, late(back_got, ctx0), 0)
-    ctx_parts = [ctx0, hop(ctx1, "mp", 1), hop(ctx2, "mp", 2), hop(ctx3, "mp", 3)]
+    in_half, back_half, ctx_got2, ctx_got3 = together(in_half, back_half, ctx_got2, ctx_got3)
+    ctx_parts = [ctx0, hop(ctx1, "mp", 1), ctx_got2, ctx_got3]
     seg_own = lax.dynamic_slice_in_dim(segment_ids, member, 1)
     pair_own = lax.dynamic_slice_in_dim(pair_ids, member, 1).reshape(-1, 1)
     pair_code = jnp.concatenate(
@@ -832,10 +834,13 @@
     )
 
     everyone = msg[None]
-    for flip in reversed(bits_below(lax.axis_size("dp"))):
-        everyone = both_ways("dp", flip, everyone)
-    for flip in reversed(bits_below(lax.axis_size("mp"))):
-        everyone = both_ways("mp", flip, everyone)
+    steps = [("dp", flip) for flip in reversed(bits_below(lax.axis_size("dp")))]
+    steps += [("mp", flip) for flip in reversed(bits_below(lax.axis_size("mp")))]
+    while len(steps) > 1:
+        everyone = four_ways(everyone, *steps[:2])
+        steps = steps[2:]
+    if steps:
+        everyone = both_ways(everyone, hop(everyone, *steps[0]), *steps[0])
     everyone = everyone.reshape(-1, msg.shape[1])
 
     loss, grad_pooled = pl.pallas_call(
@@ -921,13 +926,10 @@
     first_got = hop(first_send, "mp", 1)
     got2 = hop(late(ctx_grads[2], first_send), "mp", 2)
     first_keep = first_grads((2, 0), attn_low)
-    first_sum = add_low(first_keep, first_got)
-    own_grad, first_sum, got2, back_sum, out_other = together(
-        ctx_grads[0], first_sum, got2, back_sum, out_other
-    )
-    first_far, first_near = first_sum[0], first_sum[1]
-    cut = first_far.shape[0] // 4
-    far0 = hop(first_far[:cut], "mp", 2)
+    own_grad, first_keep, first_got, got2, back_sum, out_other = together(
+        ctx_grads[0], first_keep, first_got, got2, back_sum, out_other
+    )
+    first_far = hop(add_low(first_keep[0], first_got[0]), "mp", 2)
     back_got = rows.send(back_sum, 1)
     got1 = hop(late(ctx_grads[1], own_grad), "mp", 1)
 
@@ -970,19 +972,19 @@
         )(m_arr, tokens, w_t, qkv, probs, *grads, *sums)
 
     back0, *sums = attend_back(1, lambda i: 0, 0, qkv_own, probs_own, [own_grad], [])
-    far0, back_got, got1, *sums = together(far0, back_got, got1, *sums)
-    far1 = hop(first_far[cut : 3 * cut], "mp", 2)
+    back_got, got1, *sums = together(back_got, got1, *sums)
     back_sum = rows.keep(back_sum, back_got, 1)
     back_got = rows.send(back_sum, 2)
     back3, back2, *sums = attend_back(2, lambda i: 3 - i, 0, qkv_away, probs_away, [got3, got2], sums)
-    far1, back_got, *sums = together(far1, back_got, *sums)
-    far2 = hop(first_far[3 * cut :], "mp", 2)
+    back_got, *sums = together(back_got, *sums)
     back_sum = rows.keep(back_sum, back_got, 2)
     for step in range(3, rows.steps):
         back_sum = rows.keep(back_sum, rows.send(back_sum, step), step)
     back_got = hop(back_sum[0], "mp", 2)
-    far2, first_near, back3, *sums = together(far2, first_near, back3, *sums)
-    first_sum = add_low(first_near, jnp.concatenate([far0, far1, far2], axis=0))
+    first_far, first_keep, first_got, back3, *sums = together(
+        first_far, first_keep, first_got, back3, *sums
+    )
+    first_sum = (first_keep[1].astype(f32) + first_got[1].astype(f32) + first_far.astype(f32)).astype(bf16)
     first_got = rows.send(first_sum, 0)
     tok_got3 = hop(back3, "mp", 1)
     back1, d_qkv = attend_back(1, lambda i: 1, 2, qkv_away, probs_away, [got1], sums)
@@ -999,38 +1001,26 @@
         Running(rows, d_qkv, down + up),
         Running(rows, back_sum, [("join", last)] + up),
     ]
-    sizes = [length // 48 * 16] * 2
-    sizes.append(length - sum(sizes))
-    mine, pieces, tok_totals, at, stage = None, None, [], 0, 0
+    stage, extra = 0, [tok_got1, hop(far, "mp", 2)]
     while any(part.plan for part in sums):
         parts = [part for part in sums if part.plan]
-        hops = [part.start() for part in parts]
-        if stage == 0:
-            hops.append(tok_got1)
-        elif stage <= len(sizes):
-            rows_now = slice(at, at + sizes[stage - 1])
-            at += sizes[stage - 1]
-            hops.append(hop(jnp.stack([mine[rows_now], far[rows_now]]), "mp", 2))
-        elif stage == len(sizes) + 1:
-            tok_pair = jnp.concatenate(tok_totals, axis=1)
-            hops.append(hop(tok_pair, "mp", 1))
-        hops = list(together(*hops))
+        starts = [part.start() for part in parts]
+        if extra:
+            tied = list(together(starts[1], *extra))
+            starts[1] = tied.pop(0)
+        hops = starts + (tied if extra else [])
         for part in parts:
             part.finish(hops.pop(0))
         if stage == 0:
-            mine = add_low(back0.astype(f32) + grad_resid1, hops[0])
-        elif stage <= len(sizes):
-            got = hops[0]
-            tok_totals.append(
-                ordered(
-                    bit_of("mp", 2),
-                    add_low(mine[rows_now], got[1])[None],
-                    add_low(far[rows_now], got[0])[None],
-                    0,
-                )
-            )
-        elif stage == len(sizes) + 1:
+            own = back0.astype(f32) + grad_resid1 + hops[0].astype(f32) + hops[1].astype(f32)
+            own = own.astype(bf16)
+            extra = [hop(own, "mp", 2)]
+        elif stage == 1:
+            tok_pair = ordered(bit_of("mp", 2), own[None], hops[0][None], 0)
+            extra = [hop(tok_pair, "mp", 1)]
+        elif stage == 2:
             d_tokens = rows_of_all(tok_pair, hops[0])
+            extra = []
         stage += 1
     sum_first, sum_qkv, sum_back = (part.array for part in sums)
     layer_out = rows_of_all(out_pair, out_other)
@@ -1060,12 +1050,25 @@
     )
 
 
-def both_ways(axis, flip, array):
-    other = hop(array, axis, flip)
+def both_ways(array, other, axis, flip):
     low_first = jnp.stack([array, other], axis=1)
     high_first = jnp.stack([other, array], axis=1)
     joined = jnp.where(bit_of(axis, flip) == 0, low_first, high_first)
     return joined.reshape(-1, *array.shape[1:])
+
+
+def four_ways(array, first, second):
+    dp, mp = lax.axis_size("dp"), lax.axis_size("mp")
+
+    def fetch(*steps):
+        flip = sum(step * (mp if axis == "dp" else 1) for axis, step in steps)
+        return lax.ppermute(array, ("dp", "mp"), [(i, i ^ flip) for i in range(dp * mp)])
+
+    far, near, corner = fetch(first), fetch(second), fetch(first, second)
+    count = array.shape[0]
+    mine = both_ways(array, near, *second).reshape(count, 2, *array.shape[1:])
+    theirs = both_ways(far, corner, *second).reshape(count, 2, *array.shape[1:])
+    return both_ways(mine, theirs, *first).reshape(-1, *array.shape[1:])
 
 
 def rows_of_all(pair, other):

time: 325 us -> 307 us (0.945)
  Pallas kernels: 121 us -> 112 us
  waiting for transfers between devices: 88.3 us -> 79.4 us
    ppermute x38 -> x31, waiting for transfers between devices: 50.3 us -> 21.4 us  [hop(): return lax.ppermute(array, axis, [(i, i ^ flip) for i in range(size)])]
    ppermute x16, waiting for transfers between devices: 38 us -> 51.1 us  [swap(): return lax.ppermute(values, ('dp', 'mp'), pairs)]
    ppermute x38 -> x31, starting transfers between devices: 31.1 us -> 20.8 us  [hop(): return lax.ppermute(array, axis, [(i, i ^ flip) for i in range(size)])]
    ppermute x0 -> x6, starting transfers between devices: none -> 8.01 us  [fetch(): lax.ppermute(array, ('dp', 'mp'), [(i, i ^ flip) for i in range(dp * mp)])]
    ppermute x0 -> x6, waiting for transfers between devices: none -> 6.88 us  [fetch(): lax.ppermute(array, ('dp', 'mp'), [(i, i ^ flip) for i in range(dp * mp)])]
    convert_element_type x0 -> x2, other arithmetic: none -> 4.32 us  [the longest x1 2.44 us: shards(): (first_keep[1].astype(f32) + first_got[1].astype(f32) + first_far.astype(...]
    convert_element_type x15 -> x13, other arithmetic: 12.8 us -> 16.6 us  [add_low(): return (left_side.astype(f32) + right_side.astype(f32)).astype(bf16)]
  transfers between devices with their start and end apart: 54 -> 53, of which waited for: 22 -> 24; matrix products, arithmetic and copies ran while one was open for 12% -> 14% of each run, Pallas kernels for 31% -> 31%
where the time goes in v3:
time: 307 us; the launch traced here: 301 us
  Pallas kernels  112 us (36%)
  waiting for transfers between devices  79.4 us (26%)
  starting transfers between devices  51.7 us (17%)
  other arithmetic  40.9 us (13%)
  local copies, waits for them, and re-layouts  15.3 us (5%)
    ppermute x16, waiting for transfers between devices, swap(): return lax.ppermute(values, ('dp', 'mp'), pairs)  51.1 us
    pallas_call x3, Pallas kernels, attend_back(): pl.pallas_call(functools.partial(attend_backward, count, len(sums) == 0,...  28 us
    ppermute x16, starting transfers between devices, swap(): return lax.ppermute(values, ('dp', 'mp'), pairs)  22.9 us
    ppermute x31, waiting for transfers between devices, hop(): return lax.ppermute(array, axis, [(i, i ^ flip) for i in range(size)])  21.4 us
    ppermute x31, starting transfers between devices, hop(): return lax.ppermute(array, axis, [(i, i ^ flip) for i in range(size)])  20.8 us
    pallas_call x2, Pallas kernels, attend(): pl.pallas_call(attend_forward, grid_spec=pltpu.PrefetchScalarGridSpec(num...  17.2 us
    convert_element_type x13, other arithmetic, add_low(): return (left_side.astype(f32) + right_side.astype(f32)).astype(bf16)  16.6 us
    pallas_call x1, Pallas kernels, shards(): pl.pallas_call(back_first, in_specs=[vmem_spec] * 5 + [any_spec] * 14, ou...  16.2 us
  transfers between devices with their start and end apart: 53, of which 24 were waited for; matrix products, arithmetic and copies ran while one was open for 14% of the time, Pallas kernels for 31%

profile of v3, /device:TPU:0, one launch (start us, length us, event | category | flops | bytes accessed | tf_op | source)
XLA Modules:
  0.0 300.9 jit_solution(3610031181816429999)
XLA Ops:
  3.0 1.6 prepare.1
  5.1 2.6 collective-permute-start.5
  7.8 1.9 collective-permute-start.4
  10.0 12.5 %attend_forward.3 = (bf16[3,3,512,192]{3,2,1,0:T(8,128)(2,1)}, bf16[3,12,128,256]{3,2,1,0:T(8,128)(2,1)}, bf16[512,192]{1,0:T(8,128)(2,1)S(1)}, bf16[512,192]{1,0:T(8,128)(2,1)S(1)}, bf16[512,192]{1,0:T(8,128)(2,1)S(1)}) custom-call(s32[1]{0:T(128)} %bitcast.5.m_ref, bf16[2048,768]{1,0:T(8,128)(2,1)} %tok_ref.9, bf16[3,192,768]{2,1,0:T(8,128)(2,1)S(1)} %bitcast.67, ...), custom_call_target="tpu_custom_call" | custom-call | flops 1358954496 | bytes 6000000 | tf_op jit(solution)/shard_map/attend_forward/pallas_call | solution.py:744
  23.1 5.5 %collective-permute-done.4 = bf16[192,768]{1,0:T(8,128)(2,1)} collective-permute-done((bf16[192,768]{1,0:T(8,128)(2,1)S(1)}, bf16[192,768]{1,0:T(8,128)(2,1)}, u32[]{:S(2)}, u32[]{:S(2)}) %collective-permute-start.4) | collective-permute-done | bytes 294944 | tf_op jit(solution)/shard_map/ppermute | solution.py:580
  28.6 1.8 collective-permute-start.7
  30.4 1.5 collective-permute-start.8
  31.9 1.5 collective-permute-start.9
  33.4 4.8 %attend_forward.2 = (bf16[1,3,512,192]{3,2,1,0:T(8,128)(2,1)S(1)}, bf16[1,12,128,256]{3,2,1,0:T(8,128)(2,1)S(1)}, bf16[512,192]{1,0:T(8,128)(2,1)S(1)}) custom-call(s32[1]{0:T(128)} %bitcast.5.m_ref, bf16[2048,768]{1,0:T(8,128)(2,1)} %tok_ref.9, bf16[3,192,768]{2,1,0:T(8,128)(2,1)} %bitcast.64, f32[2,192]{1,0:T(2,128)S(1)} %copy-done.20, ...), custom_call_target="tpu_custom_call" | custom-call | flops 452984832 | bytes 2000000 | tf_op jit(solution)/shard_map/attend_forward/pallas_call | solution.py:744
  41.1 1.4 maximum_select_fusion.13
  42.5 1.6 collective-permute-done.10.c3.ca
  47.0 12.3 %middle_first.1 = (bf16[2,512,768]{2,1,0:T(8,128)(2,1)}, bf16[2,512,768]{2,1,0:T(8,128)(2,1)}, f32[512,768]{1,0:T(8,128)}, f32[512,128]{1,0:T(8,128)S(1)}, bf16[512,768]{1,0:T(8,128)(2,1)}, /*index=5*/f32[512,768]{1,0:T(8,128)}) custom-call(s32[1]{0:T(128)} %bitcast.5.m_ref, bf16[2048,768]{1,0:T(8,128)(2,1)} %tok_ref.9, f32[6,128]{1,0:T(8,128)S(1)} %bitcast.78, ...), custom_call_target="tpu_custom_call" | custom-call | flops 3019898880 | bytes 18000000 | tf_op jit(solution)/shard_map/middle_first/pallas_call | solution.py:790
  60.1 1.5 maximum_select_fusion.6.wi2
  61.7 1.5 maximum_select_fusion.7.wb2
  64.9 1.7 collective-permute-done.15.wb3
  66.6 11.4 %middle_second.1 = (bf16[2,512,768]{2,1,0:T(8,128)(2,1)}, bf16[2,512,768]{2,1,0:T(8,128)(2,1)}, f32[512,768]{1,0:T(8,128)}, f32[512,128]{1,0:T(8,128)S(1)}, bf16...) custom-call(s32[1,512]{1,0:T(1,128)S(1)} %constant_dynamic-slice_fusion.9, ...), custom_call_target="tpu_custom_call" | custom-call | flops 2415919104 | bytes 12000000 | tf_op jit(solution)/shard_map/middle_second/pallas_call | solution.py:815
  77.9 2.5 collective-permute-start.18
  80.7 1.7 collective-permute-start.16
  82.4 1.4 collective-permute-done.18
  83.8 1.8 collective-permute-done.17
  85.6 2.1 collective-permute-start.21
  89.1 2.3 collective-permute-done.21
  93.2 1.7 collective-permute-done.22
  96.3 7.0 %back_second.1 = (bf16[512,768]{1,0:T(8,128)(2,1)S(1)}, f32[512,768]{1,0:T(8,128)}, f32[8,768]{1,0:T(8,128)S(1)}, bf16[2,768,768]{2,1,0:T(8,128)(2,1)}) custom-call(f32[16,768]{1,0:T(8,128)S(1)} %get-tuple-element.157.gp_ref, s32[1,512]{1,0:T(1,128)S(1)} %constant_dynamic-slice_fusion.9.seg_ref, f32[512,768]{1,0:T(8,128)} %get-tuple-element.158.xhat_ref, ...), custom_call_target="tpu_custom_call" | custom-call | flops 1207959552 | bytes 14000000 | tf_op jit(solution)/shard_map/back_second/pallas_call | solution.py:857
  103.5 4.4 %back_outer.1 = bf16[2,768,768]{2,1,0:T(8,128)(2,1)} custom-call(bf16[512,768]{1,0:T(8,128)(2,1)S(1)} %get-tuple-element.164.low_ref, bf16[2,512,768]{2,1,0:T(8,128)(2,1)} %get-tuple-element.160.act01_hbm, bf16[2,512,768]{2,1,0:T(8,128)(2,1)} %get-tuple-element.161.act23_hbm), custom_call_target="tpu_custom_call" | custom-call | flops 1207959552 | bytes 8000000 | tf_op jit(solution)/shard_map/back_outer/pallas_call | solution.py:873
  108.3 2.9 add_convert_fusion
  111.3 1.6 collective-permute-start.25
  113.6 16.2 %back_first.1 = (bf16[4,512,768]{2,1,0:T(8,128)(2,1)}, f32[512,768]{1,0:T(8,128)}, bf16[512,768]{1,0:T(8,128)(2,1)}, f32[8,768]{1,0:T(8,128)S(1)}, f32[4,768]{1,...) custom-call(bf16[512,768]{1,0:T(8,128)(2,1)} %copy-done.6, ...), custom_call_target="tpu_custom_call" | custom-call | flops 5435817984 | bytes 25000000 | tf_op jit(solution)/shard_map/back_first/pallas_call | solution.py:887
  131.3 6.4 %weight_grads.2 = bf16[2,1024,768]{2,1,0:T(8,128)(2,1)} custom-call(bf16[512,768]{1,0:T(8,128)(2,1)S(1)} %copy-done.4, bf16[512,768]{1,0:T(8,128)(2,1)} %get-tuple-element.183.attn_ref, f32[8,768]{1,0:T(8,128)S(1)} %get-tuple-element.176.vec1_ref, f32[8,768]{1,0:T(8,128)S(1)} %get-tuple-element.177.vec2_ref, f32[4,768]{1,0:T(4,128)S(1)} %get-tuple-element.178.bin_ref, ...), custom_call_target="tpu_custom_call" | custom-call | flops 1509949440 | bytes 7000000 | tf_op jit(solution)/shard_map/weight_grads/pallas_call | solution.py:913
  137.7 1.4 maximum_select_fusion.2
  140.8 2.9 add_convert_fusion.2
  143.7 5.9 %weight_grads.3 = bf16[2,1024,768]{2,1,0:T(8,128)(2,1)} custom-call(bf16[512,768]{1,0:T(8,128)(2,1)S(1)} %copy-done.4, bf16[512,768]{1,0:T(8,128)(2,1)} %get-tuple-element.183.attn_ref, f32[8,768]{1,0:T(8,128)S(1)} %get-tuple-element.176.vec1_ref, f32[8,768]{1,0:T(8,128)S(1)} %get-tuple-element.177.vec2_ref, f32[4,768]{1,0:T(4,128)S(1)} %get-tuple-element.178.bin_ref, ...), custom_call_target="tpu_custom_call" | custom-call | flops 1509949440 | bytes 7000000 | tf_op jit(solution)/shard_map/weight_grads/pallas_call | solution.py:913
  149.7 3.5 %fusion.1 = bf16[1024,768]{1,0:T(8,128)(2,1)} fusion(bf16[2,1024,768]{2,1,0:T(8,128)(2,1)} %collective-permute-done.27, bf16[2,1024,768]{2,1,0:T(8,128)(2,1)} %weight_grads.3), kind=kLoop, calls=%fused_computation.8 | loop fusion | flops 3145728 | bytes 4718592 | tf_op jit(solution)/shard_map/convert_element_type | solution.py:620
  155.2 1.5 collective-permute-start.30
  156.8 7.0 %attend_backward.3 = (bf16[512,768]{1,0:T(8,128)(2,1)S(1)}, f32[576,768]{1,0:T(8,128)}, f32[8,192]{1,0:T(8,128)S(1)}) custom-call(s32[1]{0:T(128)} %bitcast.5.m_ref, bf16[2048,768]{1,0:T(8,128)(2,1)} %tok_ref.9, bf16[3,192,768]{2,1,0:T(8,128)(2,1)} %bitcast.65, bf16[1,3,512,192]{3,2,1,0:T(8,128)(2,1)S(1)} %get-tuple-element.189.qkv_ref, ...), custom_call_target="tpu_custom_call" | custom-call | flops 905969664 | bytes 4000000 | tf_op jit(solution)/shard_map/attend_backward/pallas_call | solution.py:947
  163.8 1.5 collective-permute-done.30
  166.6 2.4 collective-permute-start.33
  169.0 13.7 %attend_backward.4 = (bf16[512,768]{1,0:T(8,128)(2,1)}, bf16[512,768]{1,0:T(8,128)(2,1)}, f32[576,768]{1,0:T(8,128)}, f32[8,192]{1,0:T(8,128)S(1)}) custom-call(s32[1]{0:T(128)} %bitcast.5.m_ref, bf16[2048,768]{1,0:T(8,128)(2,1)} %tok_ref.9, bf16[3,192,768]{2,1,0:T(8,128)(2,1)} %bitcast.66, bf16[3,3,512,192]{3,2,1,0:T(8,128)(2,1)} %get-tuple-element.194.qkv_ref, ...), custom_call_target="tpu_custom_call" | custom-call | flops 1811939328 | bytes 8000000 | tf_op jit(solution)/shard_map/attend_backward/pallas_call | solution.py:947
  182.7 6.8 %collective-permute-done.32 = bf16[1024,768]{1,0:T(8,128)(2,1)} collective-permute-done((bf16[1024,768]{1,0:T(8,128)(2,1)}, bf16[1024,768]{1,0:T(8,128)(2,1)}, u32[]{:S(2)}, u32[]{:S(2)}) %collective-permute-start.32) | collective-permute-done | bytes 1572896 | tf_op jit(solution)/shard_map/ppermute | solution.py:580
  189.6 2.4 fusion
  196.2 1.5 collective-permute-start.35
  197.7 7.3 %attend_backward.5 = (bf16[512,768]{1,0:T(8,128)(2,1)S(1)}, bf16[640,768]{1,0:T(8,128)(2,1)}) custom-call(s32[1]{0:T(128)} %bitcast.5.m_ref, bf16[2048,768]{1,0:T(8,128)(2,1)} %tok_ref.9, bf16[3,192,768]{2,1,0:T(8,128)(2,1)S(1)} %bitcast.68, bf16[3,3,512,192]{3,2,1,0:T(8,128)(2,1)} %get-tuple-element.194.qkv_ref, ...), custom_call_target="tpu_custom_call" | custom-call | flops 905969664 | bytes 4000000 | tf_op jit(solution)/shard_map/attend_backward/pallas_call | solution.py:947
  206.4 2.2 add_convert_fusion.5
  211.8 1.4 collective-permute-start.46
  214.9 1.6 collective-permute-start.37
  216.5 1.9 collective-permute-start.50
  218.4 11.6 %collective-permute-done.46 = bf16[256,768]{1,0:T(8,128)(2,1)} collective-permute-done((bf16[256,768]{1,0:T(8,128)(2,1)}, bf16[256,768]{1,0:T(8,128)(2,1)}, u32[]{:S(2)}, u32[]{:S(2)}) %collective-permute-start.46) | collective-permute-done | bytes 393248 | tf_op jit(solution)/shard_map/ppermute | solution.py:635
  231.2 1.9 collective-permute-start.51
  233.2 1.9 add_convert_fusion.4
  236.3 6.7 %collective-permute-done.47 = bf16[256,768]{1,0:T(8,128)(2,1)S(1)} collective-permute-done((bf16[256,768]{1,0:T(8,128)(2,1)S(1)}, bf16[256,768]{1,0:T(8,128)(2,1)S(1)}, u32[]{:S(2)}, u32[]{:S(2)}) %collective-permute-start.47) | collective-permute-done | bytes 393248 | tf_op jit(solution)/shard_map/ppermute | solution.py:635
  243.4 2.1 collective-permute-start.40
  245.7 2.0 collective-permute-start.52
  247.7 7.6 %collective-permute-done.48 = bf16[256,768]{1,0:T(8,128)(2,1)S(1)} collective-permute-done((bf16[256,768]{1,0:T(8,128)(2,1)S(1)}, bf16[256,768]{1,0:T(8,128)(2,1)S(1)}, u32[]{:S(2)}, u32[]{:S(2)}) %collective-permute-start.48) | collective-permute-done | bytes 393248 | tf_op jit(solution)/shard_map/ppermute | solution.py:635
  255.6 2.0 collective-permute-start.49
  257.6 2.9 collective-permute-done.40
  260.9 3.6 %maximum_select_fusion = bf16[2,2,512,768]{3,2,0,1:T(8,128)(2,1)S(1)} fusion(bf16[2,1,512,768]{3,2,0,1:T(8,128)(2,1)} %bitcast.31, bf16[2,1,512,768]{3,2,0,1:T(8,128)(2,1)} %bitcast.30, pred[]{:T(512)S(6)} %eq.138), kind=kLoop, calls=%fused_computation.1 | loop fusion | flops 4718592 | bytes 6291457 | tf_op jit(solution)/shard_map/jit(_where)/select_n | solution.py:1077
  264.5 1.9 copy.42
  266.4 1.6 fusion.2
  270.3 1.6 slice_convert_fusion
  271.9 10.8 %collective-permute-done.42 = bf16[160,768]{1,0:T(8,128)(2,1)S(1)} collective-permute-done((bf16[160,768]{1,0:T(8,128)(2,1)S(1)}, bf16[160,768]{1,0:T(8,128)(2,1)S(1)}, u32[]{:S(2)}, u32[]{:S(2)}) %collective-permute-start.42) | collective-permute-done | bytes 245792 | tf_op jit(solution)/shard_map/ppermute | solution.py:635
  283.7 5.3 %collective-permute-done.44 = bf16[160,768]{1,0:T(8,128)(2,1)S(1)} collective-permute-done((bf16[160,768]{1,0:T(8,128)(2,1)S(1)}, bf16[160,768]{1,0:T(8,128)(2,1)S(1)}, u32[]{:S(2)}, u32[]{:S(2)}) %collective-permute-start.44) | collective-permute-done | bytes 245792 | tf_op jit(solution)/shard_map/ppermute | solution.py:635
  289.1 1.9 collective-permute-start.45
  292.8 1.9 copy.43
  294.7 3.3 %collective-permute-done.45 = bf16[320,768]{1,0:T(8,128)(2,1)S(1)} collective-permute-done((bf16[320,768]{1,0:T(8,128)(2,1)S(1)}, bf16[320,768]{1,0:T(8,128)(2,1)S(1)}, u32[]{:S(2)}, u32[]{:S(2)}) %collective-permute-start.45) | collective-permute-done | bytes 491552 | tf_op jit(solution)/shard_map/ppermute | solution.py:635
  (233 shorter events, 46.2 us)
Async XLA Ops:
  0.6 63.0 %copy-start = (s32[4,8]{1,0:T(4,128)S(1)}, s32[4,8]{1,0:T(4,128)}, u32[]{:S(2)}) copy-start(s32[4,8]{1,0:T(4,128)} %param.29) | copy-start | bytes 388
  0.7 9.2 %collective-permute-start = (bf16[768,768]{1,0:T(8,128)(2,1)}, bf16[768,768]{1,0:T(8,128)(2,1)}, u32[]{:S(2)}, u32[]{:S(2)}) collective-permute-start(bf16[768,768]{1,0:T(8,128)(2,1)} %wi0.3), channel_id=1, source_target_pairs={{0,1},{1,0},{2,3},{3,2},{4,5},{5,4},{6,7},{7,6},{8,9},{9,8},{10,11... | collective-permute-start | bytes 3538952 | tf_op jit(solution)/shard_map/ppermute | solution.py:580
  1.2 8.7 %collective-permute-start.1 = (bf16[768,768]{1,0:T(8,128)(2,1)}, bf16[768,768]{1,0:T(8,128)(2,1)}, u32[]{:S(2)}, u32[]{:S(2)}) collective-permute-start(bf16[768,768]{1,0:T(8,128)(2,1)} %wb0.3), channel_id=1, source_target_pairs={{0,1},{1,0},{2,3},{3,2},{4,5},{5,4},{6,7},{7,6},{8,9},{9,8},{10,11... | collective-permute-start | bytes 3538952 | tf_op jit(solution)/shard_map/ppermute | solution.py:580
  4.6 41.7 %copy-start.21 = (bf16[208,768]{1,0:T(8,128)(2,1)}, bf16[208,768]{1,0:T(8,128)(2,1)S(1)}, u32[]{:S(2)}) copy-start(bf16[208,768]{1,0:T(8,128)(2,1)S(1)} %get-tuple-element.125.wo0) | copy-start | bytes 958468
  4.6 3.2 %collective-permute-start.2 = (bf16[208,768]{1,0:T(8,128)(2,1)S(1)}, bf16[208,768]{1,0:T(8,128)(2,1)S(1)}, u32[]{:S(2)}, u32[]{:S(2)}) collective-permute-start(bf16[208,768]{1,0:T(8,128)(2,1)S(1)} %get-tuple-element.125.wo0), channel_id=1, source_target_pairs={{0,1},{1,0},{2,3},{3,2},{4,5},{5,4},{6,7},{7,6},{8,9},{9,8},{10,11... | collective-permute-start | bytes 958472 | tf_op jit(solution)/shard_map/ppermute | solution.py:580
  5.1 23.5 %collective-permute-start.5 = (bf16[208,768]{1,0:T(8,128)(2,1)S(1)}, bf16[208,768]{1,0:T(8,128)(2,1)S(1)}, u32[]{:S(2)}, u32[]{:S(2)}) collective-permute-start(bf16[208,768]{1,0:T(8,128)(2,1)S(1)} %get-tuple-element.125.wo0), channel_id=1, source_target_pairs={{0,2},{1,3},{2,0},{3,1},{4,6},{5,7},{6,4},{7,5},{8,10},{9,11},{10,... | collective-permute-start | bytes 958472 | tf_op jit(solution)/shard_map/ppermute | solution.py:580
  7.7 15.4 %collective-permute-start.3 = (bf16[192,768]{1,0:T(8,128)(2,1)S(1)}, bf16[192,768]{1,0:T(8,128)(2,1)S(1)}, u32[]{:S(2)}, u32[]{:S(2)}) collective-permute-start(bf16[192,768]{1,0:T(8,128)(2,1)S(1)} %get-tuple-element.131), channel_id=1, source_target_pairs={{0,2},{1,3},{2,0},{3,1},{4,6},{5,7},{6,4},{7,5},{8,10},{9,11},{10,... | collective-permute-start | bytes 884744 | tf_op jit(solution)/shard_map/ppermute | solution.py:580
  7.8 38.5 %copy-start.23 = (bf16[208,768]{1,0:T(8,128)(2,1)}, bf16[208,768]{1,0:T(8,128)(2,1)S(1)}, u32[]{:S(2)}) copy-start(bf16[208,768]{1,0:T(8,128)(2,1)S(1)} %collective-permute-done.2.wo1) | copy-start | bytes 958468
  7.8 20.8 %collective-permute-start.4 = (bf16[192,768]{1,0:T(8,128)(2,1)S(1)}, bf16[192,768]{1,0:T(8,128)(2,1)}, u32[]{:S(2)}, u32[]{:S(2)}) collective-permute-start(bf16[192,768]{1,0:T(8,128)(2,1)S(1)} %get-tuple-element.132), channel_id=1, source_target_pairs={{0,2},{1,3},{2,0},{3,1},{4,6},{5,7},{6,4},{7,5},{8,10},{9,11},{10,... | collective-permute-start | bytes 884744 | tf_op jit(solution)/shard_map/ppermute | solution.py:580
  28.6 11.2 %collective-permute-start.7 = (bf16[192,768]{1,0:T(8,128)(2,1)S(1)}, bf16[192,768]{1,0:T(8,128)(2,1)}, u32[]{:S(2)}, u32[]{:S(2)}) collective-permute-start(bf16[192,768]{1,0:T(8,128)(2,1)S(1)} %collective-permute-done.3), channel_id=1, source_target_pairs={{0,8},{4,12},{8,0},{12,4},{16,24},{20,28},{24,16},{28,20},{1,9},{5... | collective-permute-start | bytes 884744 | tf_op jit(solution)/shard_map/ppermute | solution.py:580
  30.4 9.4 %collective-permute-start.8 = (bf16[192,768]{1,0:T(8,128)(2,1)}, bf16[192,768]{1,0:T(8,128)(2,1)}, u32[]{:S(2)}, u32[]{:S(2)}) collective-permute-start(bf16[192,768]{1,0:T(8,128)(2,1)} %collective-permute-done.4), channel_id=1, source_target_pairs={{0,4},{4,0},{8,12},{12,8},{16,20},{20,16},{24,28},{28,24},{1,5},{5... | collective-permute-start | bytes 884744 | tf_op jit(solution)/shard_map/ppermute | solution.py:580
  31.9 10.5 %collective-permute-start.9 = (bf16[512,192]{1,0:T(8,128)(2,1)}, bf16[512,192]{1,0:T(8,128)(2,1)S(1)}, u32[]{:S(2)}, u32[]{:S(2)}) collective-permute-start(bf16[512,192]{1,0:T(8,128)(2,1)} %copy-done.33), channel_id=1, source_target_pairs={{0,2},{1,3},{2,0},{3,1},{4,6},{5,7},{6,4},{7,5},{8,10},{9,11},{10,... | collective-permute-start | bytes 589832 | tf_op jit(solution)/shard_map/ppermute | solution.py:580
  33.4 10.6 %collective-permute-start.10 = (bf16[512,192]{1,0:T(8,128)(2,1)S(1)}, bf16[512,192]{1,0:T(8,128)(2,1)S(1)}, u32[]{:S(2)}, u32[]{:S(2)}) collective-permute-start(bf16[512,192]{1,0:T(8,128)(2,1)S(1)} %get-tuple-element.139), channel_id=1, source_target_pairs={{0,3},{1,2},{2,1},{3,0},{4,7},{5,6},{6,5},{7,4},{8,11},{9,10},{10,... | collective-permute-start | bytes 589832 | tf_op jit(solution)/shard_map/ppermute | solution.py:580
  39.1 20.3 %copy-start.8 = (bf16[512,192]{1,0:T(8,128)(2,1)}, bf16[512,192]{1,0:T(8,128)(2,1)S(1)}, u32[]{:S(2)}) copy-start(bf16[512,192]{1,0:T(8,128)(2,1)S(1)} %get-tuple-element.127.c0.cb) | copy-start | bytes 589828
  39.1 7.2 %collective-permute-start.11 = (bf16[208,768]{1,0:T(8,128)(2,1)S(1)}, bf16[208,768]{1,0:T(8,128)(2,1)S(1)}, u32[]{:S(2)}, u32[]{:S(2)}) collective-permute-start(bf16[208,768]{1,0:T(8,128)(2,1)S(1)} %collective-permute-done.5.wo2), channel_id=1, source_target_pairs={{0,1},{1,0},{2,3},{3,2},{4,5},{5,4},{6,7},{7,6},{8,9},{9,8},{10,11... | collective-permute-start | bytes 958472 | tf_op jit(solution)/shard_map/ppermute | solution.py:580
  44.1 15.3 %copy-start.10 = (bf16[512,192]{1,0:T(8,128)(2,1)}, bf16[512,192]{1,0:T(8,128)(2,1)S(1)}, u32[]{:S(2)}) copy-start(bf16[512,192]{1,0:T(8,128)(2,1)S(1)} %collective-permute-done.10.c3.ca) | copy-start | bytes 589828
  44.1 16.0 %collective-permute-start.12 = (bf16[384,768]{1,0:T(8,128)(2,1)S(1)}, bf16[384,768]{1,0:T(8,128)(2,1)S(1)}, u32[]{:S(2)}, u32[]{:S(2)}) collective-permute-start(bf16[384,768]{1,0:T(8,128)(2,1)S(1)} %maximum_select_fusion.12), channel_id=1, source_target_pairs={{0,4},{4,0},{8,12},{12,8},{16,20},{20,16},{24,28},{28,24},{1,5},{5... | collective-permute-start | bytes 1769480 | tf_op jit(solution)/shard_map/ppermute | solution.py:580
  44.6 1.7 collective-permute-start.6
  45.1 16.6 %collective-permute-start.14 = (bf16[384,768]{1,0:T(8,128)(2,1)S(1)}, bf16[384,768]{1,0:T(8,128)(2,1)S(1)}, u32[]{:S(2)}, u32[]{:S(2)}) collective-permute-start(bf16[384,768]{1,0:T(8,128)(2,1)S(1)} %maximum_select_fusion.13), channel_id=1, source_target_pairs={{0,8},{4,12},{8,0},{12,4},{16,24},{20,28},{24,16},{28,20},{1,9},{5... | collective-permute-start | bytes 1769480 | tf_op jit(solution)/shard_map/ppermute | solution.py:580
  61.6 3.3 %collective-permute-start.13 = (bf16[768,768]{1,0:T(8,128)(2,1)}, bf16[768,768]{1,0:T(8,128)(2,1)}, u32[]{:S(2)}, u32[]{:S(2)}) collective-permute-start(bf16[768,768]{1,0:T(8,128)(2,1)} %maximum_select_fusion.6.wi2), channel_id=1, source_target_pairs={{0,1},{1,0},{2,3},{3,2},{4,5},{5,4},{6,7},{7,6},{8,9},{9,8},{10,11... | collective-permute-start | bytes 3538952 | tf_op jit(solution)/shard_map/ppermute | solution.py:580
  63.2 3.4 %collective-permute-start.15 = (bf16[768,768]{1,0:T(8,128)(2,1)}, bf16[768,768]{1,0:T(8,128)(2,1)}, u32[]{:S(2)}, u32[]{:S(2)}) collective-permute-start(bf16[768,768]{1,0:T(8,128)(2,1)} %maximum_select_fusion.7.wb2), channel_id=1, source_target_pairs={{0,1},{1,0},{2,3},{3,2},{4,5},{5,4},{6,7},{7,6},{8,9},{9,8},{10,11... | collective-permute-start | bytes 3538952 | tf_op jit(solution)/shard_map/ppermute | solution.py:580
  77.9 5.8 %collective-permute-start.18 = (bf16[1,8,1664]{2,1,0:T(8,128)(2,1)S(1)}, bf16[1,8,1664]{2,1,0:T(8,128)(2,1)S(1)}, u32[]{:S(2)}, u32[]{:S(2)}) collective-permute-start(bf16[1,8,1664]{2,1,0:T(8,128)(2,1)S(1)} %bitcast.71), channel_id=1, source_target_pairs={{0,24},{1,25},{2,26},{3,27},{4,28},{5,29},{6,30},{7,31},{8,16},{9,... | collective-permute-start | bytes 79880 | tf_op jit(solution)/shard_map/ppermute | solution.py:1065
  80.5 5.0 %collective-permute-start.17 = (bf16[1,8,1664]{2,1,0:T(8,128)(2,1)S(1)}, bf16[1,8,1664]{2,1,0:T(8,128)(2,1)S(1)}, u32[]{:S(2)}, u32[]{:S(2)}) collective-permute-start(bf16[1,8,1664]{2,1,0:T(8,128)(2,1)S(1)} %bitcast.72), channel_id=1, source_target_pairs={{0,16},{1,17},{2,18},{3,19},{4,20},{5,21},{6,22},{7,23},{8,24},{9,... | collective-permute-start | bytes 79880 | tf_op jit(solution)/shard_map/ppermute | solution.py:1065
  80.7 4.9 %collective-permute-start.16 = (bf16[1,8,1664]{2,1,0:T(8,128)(2,1)S(1)}, bf16[1,8,1664]{2,1,0:T(8,128)(2,1)S(1)}, u32[]{:S(2)}, u32[]{:S(2)}) collective-permute-start(bf16[1,8,1664]{2,1,0:T(8,128)(2,1)S(1)} %bitcast.73), channel_id=1, source_target_pairs={{0,8},{1,9},{2,10},{3,11},{4,12},{5,13},{6,14},{7,15},{8,0},{9,1},... | collective-permute-start | bytes 79880 | tf_op jit(solution)/shard_map/ppermute | solution.py:1065
  85.6 5.9 %collective-permute-start.21 = (bf16[4,8,1664]{2,1,0:T(8,128)(2,1)S(1)}, bf16[4,8,1664]{2,1,0:T(8,128)(2,1)S(1)}, u32[]{:S(2)}, u32[]{:S(2)}) collective-permute-start(bf16[4,8,1664]{2,1,0:T(8,128)(2,1)S(1)} %bitcast.96), channel_id=1, source_target_pairs={{0,6},{1,7},{2,4},{3,5},{4,2},{5,3},{6,0},{7,1},{8,14},{9,15},{10,... | collective-permute-start | bytes 319496 | tf_op jit(solution)/shard_map/ppermute | solution.py:1065
  87.7 4.7 %collective-permute-start.20 = (bf16[4,8,1664]{2,1,0:T(8,128)(2,1)S(1)}, bf16[4,8,1664]{2,1,0:T(8,128)(2,1)S(1)}, u32[]{:S(2)}, u32[]{:S(2)}) collective-permute-start(bf16[4,8,1664]{2,1,0:T(8,128)(2,1)S(1)} %bitcast.97), channel_id=1, source_target_pairs={{0,4},{1,5},{2,6},{3,7},{4,0},{5,1},{6,2},{7,3},{8,12},{9,13},{10,... | collective-permute-start | bytes 319496 | tf_op jit(solution)/shard_map/ppermute | solution.py:1065
  88.2 4.7 %collective-permute-start.19 = (bf16[4,8,1664]{2,1,0:T(8,128)(2,1)S(1)}, bf16[4,8,1664]{2,1,0:T(8,128)(2,1)S(1)}, u32[]{:S(2)}, u32[]{:S(2)}) collective-permute-start(bf16[4,8,1664]{2,1,0:T(8,128)(2,1)S(1)} %bitcast.98), channel_id=1, source_target_pairs={{0,2},{1,3},{2,0},{3,1},{4,6},{5,7},{6,4},{7,5},{8,10},{9,11},{10,... | collective-permute-start | bytes 319496 | tf_op jit(solution)/shard_map/ppermute | solution.py:1065
  93.1 1.8 collective-permute-start.22
  103.3 4.9 %collective-permute-start.23 = (bf16[2,768,768]{2,1,0:T(8,128)(2,1)}, bf16[2,768,768]{2,1,0:T(8,128)(2,1)}, u32[]{:S(2)}, u32[]{:S(2)}) collective-permute-start(bf16[2,768,768]{2,1,0:T(8,128)(2,1)} %get-tuple-element.163), channel_id=1, source_target_pairs={{0,1},{1,0},{2,3},{3,2},{4,5},{5,4},{6,7},{7,6},{8,9},{9,8},{10,11... | collective-permute-start | bytes 7077896 | tf_op jit(solution)/shard_map/ppermute | solution.py:580
  111.2 18.6 %copy-start.42 = (bf16[2,768,768]{2,1,0:T(8,128)(2,1)}, bf16[2,768,768]{2,1,0:T(8,128)(2,1)S(1)}, u32[]{:S(2)}) copy-start(bf16[2,768,768]{2,1,0:T(8,128)(2,1)S(1)} %add_convert_fusion) | copy-start | bytes 7077892
  111.3 20.0 %collective-permute-start.25 = (bf16[2,384,768]{2,1,0:T(8,128)(2,1)S(1)}, bf16[2,384,768]{2,1,0:T(8,128)(2,1)S(1)}, u32[]{:S(2)}, u32[]{:S(2)}) collective-permute-start(bf16[2,384,768]{2,1,0:T(8,128)(2,1)S(1)} %constant_dynamic-slice_fusion.7), channel_id=1, source_target_pairs={{0,4},{1,9},{2,6},{3,11},{4,0},{5,13},{6,2},{7,15},{8,12},{9,1},{1... | collective-permute-start | bytes 3538952 | tf_op jit(solution)/shard_map/ppermute | solution.py:635
  112.9 18.4 %collective-permute-start.26 = (bf16[512,768]{1,0:T(8,128)(2,1)S(1)}, bf16[512,768]{1,0:T(8,128)(2,1)S(1)}, u32[]{:S(2)}, u32[]{:S(2)}) collective-permute-start(bf16[512,768]{1,0:T(8,128)(2,1)S(1)} %get-tuple-element.174), channel_id=1, source_target_pairs={{0,2},{1,3},{2,0},{3,1},{4,6},{5,7},{6,4},{7,5},{8,10},{9,11},{10,... | collective-permute-start | bytes 2359304 | tf_op jit(solution)/shard_map/ppermute | solution.py:580
  113.6 17.7 %copy-start.4 = (bf16[512,768]{1,0:T(8,128)(2,1)S(1)}, bf16[512,768]{1,0:T(8,128)(2,1)}, u32[]{:S(2)}) copy-start(bf16[512,768]{1,0:T(8,128)(2,1)} %get-tuple-element.147.low1_ref) | copy-start | bytes 2359300
  113.6 17.7 %copy-start.11 = (bf16[512,192]{1,0:T(8,128)(2,1)S(1)}, bf16[512,192]{1,0:T(8,128)(2,1)}, u32[]{:S(2)}) copy-start(bf16[512,192]{1,0:T(8,128)(2,1)} %copy-done.10) | copy-start | bytes 589828
  113.6 17.7 %copy-start.13 = (bf16[512,192]{1,0:T(8,128)(2,1)S(1)}, bf16[512,192]{1,0:T(8,128)(2,1)}, u32[]{:S(2)}) copy-start(bf16[512,192]{1,0:T(8,128)(2,1)} %copy-done.12) | copy-start | bytes 589828
  129.9 9.3 %collective-permute-start.24 = (bf16[512,192]{1,0:T(8,128)(2,1)S(1)}, bf16[512,192]{1,0:T(8,128)(2,1)S(1)}, u32[]{:S(2)}, u32[]{:S(2)}) collective-permute-start(bf16[512,192]{1,0:T(8,128)(2,1)S(1)} %get-tuple-element.170), channel_id=1, source_target_pairs={{0,3},{1,2},{2,1},{3,0},{4,7},{5,6},{6,5},{7,4},{8,11},{9,10},{10,... | collective-permute-start | bytes 589832 | tf_op jit(solution)/shard_map/ppermute | solution.py:580
  139.2 10.5 %collective-permute-start.27 = (bf16[2,1024,768]{2,1,0:T(8,128)(2,1)}, bf16[2,1024,768]{2,1,0:T(8,128)(2,1)}, u32[]{:S(2)}, u32[]{:S(2)}) collective-permute-start(bf16[2,1024,768]{2,1,0:T(8,128)(2,1)} %weight_grads.2), channel_id=1, source_target_pairs={{0,1},{1,0},{2,3},{3,2},{4,5},{5,4},{6,7},{7,6},{8,9},{9,8},{10,11... | collective-permute-start | bytes 9437192 | tf_op jit(solution)/shard_map/ppermute | solution.py:580
  139.4 10.3 %collective-permute-start.29 = (bf16[2,512,768]{2,1,0:T(8,128)(2,1)}, bf16[2,512,768]{2,1,0:T(8,128)(2,1)}, u32[]{:S(2)}, u32[]{:S(2)}) collective-permute-start(bf16[2,512,768]{2,1,0:T(8,128)(2,1)} %maximum_select_fusion.2), channel_id=1, source_target_pairs={{0,1},{1,0},{2,3},{3,2},{4,5},{5,4},{6,7},{7,6},{8,9},{9,8},{10,11... | collective-permute-start | bytes 4718600 | tf_op jit(solution)/shard_map/ppermute | solution.py:580
  139.7 9.9 %collective-permute-start.28 = (bf16[512,192]{1,0:T(8,128)(2,1)S(1)}, bf16[512,192]{1,0:T(8,128)(2,1)S(1)}, u32[]{:S(2)}, u32[]{:S(2)}) collective-permute-start(bf16[512,192]{1,0:T(8,128)(2,1)S(1)} %copy-done.32), channel_id=1, source_target_pairs={{0,2},{1,3},{2,0},{3,1},{4,6},{5,7},{6,4},{7,5},{8,10},{9,11},{10,... | collective-permute-start | bytes 589832 | tf_op jit(solution)/shard_map/ppermute | solution.py:580
  153.1 36.4 %collective-permute-start.32 = (bf16[1024,768]{1,0:T(8,128)(2,1)}, bf16[1024,768]{1,0:T(8,128)(2,1)}, u32[]{:S(2)}, u32[]{:S(2)}) collective-permute-start(bf16[1024,768]{1,0:T(8,128)(2,1)} %fusion.1), channel_id=1, source_target_pairs={{0,2},{1,3},{2,0},{3,1},{4,6},{5,7},{6,4},{7,5},{8,10},{9,11},{10,... | collective-permute-start | bytes 4718600 | tf_op jit(solution)/shard_map/ppermute | solution.py:580
  155.2 10.1 %collective-permute-start.30 = (bf16[2,192,768]{2,1,0:T(8,128)(2,1)S(1)}, bf16[2,192,768]{2,1,0:T(8,128)(2,1)}, u32[]{:S(2)}, u32[]{:S(2)}) collective-permute-start(bf16[2,192,768]{2,1,0:T(8,128)(2,1)S(1)} %constant_dynamic-slice_fusion.6), channel_id=1, source_target_pairs={{0,8},{1,5},{2,10},{3,7},{4,12},{5,1},{6,14},{7,3},{8,0},{9,13},{1... | collective-permute-start | bytes 1769480 | tf_op jit(solution)/shard_map/ppermute | solution.py:635
  156.8 7.0 %collective-permute-start.31 = (bf16[512,192]{1,0:T(8,128)(2,1)S(1)}, bf16[512,192]{1,0:T(8,128)(2,1)S(1)}, u32[]{:S(2)}, u32[]{:S(2)}) collective-permute-start(bf16[512,192]{1,0:T(8,128)(2,1)S(1)} %copy-done.30), channel_id=1, source_target_pairs={{0,1},{1,0},{2,3},{3,2},{4,5},{5,4},{6,7},{7,6},{8,9},{9,8},{10,11... | collective-permute-start | bytes 589832 | tf_op jit(solution)/shard_map/ppermute | solution.py:580
  166.6 16.1 %collective-permute-start.33 = (bf16[2,96,768]{2,1,0:T(8,128)(2,1)S(1)}, bf16[2,96,768]{2,1,0:T(8,128)(2,1)S(1)}, u32[]{:S(2)}, u32[]{:S(2)}) collective-permute-start(bf16[2,96,768]{2,1,0:T(8,128)(2,1)S(1)} %constant_dynamic-slice_fusion.5), channel_id=1, source_target_pairs={{0,16},{1,17},{2,18},{3,19},{4,20},{5,21},{6,22},{7,23},{8,24},{9,... | collective-permute-start | bytes 884744 | tf_op jit(solution)/shard_map/ppermute | solution.py:635
  169.0 20.6 %copy-start.41 = (bf16[2,1024,768]{2,1,0:T(8,128)(2,1)S(1)}, bf16[2,1024,768]{2,1,0:T(8,128)(2,1)}, u32[]{:S(2)}) copy-start(bf16[2,1024,768]{2,1,0:T(8,128)(2,1)} %weight_grads.3) | copy-start | bytes 9437188
  189.5 15.5 %collective-permute-start.34 = (bf16[512,768]{1,0:T(8,128)(2,1)}, bf16[512,768]{1,0:T(8,128)(2,1)}, u32[]{:S(2)}, u32[]{:S(2)}) collective-permute-start(bf16[512,768]{1,0:T(8,128)(2,1)} %get-tuple-element.217), channel_id=1, source_target_pairs={{0,1},{1,0},{2,3},{3,2},{4,5},{5,4},{6,7},{7,6},{8,9},{9,8},{10,11... | collective-permute-start | bytes 2359304 | tf_op jit(solution)/shard_map/ppermute | solution.py:580
  194.1 12.3 %collective-permute-start.36 = (bf16[512,768]{1,0:T(8,128)(2,1)}, bf16[512,768]{1,0:T(8,128)(2,1)}, u32[]{:S(2)}, u32[]{:S(2)}) collective-permute-start(bf16[512,768]{1,0:T(8,128)(2,1)} %constant_dynamic-slice_fusion.4), channel_id=1, source_target_pairs={{0,4},{1,9},{2,6},{3,11},{4,0},{5,13},{6,2},{7,15},{8,12},{9,1},{1... | collective-permute-start | bytes 2359304 | tf_op jit(solution)/shard_map/ppermute | solution.py:635
  196.2 8.8 %collective-permute-start.35 = (bf16[96,768]{1,0:T(8,128)(2,1)S(1)}, bf16[96,768]{1,0:T(8,128)(2,1)S(1)}, u32[]{:S(2)}, u32[]{:S(2)}) collective-permute-start(bf16[96,768]{1,0:T(8,128)(2,1)S(1)} %slice_bitcast_fusion.1), channel_id=1, source_target_pairs={{0,2},{1,3},{2,0},{3,1},{4,6},{5,7},{6,4},{7,5},{8,10},{9,11},{10,... | collective-permute-start | bytes 442376 | tf_op jit(solution)/shard_map/ppermute | solution.py:580
  205.0 28.1 %collective-permute-start.38 = (bf16[512,768]{1,0:T(8,128)(2,1)S(1)}, bf16[512,768]{1,0:T(8,128)(2,1)}, u32[]{:S(2)}, u32[]{:S(2)}) collective-permute-start(bf16[512,768]{1,0:T(8,128)(2,1)S(1)} %get-tuple-element.223), channel_id=1, source_target_pairs={{0,1},{1,0},{2,3},{3,2},{4,5},{5,4},{6,7},{7,6},{8,9},{9,8},{10,11... | collective-permute-start | bytes 2359304 | tf_op jit(solution)/shard_map/ppermute | solution.py:580
  208.6 24.6 %collective-permute-start.39 = (bf16[512,768]{1,0:T(8,128)(2,1)}, bf16[512,768]{1,0:T(8,128)(2,1)}, u32[]{:S(2)}, u32[]{:S(2)}) collective-permute-start(bf16[512,768]{1,0:T(8,128)(2,1)} %add_convert_fusion.5), channel_id=1, source_target_pairs={{0,2},{1,3},{2,0},{3,1},{4,6},{5,7},{6,4},{7,5},{8,10},{9,11},{10,... | collective-permute-start | bytes 2359304 | tf_op jit(solution)/shard_map/ppermute | solution.py:580
  211.8 18.2 %collective-permute-start.46 = (bf16[256,768]{1,0:T(8,128)(2,1)}, bf16[256,768]{1,0:T(8,128)(2,1)}, u32[]{:S(2)}, u32[]{:S(2)}) collective-permute-start(bf16[256,768]{1,0:T(8,128)(2,1)} %constant_dynamic-slice_fusion.1), channel_id=1, source_target_pairs={{0,8},{1,5},{2,10},{3,7},{4,12},{5,1},{6,14},{7,3},{8,0},{9,13},{1... | collective-permute-start | bytes 1179656 | tf_op jit(solution)/shard_map/ppermute | solution.py:635
  213.7 19.5 %copy-start.46 = (f32[512,768]{1,0:T(8,128)S(1)}, f32[512,768]{1,0:T(8,128)}, u32[]{:S(2)}) copy-start(f32[512,768]{1,0:T(8,128)} %get-tuple-element.193) | copy-start | bytes 4718596
  214.9 18.3 %collective-permute-start.37 = (bf16[320,768]{1,0:T(8,128)(2,1)S(1)}, bf16[320,768]{1,0:T(8,128)(2,1)S(1)}, u32[]{:S(2)}, u32[]{:S(2)}) collective-permute-start(bf16[320,768]{1,0:T(8,128)(2,1)S(1)} %constant_dynamic-slice_fusion.3), channel_id=1, source_target_pairs={{0,4},{1,9},{2,6},{3,11},{4,0},{5,13},{6,2},{7,15},{8,12},{9,1},{1... | collective-permute-start | bytes 1474568 | tf_op jit(solution)/shard_map/ppermute | solution.py:635
  216.5 14.7 %collective-permute-start.50 = (bf16[96,768]{1,0:T(8,128)(2,1)S(1)}, bf16[96,768]{1,0:T(8,128)(2,1)S(1)}, u32[]{:S(2)}, u32[]{:S(2)}) collective-permute-start(bf16[96,768]{1,0:T(8,128)(2,1)S(1)} %fusion.3), channel_id=1, source_target_pairs={{0,16},{1,17},{2,18},{3,19},{4,20},{5,21},{6,22},{7,23},{8,24},{9,... | collective-permute-start | bytes 442376 | tf_op jit(solution)/shard_map/ppermute | solution.py:635
  231.1 12.0 %collective-permute-start.47 = (bf16[256,768]{1,0:T(8,128)(2,1)S(1)}, bf16[256,768]{1,0:T(8,128)(2,1)S(1)}, u32[]{:S(2)}, u32[]{:S(2)}) collective-permute-start(bf16[256,768]{1,0:T(8,128)(2,1)S(1)} %add_convert_fusion.9), channel_id=1, source_target_pairs={{0,16},{1,17},{2,18},{3,19},{4,20},{5,21},{6,22},{7,23},{8,24},{9,... | collective-permute-start | bytes 1179656 | tf_op jit(solution)/shard_map/ppermute | solution.py:635
  231.2 14.3 %collective-permute-start.51 = (bf16[192,768]{1,0:T(8,128)(2,1)S(1)}, bf16[192,768]{1,0:T(8,128)(2,1)S(1)}, u32[]{:S(2)}, u32[]{:S(2)}) collective-permute-start(bf16[192,768]{1,0:T(8,128)(2,1)S(1)} %maximum_select_fusion.17), channel_id=1, source_target_pairs={{0,8},{1,5},{2,10},{3,7},{4,12},{5,1},{6,14},{7,3},{8,0},{9,13},{1... | collective-permute-start | bytes 884744 | tf_op jit(solution)/shard_map/ppermute | solution.py:635
  235.1 25.5 %collective-permute-start.41 = (bf16[512,768]{1,0:T(8,128)(2,1)S(1)}, bf16[512,768]{1,0:T(8,128)(2,1)S(1)}, u32[]{:S(2)}, u32[]{:S(2)}) collective-permute-start(bf16[512,768]{1,0:T(8,128)(2,1)S(1)} %add_convert_fusion.4), channel_id=1, source_target_pairs={{0,2},{1,3},{2,0},{3,1},{4,6},{5,7},{6,4},{7,5},{8,10},{9,11},{10,... | collective-permute-start | bytes 2359304 | tf_op jit(solution)/shard_map/ppermute | solution.py:580
  243.1 12.1 %collective-permute-start.48 = (bf16[256,768]{1,0:T(8,128)(2,1)S(1)}, bf16[256,768]{1,0:T(8,128)(2,1)S(1)}, u32[]{:S(2)}, u32[]{:S(2)}) collective-permute-start(bf16[256,768]{1,0:T(8,128)(2,1)S(1)} %add_convert_fusion.8), channel_id=1, source_target_pairs={{0,8},{1,5},{2,10},{3,7},{4,12},{5,1},{6,14},{7,3},{8,0},{9,13},{1... | collective-permute-start | bytes 1179656 | tf_op jit(solution)/shard_map/ppermute | solution.py:635
  243.4 17.1 %collective-permute-start.40 = (bf16[160,768]{1,0:T(8,128)(2,1)S(1)}, bf16[160,768]{1,0:T(8,128)(2,1)S(1)}, u32[]{:S(2)}, u32[]{:S(2)}) collective-permute-start(bf16[160,768]{1,0:T(8,128)(2,1)S(1)} %constant_dynamic-slice_fusion.2), channel_id=1, source_target_pairs={{0,8},{1,5},{2,10},{3,7},{4,12},{5,1},{6,14},{7,3},{8,0},{9,13},{1... | collective-permute-start | bytes 737288 | tf_op jit(solution)/shard_map/ppermute | solution.py:635
  245.7 20.7 %collective-permute-start.52 = (bf16[384,768]{1,0:T(8,128)(2,1)S(1)}, bf16[384,768]{1,0:T(8,128)(2,1)S(1)}, u32[]{:S(2)}, u32[]{:S(2)}) collective-permute-start(bf16[384,768]{1,0:T(8,128)(2,1)S(1)} %maximum_select_fusion.14), channel_id=1, source_target_pairs={{0,4},{1,9},{2,6},{3,11},{4,0},{5,13},{6,2},{7,15},{8,12},{9,1},{1... | collective-permute-start | bytes 1769480 | tf_op jit(solution)/shard_map/ppermute | solution.py:635
  255.6 14.0 %collective-permute-start.49 = (bf16[512,768]{1,0:T(8,128)(2,1)S(1)}, bf16[512,768]{1,0:T(8,128)(2,1)S(1)}, u32[]{:S(2)}, u32[]{:S(2)}) collective-permute-start(bf16[512,768]{1,0:T(8,128)(2,1)S(1)} %maximum_select_fusion.11), channel_id=1, source_target_pairs={{0,4},{1,9},{2,6},{3,11},{4,0},{5,13},{6,2},{7,15},{8,12},{9,1},{1... | collective-permute-start | bytes 2359304 | tf_op jit(solution)/shard_map/ppermute | solution.py:635
  260.8 21.9 %collective-permute-start.43 = (bf16[2,512,768]{2,1,0:T(8,128)(2,1)S(1)}, bf16[2,512,768]{2,1,0:T(8,128)(2,1)S(1)}, u32[]{:S(2)}, u32[]{:S(2)}) collective-permute-start(bf16[2,512,768]{2,1,0:T(8,128)(2,1)S(1)} %maximum_select_fusion.4), channel_id=1, source_target_pairs={{0,1},{1,0},{2,3},{3,2},{4,5},{5,4},{6,7},{7,6},{8,9},{9,8},{10,11... | collective-permute-start | bytes 4718600 | tf_op jit(solution)/shard_map/ppermute | solution.py:580
  268.1 14.6 %collective-permute-start.42 = (bf16[160,768]{1,0:T(8,128)(2,1)S(1)}, bf16[160,768]{1,0:T(8,128)(2,1)S(1)}, u32[]{:S(2)}, u32[]{:S(2)}) collective-permute-start(bf16[160,768]{1,0:T(8,128)(2,1)S(1)} %add_convert_fusion.12), channel_id=1, source_target_pairs={{0,16},{1,17},{2,18},{3,19},{4,20},{5,21},{6,22},{7,23},{8,24},{9,... | collective-permute-start | bytes 737288 | tf_op jit(solution)/shard_map/ppermute | solution.py:635
  282.7 6.3 %collective-permute-start.44 = (bf16[160,768]{1,0:T(8,128)(2,1)S(1)}, bf16[160,768]{1,0:T(8,128)(2,1)S(1)}, u32[]{:S(2)}, u32[]{:S(2)}) collective-permute-start(bf16[160,768]{1,0:T(8,128)(2,1)S(1)} %add_convert_fusion.11), channel_id=1, source_target_pairs={{0,8},{1,5},{2,10},{3,7},{4,12},{5,1},{6,14},{7,3},{8,0},{9,13},{1... | collective-permute-start | bytes 737288 | tf_op jit(solution)/shard_map/ppermute | solution.py:635
  289.1 8.9 %collective-permute-start.45 = (bf16[320,768]{1,0:T(8,128)(2,1)S(1)}, bf16[320,768]{1,0:T(8,128)(2,1)S(1)}, u32[]{:S(2)}, u32[]{:S(2)}) collective-permute-start(bf16[320,768]{1,0:T(8,128)(2,1)S(1)} %maximum_select_fusion.15), channel_id=1, source_target_pairs={{0,4},{1,9},{2,6},{3,11},{4,0},{5,13},{6,2},{7,15},{8,12},{9,1},{1... | collective-permute-start | bytes 1474568 | tf_op jit(solution)/shard_map/ppermute | solution.py:635
  (41 other events, 222.6 us)

commit v4 on v3

--- a/solution.py
+++ b/solution.py
@@ -89,8 +89,8 @@
     return pieces
 
 
-def attend_forward(m_ref, tok_ref, w_ref, b_ref, seg_ref, win_ref, qkv_ref, prob_ref, *refs):
-    ctx_refs, ctx_v = refs[:-1], refs[-1]
+def attend_forward(held, m_ref, tok_ref, w_ref, b_ref, seg_ref, win_ref, *refs):
+    qkv_ref, prob_ref, *ctx_refs, ctx_v = refs[held:]
     length = tok_ref.shape[0]
     width = w_ref.shape[1]
     heads = width // HEAD_DIM
@@ -299,7 +299,7 @@
         center = values - jnp.mean(values, axis=-1, keepdims=True)
         rate = lax.rsqrt(jnp.mean(center * center, axis=-1, keepdims=True) + norm_eps)
         xhat = center * rate
-        xhat1_ref[rows, :] = xhat
+        xhat1_ref[rows, :] = xhat.astype(bf16)
         rstd1_ref[rows, :] = jnp.broadcast_to(rate, (ROW_TILE, LANES))
         normed = xhat * gain1 + shift1
         total_ref[rows, :] = normed
@@ -360,7 +360,7 @@
         center = values - jnp.mean(values, axis=-1, keepdims=True)
         rate = lax.rsqrt(jnp.mean(center * center, axis=-1, keepdims=True) + norm_eps)
         xhat = center * rate
-        xhat2_ref[rows, :] = xhat
+        xhat2_ref[rows, :] = xhat.astype(bf16)
         rstd2_ref[rows, :] = jnp.broadcast_to(rate, (ROW_TILE, LANES))
         out_ref[rows, :] = (xhat * gain2 + shift2).astype(bf16)
 
@@ -445,7 +445,7 @@
 
 def back_second(
     gp_ref, seg_ref, xhat_ref, rstd_ref, gain_ref, act01_hbm, act23_hbm,
-    low_ref, grad_ref, vec_ref, d_ref,
+    low_ref, vec_ref, d_ref,
     out_v, act_v, sums, sems,
 ):
     length, width = xhat_ref.shape
@@ -460,7 +460,7 @@
     @pl.loop(0, length // ROW_TILE)
     def _(i):
         rows = pl.ds(pl.multiple_of(i * ROW_TILE, ROW_TILE), ROW_TILE)
-        grad_out, xhat = out_v[rows, :], xhat_ref[rows, :]
+        grad_out, xhat = out_v[rows, :], xhat_ref[rows, :].astype(f32)
         sums[0] += column_total(grad_out * xhat)
         sums[1] += column_total(grad_out)
         grad = grad_out * gain
@@ -468,7 +468,6 @@
         second = jnp.mean(grad * xhat, axis=-1, keepdims=True)
         grad = (grad - first - xhat * second) * rstd_ref[rows, 0:1]
         sums[2] += column_total(grad)
-        grad_ref[rows, :] = grad
         low_ref[rows, :] = grad.astype(bf16)
 
     vec_ref[...] = jnp.zeros_like(vec_ref)
@@ -491,9 +490,9 @@
 
 
 def back_first(
-    low_ref, resid_ref, xhat_ref, rstd_ref, gain_ref, slope01_hbm, slope23_hbm,
+    low_ref, xhat_ref, rstd_ref, gain_ref, slope01_hbm, slope23_hbm,
     wo0, wo1, wo2, wo3, wi0, wi1, wi2, wi3, wb0, wb1, wb2, wb3,
-    gb_hbm, grad_ref, attn_ref, vec_ref, bin_ref, x0, x1, x2, x3,
+    gb_hbm, attn_ref, vec_ref, bin_ref, x0, x1, x2, x3,
     slope_v, wo_v, wi_v, wb_v, gb_v, total_v, sums, sems, out_sems,
 ):
     length, width = xhat_ref.shape
@@ -520,7 +519,7 @@
         copy.wait()
     for first in range(0, width, TILE):
         cols = slice(first, first + TILE)
-        total = resid_ref[:, cols]
+        total = low_ref[:, cols].astype(f32)
         for r in range(4):
             total = total + product_nt(gb_v[r], wi_v[r, cols, :])
         total_v[:, cols] = total
@@ -529,7 +528,7 @@
     @pl.loop(0, length // ROW_TILE)
     def _(i):
         rows = pl.ds(pl.multiple_of(i * ROW_TILE, ROW_TILE), ROW_TILE)
-        grad_out, xhat = total_v[rows, :], xhat_ref[rows, :]
+        grad_out, xhat = total_v[rows, :], xhat_ref[rows, :].astype(f32)
         sums[0] += column_total(grad_out * xhat)
         sums[1] += column_total(grad_out)
         grad = grad_out * gain
@@ -537,7 +536,6 @@
         second = jnp.mean(grad * xhat, axis=-1, keepdims=True)
         grad = (grad - first - xhat * second) * rstd_ref[rows, 0:1]
         sums[2] += column_total(grad)
-        grad_ref[rows, :] = grad
         attn_ref[rows, :] = grad.astype(bf16)
 
     vec_ref[...] = jnp.zeros_like(vec_ref)
@@ -740,9 +738,9 @@
     )
     seg_rows = segment_ids[:, None, :]
 
-    def attend(count, source):
+    def attend(count, source, place, held):
         return pl.pallas_call(
-            attend_forward,
+            functools.partial(attend_forward, len(held)),
             grid_spec=pltpu.PrefetchScalarGridSpec(
                 num_scalar_prefetch=1,
                 grid=(count,),
@@ -752,29 +750,33 @@
                     pl.BlockSpec(b_qv.shape, lambda i, m: (0, 0)),
                     pl.BlockSpec((1, 1, length), lambda i, m: (source(i) ^ m[0], 0, 0)),
                     pl.BlockSpec((1, blocks, K_WINDOW), lambda i, m: (source(i) ^ m[0], 0, 0)),
-                ],
+                ]
+                + [any_spec] * len(held),
                 out_specs=[
-                    pl.BlockSpec((1, 3, length, local), lambda i, m: (i, 0, 0, 0)),
-                    pl.BlockSpec((1, heads * blocks, Q_BLOCK, K_WINDOW), lambda i, m: (i, 0, 0, 0)),
+                    pl.BlockSpec((1, 3, length, local), lambda i, m: (place + i, 0, 0, 0)),
+                    pl.BlockSpec(
+                        (1, heads * blocks, Q_BLOCK, K_WINDOW), lambda i, m: (place + i, 0, 0, 0)
+                    ),
                 ]
                 + [pl.BlockSpec((length, local), lambda i, m: (0, 0))] * count,
                 scratch_shapes=[pltpu.VMEM((length, local), bf16)],
             ),
             out_shape=[
-                shape((count, 3, length, local)),
-                shape((count, heads * blocks, Q_BLOCK, K_WINDOW)),
+                shape((row_count, 3, length, local)),
+                shape((row_count, heads * blocks, Q_BLOCK, K_WINDOW)),
                 *[shape((length, local))] * count,
             ],
+            input_output_aliases={6 + i: i for i in range(len(held))},
             name="attend_forward",
             **params(cost(6 * count * length * width * local, 2e6 * count, count * heads * length * K_WINDOW)),
-        )(m_arr, tokens, w_t, b_qv, seg_rows, windows)
-
-    qkv_away, probs_away, ctx3, ctx2, ctx1 = attend(3, lambda i: 3 - i)
+        )(m_arr, tokens, w_t, b_qv, seg_rows, windows, *held)
+
+    qkv, probs, ctx3, ctx2, ctx1 = attend(3, lambda i: 3 - i, 0, ())
     ctx3, ctx2, ctx1, in_quarter, back_quarter, far_out = together(
         ctx3, ctx2, ctx1, in_quarter, back_quarter, far_out
     )
     in_got, back_got = hop(in_quarter, "dp", 2), hop(back_quarter, "dp", 1)
-    qkv_own, probs_own, ctx0 = attend(1, lambda i: 0)
+    qkv, probs, ctx0 = attend(1, lambda i: 0, 3, (qkv, probs))
     out_parts = [out_pack, near_out, far_out, hop(late(far_out, ctx0), "mp", 1)]
     ctx_got2, ctx_got3 = hop(ctx2, "mp", 2), hop(ctx3, "mp", 3)
     in_half = ordered(bit_z, in_quarter, late(in_got, ctx0), 0)
@@ -793,7 +795,7 @@
         out_specs=[any_spec] * 2 + [vmem_spec] * 4,
         out_shape=[
             shape((2, length, units)), shape((2, length, units)),
-            shape((length, width), f32), shape((length, LANES), f32), shape((length, width)),
+            shape((length, width)), shape((length, LANES), f32), shape((length, width)),
             shape((length, width), f32),
         ],
         scratch_shapes=[
@@ -818,7 +820,7 @@
         out_specs=[any_spec] * 2 + [vmem_spec] * 6,
         out_shape=[
             shape((2, length, units)), shape((2, length, units)),
-            shape((length, width), f32), shape((length, LANES), f32), shape((length, width)),
+            shape((length, width)), shape((length, LANES), f32), shape((length, width)),
             shape((16, width), f32), shape((16, LANES), f32), shape((8, 2 * width + LANES)),
         ],
         scratch_shapes=[
@@ -854,12 +856,12 @@
     )(own_row.astype(jnp.int32).reshape(1), everyone, msg, pooled, lengths)
 
     rows = Rows()
-    grad_low2, grad_resid2, vec2, back_send = pl.pallas_call(
+    grad_low2, vec2, back_send = pl.pallas_call(
         back_second,
         in_specs=[vmem_spec] * 5 + [any_spec] * 2,
-        out_specs=[vmem_spec] * 4,
+        out_specs=[vmem_spec] * 3,
         out_shape=[
-            shape((length, width)), shape((length, width), f32), shape((8, width), f32),
+            shape((length, width)), shape((8, width), f32),
             shape((2, units, width)),
         ],
         scratch_shapes=[
@@ -884,12 +886,12 @@
     back_got = rows.send(back_sum, 0)
     out_far = hop(late(out_own, grad_low2), "mp", 2)
 
-    gb, grad_resid1, attn_low, vec1, d_bin, *ctx_grads = pl.pallas_call(
+    gb, attn_low, vec1, d_bin, *ctx_grads = pl.pallas_call(
         back_first,
-        in_specs=[vmem_spec] * 5 + [any_spec] * 14,
-        out_specs=[any_spec] + [vmem_spec] * 8,
+        in_specs=[vmem_spec] * 4 + [any_spec] * 14,
+        out_specs=[any_spec] + [vmem_spec] * 7,
         out_shape=[
-            shape((4, length, units)), shape((length, width), f32), shape((length, width)),
+            shape((4, length, units)), shape((length, width)),
             shape((8, width), f32), shape((4, units), f32), *[shape((length, local))] * 4,
         ],
         scratch_shapes=[
@@ -901,7 +903,7 @@
         name="back_first",
         **params(cost(2 * length * width * (width + 8 * units), 25e6)),
     )(
-        grad_low2, grad_resid2, xhat1, rstd1, tall(norm1_gain), slope01, slope23, *out_parts, *in_parts, *back_parts,
+        grad_low2, xhat1, rstd1, tall(norm1_gain), slope01, slope23, *out_parts, *in_parts, *back_parts,
     )
 
     attn_low, back_got, out_far = together(attn_low, back_got, out_far)
@@ -925,17 +927,19 @@
     out_other = hop(out_pair, "mp", 1)
     first_got = hop(first_send, "mp", 1)
     got2 = hop(late(ctx_grads[2], first_send), "mp", 2)
+    back_sum = late(back_sum, first_send)
+    back_got = rows.send(back_sum, 1)
     first_keep = first_grads((2, 0), attn_low)
-    own_grad, first_keep, first_got, got2, back_sum, out_other = together(
-        ctx_grads[0], first_keep, first_got, got2, back_sum, out_other
-    )
+    own_grad, first_keep, first_got, got2, back_got, out_other = together(
+        ctx_grads[0], first_keep, first_got, got2, back_got, out_other
+    )
+    back_sum = rows.keep(back_sum, back_got, 1)
     first_far = hop(add_low(first_keep[0], first_got[0]), "mp", 2)
-    back_got = rows.send(back_sum, 1)
+    back_got = rows.send(back_sum, 2)
     got1 = hop(late(ctx_grads[1], own_grad), "mp", 1)
 
-    def attend_back(count, source, first, qkv, probs, grads, sums):
+    def attend_back(count, source, place, last, grads, sums):
         same = lambda i, m: (0, 0)
-        last = source(0) == 1
         out_specs = [pl.BlockSpec((length, width), same)] * count
         out_shape = [shape((length, width))] * count
         if last:
@@ -952,9 +956,9 @@
                 in_specs=[
                     pl.BlockSpec((length, width), lambda i, m: (source(i) ^ m[0], 0)),
                     pl.BlockSpec(w_t.shape, lambda i, m: (0, 0, 0)),
-                    pl.BlockSpec((1, 3, length, local), lambda i, m: (first + i, 0, 0, 0)),
+                    pl.BlockSpec((1, 3, length, local), lambda i, m: ((place + i) % row_count, 0, 0, 0)),
                     pl.BlockSpec(
-                        (1, heads * blocks, Q_BLOCK, K_WINDOW), lambda i, m: (first + i, 0, 0, 0)
+                        (1, heads * blocks, Q_BLOCK, K_WINDOW), lambda i, m: ((place + i) % row_count, 0, 0, 0)
                     ),
                 ]
                 + [pl.BlockSpec((length, local), same)] * count
@@ -971,48 +975,44 @@
             **params(cost(12 * count * length * width * local, 4e6 * count)),
         )(m_arr, tokens, w_t, qkv, probs, *grads, *sums)
 
-    back0, *sums = attend_back(1, lambda i: 0, 0, qkv_own, probs_own, [own_grad], [])
-    back_got, got1, *sums = together(back_got, got1, *sums)
-    back_sum = rows.keep(back_sum, back_got, 1)
-    back_got = rows.send(back_sum, 2)
-    back3, back2, *sums = attend_back(2, lambda i: 3 - i, 0, qkv_away, probs_away, [got3, got2], sums)
-    back_got, *sums = together(back_got, *sums)
+    back0, back3, *sums = attend_back(2, lambda i: 3 * i, 3, False, [own_grad, got3], [])
+    back_got, got1, back3, *sums = together(back_got, got1, back3, *sums)
     back_sum = rows.keep(back_sum, back_got, 2)
     for step in range(3, rows.steps):
         back_sum = rows.keep(back_sum, rows.send(back_sum, step), step)
     back_got = hop(back_sum[0], "mp", 2)
-    first_far, first_keep, first_got, back3, *sums = together(
-        first_far, first_keep, first_got, back3, *sums
-    )
+    tok_got3 = hop(back3, "mp", 1)
+    back2, back1, d_qkv = attend_back(2, lambda i: 2 - i, 1, True, [got2, got1], sums)
+    first_far, first_keep, first_got, back_got, _ = together(
+        first_far, first_keep, first_got, back_got, d_qkv
+    )
+    back_sum = add_low(back_sum[1], back_got)
     first_sum = (first_keep[1].astype(f32) + first_got[1].astype(f32) + first_far.astype(f32)).astype(bf16)
-    first_got = rows.send(first_sum, 0)
-    tok_got3 = hop(back3, "mp", 1)
-    back1, d_qkv = attend_back(1, lambda i: 1, 2, qkv_away, probs_away, [got1], sums)
     last = rows.steps - 1
-    d_qkv, tok_got3, back_got, first_got = together(d_qkv, tok_got3, back_got, first_got)
-    back_sum = add_low(back_sum[1], back_got)
-    first_sum = rows.keep(first_sum, first_got, 0)
     tok_got1 = hop(back1, "mp", 1)
     far = add_low(back2, tok_got3)
     down = [("send", step) for step in range(last)] + [("full", last)]
     up = [("join", step) for step in reversed(range(last))]
     sums = [
-        Running(rows, first_sum, down[1:] + up),
+        Running(rows, first_sum, down + up),
         Running(rows, d_qkv, down + up),
         Running(rows, back_sum, [("join", last)] + up),
     ]
     stage, extra = 0, [tok_got1, hop(far, "mp", 2)]
     while any(part.plan for part in sums):
-        parts = [part for part in sums if part.plan]
+        parts = [part for part in sums if part.plan and not (part is sums[2] and stage == 1)]
+        if stage == 2:
+            sums[2].array = late(sums[2].array, sums[0].array)
+        if stage == 2:
+            sums[1].array = late(sums[1].array, sums[0].array)
         starts = [part.start() for part in parts]
-        if extra:
-            tied = list(together(starts[1], *extra))
-            starts[1] = tied.pop(0)
-        hops = starts + (tied if extra else [])
+        if stage == 0:
+            starts[2], *extra = together(starts[2], *extra)
+        hops = starts + extra
         for part in parts:
             part.finish(hops.pop(0))
         if stage == 0:
-            own = back0.astype(f32) + grad_resid1 + hops[0].astype(f32) + hops[1].astype(f32)
+            own = back0.astype(f32) + attn_low.astype(f32) + hops[0].astype(f32) + hops[1].astype(f32)
             own = own.astype(bf16)
             extra = [hop(own, "mp", 2)]
         elif stage == 1:

time: 307 us -> 290 us (0.945)
  the two profiles are of different devices: /device:TPU:0 before, /device:TPU:1 now
where the time goes in v4:
time: 290 us; the launch traced here: 284 us
  Pallas kernels  106 us (37%)
  waiting for transfers between devices  77.1 us (27%)
  starting transfers between devices  46.8 us (16%)
  other arithmetic  35.1 us (12%)
  local copies, waits for them, and re-layouts  17 us (6%)
    ppermute x16, waiting for transfers between devices, swap(): return lax.ppermute(values, ('dp', 'mp'), pairs)  47.6 us
    ppermute x31, starting transfers between devices, hop(): return lax.ppermute(array, axis, [(i, i ^ flip) for i in range(size)])  26 us
    pallas_call x2, Pallas kernels, attend_back(): pl.pallas_call(functools.partial(attend_backward, count, len(sums) == 0,...  25.5 us
    ppermute x31, waiting for transfers between devices, hop(): return lax.ppermute(array, axis, [(i, i ^ flip) for i in range(size)])  22.3 us
    pallas_call x2, Pallas kernels, attend(): pl.pallas_call(functools.partial(attend_forward, len(held)), grid_spec=pl...  17.8 us
    pallas_call x1, Pallas kernels, shards(): pl.pallas_call(back_first, in_specs=[vmem_spec] * 4 + [any_spec] * 14, ou...  14.9 us
    ppermute x16, starting transfers between devices, swap(): return lax.ppermute(values, ('dp', 'mp'), pairs)  14.6 us
    convert_element_type x13, other arithmetic, add_low(): return (left_side.astype(f32) + right_side.astype(f32)).astype(bf16)  12.5 us
  transfers between devices with their start and end apart: 53, of which 27 were waited for; matrix products, arithmetic and copies ran while one was open for 12% of the time, Pallas kernels for 31%

profile of v4, /device:TPU:1, one launch (start us, length us, event | category | flops | bytes accessed | tf_op | source)
XLA Modules:
  0.0 283.9 jit_solution(394966628771910439)
XLA Ops:
  3.0 1.6 prepare.1
  4.7 2.7 collective-permute-start.5
  7.4 1.4 collective-permute-start.4
  9.1 12.6 %attend_forward.2 = (bf16[4,3,512,192]{3,2,1,0:T(8,128)(2,1)}, bf16[4,12,128,256]{3,2,1,0:T(8,128)(2,1)}, bf16[512,192]{1,0:T(8,128)(2,1)S(1)}, bf16[512,192]{1,0:T(8,128)(2,1)}, bf16[512,192]{1,0:T(8,128)(2,1)S(1)}) custom-call(s32[1]{0:T(128)} %bitcast.5.m_ref, bf16[2048,768]{1,0:T(8,128)(2,1)} %tok_ref.7, bf16[3,192,768]{2,1,0:T(8,128)(2,1)S(1)} %bitcast.66, ...), custom_call_target="tpu_custom_call" | custom-call | flops 1358954496 | bytes 6000000 | tf_op jit(solution)/shard_map/attend_forward/pallas_call | solution.py:742
  22.4 5.6 %collective-permute-done.4 = bf16[192,768]{1,0:T(8,128)(2,1)} collective-permute-done((bf16[192,768]{1,0:T(8,128)(2,1)S(1)}, bf16[192,768]{1,0:T(8,128)(2,1)}, u32[]{:S(2)}, u32[]{:S(2)}) %collective-permute-start.4) | collective-permute-done | bytes 294944 | tf_op jit(solution)/shard_map/ppermute | solution.py:578
  28.0 1.3 collective-permute-start.7
  31.8 1.8 collective-permute-start.10
  33.6 5.3 %attend_forward.3 = (bf16[4,3,512,192]{3,2,1,0:T(8,128)(2,1)}, bf16[4,12,128,256]{3,2,1,0:T(8,128)(2,1)}, bf16[512,192]{1,0:T(8,128)(2,1)S(1)}) custom-call(s32[1]{0:T(128)} %bitcast.5.m_ref, bf16[2048,768]{1,0:T(8,128)(2,1)} %tok_ref.7, bf16[3,192,768]{2,1,0:T(8,128)(2,1)S(1)} %bitcast.67, ...), custom_call_target="tpu_custom_call", output_to_operand_aliasing={{0}: (6, {}), {1}: (7, {})} | custom-call | flops 452984832 | bytes 2000000 | tf_op jit(solution)/shard_map/attend_forward/pallas_call | solution.py:742
  39.0 1.2 maximum_select_fusion.12
  40.2 1.4 maximum_select_fusion.13
  41.6 2.8 collective-permute-done.10.c3.ca
  44.8 1.4 collective-permute-done.6.c1.cb
  46.9 12.0 %middle_first.1 = (bf16[2,512,768]{2,1,0:T(8,128)(2,1)}, bf16[2,512,768]{2,1,0:T(8,128)(2,1)}, bf16[512,768]{1,0:T(8,128)(2,1)}, f32[512,128]{1,0:T(8,128)S(1)},...) custom-call(s32[1]{0:T(128)} %bitcast.5.m_ref, bf16[2048,768]{1,0:T(8,128)(2,1)} %tok_ref.7, f32[6,128]{1,0:T(8,128)S(1)} %bitcast.74, ...), custom_call_target="tpu_custom_call" | custom-call | flops 3019898880 | bytes 18000000 | tf_op jit(solution)/shard_map/middle_first/pallas_call | solution.py:792
  59.6 1.5 maximum_select_fusion.6.wi2
  61.7 1.5 maximum_select_fusion.7.wb2
  64.5 1.9 collective-permute-done.15.wb3
  66.4 11.1 %middle_second.1 = (bf16[2,512,768]{2,1,0:T(8,128)(2,1)}, bf16[2,512,768]{2,1,0:T(8,128)(2,1)}, bf16[512,768]{1,0:T(8,128)(2,1)S(1)}, f32[512,128]{1,0:T(8,128)S...) custom-call(s32[1,512]{1,0:T(1,128)S(1)} %constant_dynamic-slice_fus, ...), custom_call_target="tpu_custom_call" | custom-call | flops 2415919104 | bytes 12000000 | tf_op jit(solution)/shard_map/middle_second/pallas_call | solution.py:817
  79.2 2.3 collective-permute-start.18
  83.7 1.7 collective-permute-done.17
  85.4 2.0 collective-permute-start.21
  88.1 1.8 collective-permute-done.21
  89.9 1.5 collective-permute-done.20
  91.4 1.3 collective-permute-done.19
  92.9 2.0 collective-permute-start.22
  94.8 1.4 collective-permute-done.22
  97.7 5.3 %back_second.1 = (bf16[512,768]{1,0:T(8,128)(2,1)S(1)}, f32[8,768]{1,0:T(8,128)S(1)}, bf16[2,768,768]{2,1,0:T(8,128)(2,1)}) custom-call(f32[16,768]{1,0:T(8,128)S(1)} %get-tuple-element.146.gp_ref, s32[1,512]{1,0:T(1,128)S(1)} %constant_dynamic-slice_fusion.9.seg_ref, bf16[512,768]{1,0:T(8,128)(2,1)S(1)} %copy-done.25, f32[512,128]{1,0:T(8,128)S(1)} %copy-done.27, ...), custom_call_target="tpu_custom_call" | custom-call | flops 1207959552 | bytes 14000000 | tf_op jit(solution)/shard_map/back_second/pallas_call | solution.py:859
  103.4 4.3 %back_outer.1 = bf16[2,768,768]{2,1,0:T(8,128)(2,1)} custom-call(bf16[512,768]{1,0:T(8,128)(2,1)S(1)} %get-tuple-element.153.low_ref, bf16[2,512,768]{2,1,0:T(8,128)(2,1)} %get-tuple-element.149.act01_hbm, bf16[2,512,768]{2,1,0:T(8,128)(2,1)} %get-tuple-element.150.act23_hbm), custom_call_target="tpu_custom_call" | custom-call | flops 1207959552 | bytes 8000000 | tf_op jit(solution)/shard_map/back_outer/pallas_call | solution.py:875
  107.9 2.9 %add_convert_fusion = bf16[2,768,768]{2,1,0:T(8,128)(2,1)S(1)} fusion(bf16[2,768,768]{2,1,0:T(8,128)(2,1)} %collective-permute-done.23, bf16[2,768,768]{2,1,0:T(8,128)(2,1)} %back_outer.1), kind=kLoop, calls=%fused_computation | loop fusion | flops 4718592 | bytes 7077888 | tf_op jit(solution)/shard_map/convert_element_type | solution.py:618
  113.1 14.9 %back_first.1 = (bf16[4,512,768]{2,1,0:T(8,128)(2,1)}, bf16[512,768]{1,0:T(8,128)(2,1)}, f32[8,768]{1,0:T(8,128)S(1)}, f32[4,768]{1,0:T(4,128)S(1)}, bf16[512,19...) custom-call(bf16[512,768]{1,0:T(8,128)(2,1)} %copy-done.4, ...), custom_call_target="tpu_custom_call" | custom-call | flops 5435817984 | bytes 25000000 | tf_op jit(solution)/shard_map/back_first/pallas_call | solution.py:889
  128.6 1.5 collective-permute-start.24
  131.3 6.5 %weight_grads.2 = bf16[2,1024,768]{2,1,0:T(8,128)(2,1)} custom-call(bf16[512,768]{1,0:T(8,128)(2,1)S(1)} %copy-done.3, bf16[512,768]{1,0:T(8,128)(2,1)} %get-tuple-element.171.attn_ref, f32[8,768]{1,0:T(8,128)S(1)} %get-tuple-element.164.vec1_ref, f32[8,768]{1,0:T(8,128)S(1)} %get-tuple-element.165.vec2_ref, f32[4,768]{1,0:T(4,128)S(1)} %get-tuple-element.166.bin_ref, ...), custom_call_target="tpu_custom_call" | custom-call | flops 1509949440 | bytes 7000000 | tf_op jit(solution)/shard_map/weight_grads/pallas_call | solution.py:915
  137.8 1.4 maximum_select_fusion.2
  139.2 1.4 collective-permute-start.27
  140.6 1.9 add_convert_fusion.2
  142.6 1.4 collective-permute-start.29
  144.1 6.0 %weight_grads.3 = bf16[2,1024,768]{2,1,0:T(8,128)(2,1)} custom-call(bf16[512,768]{1,0:T(8,128)(2,1)S(1)} %copy-done.3, bf16[512,768]{1,0:T(8,128)(2,1)} %get-tuple-element.171.attn_ref, f32[8,768]{1,0:T(8,128)S(1)} %get-tuple-element.164.vec1_ref, f32[8,768]{1,0:T(8,128)S(1)} %get-tuple-element.165.vec2_ref, f32[4,768]{1,0:T(4,128)S(1)} %get-tuple-element.166.bin_ref, ...), custom_call_target="tpu_custom_call" | custom-call | flops 1509949440 | bytes 7000000 | tf_op jit(solution)/shard_map/weight_grads/pallas_call | solution.py:915
  150.1 1.8 collective-permute-done.28.refs_0_
  151.9 3.5 %fusion.1 = bf16[1024,768]{1,0:T(8,128)(2,1)} fusion(bf16[2,1024,768]{2,1,0:T(8,128)(2,1)} %collective-permute-done.27, bf16[2,1024,768]{2,1,0:T(8,128)(2,1)} %weight_grads.3), kind=kLoop, calls=%fused_computation.8 | loop fusion | flops 3145728 | bytes 4718592 | tf_op jit(solution)/shard_map/convert_element_type | solution.py:618
  156.9 1.5 collective-permute-start.31
  158.4 1.8 collective-permute-start.32
  160.2 12.5 %attend_backward.2 = (bf16[512,768]{1,0:T(8,128)(2,1)S(1)}, bf16[512,768]{1,0:T(8,128)(2,1)}, f32[576,768]{1,0:T(8,128)}, f32[8,192]{1,0:T(8,128)S(1)}) custom-call(s32[1]{0:T(128)} %bitcast.5.m_ref, bf16[2048,768]{1,0:T(8,128)(2,1)} %tok_ref.7, bf16[3,192,768]{2,1,0:T(8,128)(2,1)} %bitcast.64, bf16[4,3,512,192]{3,2,1,0:T(8,128)(2,1)} %get-tuple-element.178.qkv_ref, ...), custom_call_target="tpu_custom_call" | custom-call | flops 1811939328 | bytes 8000000 | tf_op jit(solution)/shard_map/attend_backward/pallas_call | solution.py:951
  175.3 1.3 collective-permute-start.34
  176.6 13.1 %attend_backward.3 = (bf16[512,768]{1,0:T(8,128)(2,1)S(1)}, bf16[512,768]{1,0:T(8,128)(2,1)}, bf16[640,768]{1,0:T(8,128)(2,1)}) custom-call(s32[1]{0:T(128)} %bitcast.5.m_ref, bf16[2048,768]{1,0:T(8,128)(2,1)} %tok_ref.7, bf16[3,192,768]{2,1,0:T(8,128)(2,1)} %bitcast.65, bf16[4,3,512,192]{3,2,1,0:T(8,128)(2,1)} %get-tuple-element.178.qkv_ref, ...), custom_call_target="tpu_custom_call" | custom-call | flops 1811939328 | bytes 8000000 | tf_op jit(solution)/shard_map/attend_backward/pallas_call | solution.py:951
  193.6 2.5 fusion
  196.3 1.6 collective-permute-start.35
  198.0 1.3 collective-permute-done.41
  201.3 9.8 %collective-permute-done.35 = bf16[96,768]{1,0:T(8,128)(2,1)S(1)} collective-permute-done((bf16[96,768]{1,0:T(8,128)(2,1)S(1)}, bf16[96,768]{1,0:T(8,128)(2,1)S(1)}, u32[]{:S(2)}, u32[]{:S(2)}) %collective-permute-start.35) | collective-permute-done | bytes 147488 | tf_op jit(solution)/shard_map/ppermute | solution.py:633
  216.9 4.4 %collective-permute-done.44 = bf16[256,768]{1,0:T(8,128)(2,1)S(1)} collective-permute-done((bf16[256,768]{1,0:T(8,128)(2,1)}, bf16[256,768]{1,0:T(8,128)(2,1)S(1)}, u32[]{:S(2)}, u32[]{:S(2)}) %collective-permute-start.44) | collective-permute-done | bytes 393248 | tf_op jit(solution)/shard_map/ppermute | solution.py:633
  221.5 2.4 collective-permute-start.45
  224.0 1.3 collective-permute-start.51
  225.3 4.0 %collective-permute-done.39 = bf16[512,768]{1,0:T(8,128)(2,1)S(1)} collective-permute-done((bf16[512,768]{1,0:T(8,128)(2,1)S(1)}, bf16[512,768]{1,0:T(8,128)(2,1)S(1)}, u32[]{:S(2)}, u32[]{:S(2)}) %collective-permute-start.39) | collective-permute-done | bytes 786464 | tf_op jit(solution)/shard_map/ppermute | solution.py:578
  229.6 2.3 collective-permute-start.40
  231.9 10.6 %collective-permute-done.45 = bf16[160,768]{1,0:T(8,128)(2,1)S(1)} collective-permute-done((bf16[160,768]{1,0:T(8,128)(2,1)S(1)}, bf16[160,768]{1,0:T(8,128)(2,1)S(1)}, u32[]{:S(2)}, u32[]{:S(2)}) %collective-permute-start.45) | collective-permute-done | bytes 245792 | tf_op jit(solution)/shard_map/ppermute | solution.py:633
  244.1 6.9 %collective-permute-done.48 = bf16[256,768]{1,0:T(8,128)(2,1)S(1)} collective-permute-done((bf16[256,768]{1,0:T(8,128)(2,1)S(1)}, bf16[256,768]{1,0:T(8,128)(2,1)S(1)}, u32[]{:S(2)}, u32[]{:S(2)}) %collective-permute-start.48) | collective-permute-done | bytes 393248 | tf_op jit(solution)/shard_map/ppermute | solution.py:633
  252.6 3.4 %maximum_select_fusion = bf16[2,2,512,768]{3,2,0,1:T(8,128)(2,1)S(1)} fusion(bf16[2,1,512,768]{3,2,0,1:T(8,128)(2,1)} %bitcast.31, bf16[2,1,512,768]{3,2,0,1:T(8,128)(2,1)} %bitcast.30, pred[]{:T(512)S(6)} %eq.138), kind=kLoop, calls=%fused_computation.1 | loop fusion | flops 4718592 | bytes 6291457 | tf_op jit(solution)/shard_map/jit(_where)/select_n | solution.py:1077
  256.0 1.9 copy.44
  258.1 2.1 collective-permute-done.49
  261.1 4.0 %collective-permute-done.52 = bf16[384,768]{1,0:T(8,128)(2,1)S(1)} collective-permute-done((bf16[384,768]{1,0:T(8,128)(2,1)S(1)}, bf16[384,768]{1,0:T(8,128)(2,1)S(1)}, u32[]{:S(2)}, u32[]{:S(2)}) %collective-permute-start.52) | collective-permute-done | bytes 589856 | tf_op jit(solution)/shard_map/ppermute | solution.py:633
  265.1 1.6 fusion.2
  266.7 4.3 %collective-permute-done.47 = bf16[320,768]{1,0:T(8,128)(2,1)S(1)} collective-permute-done((bf16[320,768]{1,0:T(8,128)(2,1)S(1)}, bf16[320,768]{1,0:T(8,128)(2,1)S(1)}, u32[]{:S(2)}, u32[]{:S(2)}) %collective-permute-start.47) | collective-permute-done | bytes 491552 | tf_op jit(solution)/shard_map/ppermute | solution.py:633
  272.0 1.3 convert_bitcast_fusion
  273.9 1.9 copy.45
  275.7 3.4 %collective-permute-done.50 = bf16[512,768]{1,0:T(8,128)(2,1)S(1)} collective-permute-done((bf16[512,768]{1,0:T(8,128)(2,1)S(1)}, bf16[512,768]{1,0:T(8,128)(2,1)S(1)}, u32[]{:S(2)}, u32[]{:S(2)}) %collective-permute-start.50) | collective-permute-done | bytes 786464 | tf_op jit(solution)/shard_map/ppermute | solution.py:633
  280.6 1.6 slice_convert_fusion
  (208 shorter events, 45.8 us)
Async XLA Ops:
  0.6 62.6 %copy-start = (s32[4,8]{1,0:T(4,128)S(1)}, s32[4,8]{1,0:T(4,128)}, u32[]{:S(2)}) copy-start(s32[4,8]{1,0:T(4,128)} %param.29) | copy-start | bytes 388
  0.7 8.4 %copy-start.2 = (bf16[3,768,192]{1,2,0:T(8,128)(2,1)S(1)}, bf16[3,768,192]{1,2,0:T(8,128)(2,1)}, u32[]{:S(2)}) copy-start(bf16[3,768,192]{1,2,0:T(8,128)(2,1)} %param.16) | copy-start | bytes 2654212
  0.7 8.4 %collective-permute-start = (bf16[768,768]{1,0:T(8,128)(2,1)}, bf16[768,768]{1,0:T(8,128)(2,1)}, u32[]{:S(2)}, u32[]{:S(2)}) collective-permute-start(bf16[768,768]{1,0:T(8,128)(2,1)} %wi0.3), channel_id=1, source_target_pairs={{0,1},{1,0},{2,3},{3,2},{4,5},{5,4},{6,7},{7,6},{8,9},{9,8},{10,11... | collective-permute-start | bytes 3538952 | tf_op jit(solution)/shard_map/ppermute | solution.py:578
  0.8 8.3 %collective-permute-start.1 = (bf16[768,768]{1,0:T(8,128)(2,1)}, bf16[768,768]{1,0:T(8,128)(2,1)}, u32[]{:S(2)}, u32[]{:S(2)}) collective-permute-start(bf16[768,768]{1,0:T(8,128)(2,1)} %wb0.3), channel_id=1, source_target_pairs={{0,1},{1,0},{2,3},{3,2},{4,5},{5,4},{6,7},{7,6},{8,9},{9,8},{10,11... | collective-permute-start | bytes 3538952 | tf_op jit(solution)/shard_map/ppermute | solution.py:578
  3.0 6.1 %copy-start.7 = (f32[2,192]{1,0:T(2,128)S(1)}, f32[2,192]{1,0:T(2,128)}, u32[]{:S(2)}) copy-start(f32[2,192]{1,0:T(2,128)} %b_ref.1) | copy-start | bytes 4612
  4.6 2.8 %collective-permute-start.2 = (bf16[208,768]{1,0:T(8,128)(2,1)S(1)}, bf16[208,768]{1,0:T(8,128)(2,1)S(1)}, u32[]{:S(2)}, u32[]{:S(2)}) collective-permute-start(bf16[208,768]{1,0:T(8,128)(2,1)S(1)} %get-tuple-element.112.wo0), channel_id=1, source_target_pairs={{0,1},{1,0},{2,3},{3,2},{4,5},{5,4},{6,7},{7,6},{8,9},{9,8},{10,11... | collective-permute-start | bytes 958472 | tf_op jit(solution)/shard_map/ppermute | solution.py:578
  4.7 23.2 %collective-permute-start.5 = (bf16[208,768]{1,0:T(8,128)(2,1)S(1)}, bf16[208,768]{1,0:T(8,128)(2,1)S(1)}, u32[]{:S(2)}, u32[]{:S(2)}) collective-permute-start(bf16[208,768]{1,0:T(8,128)(2,1)S(1)} %get-tuple-element.112.wo0), channel_id=1, source_target_pairs={{0,2},{1,3},{2,0},{3,1},{4,6},{5,7},{6,4},{7,5},{8,10},{9,11},{10,... | collective-permute-start | bytes 958472 | tf_op jit(solution)/shard_map/ppermute | solution.py:578
  7.4 14.9 %collective-permute-start.3 = (bf16[192,768]{1,0:T(8,128)(2,1)S(1)}, bf16[192,768]{1,0:T(8,128)(2,1)}, u32[]{:S(2)}, u32[]{:S(2)}) collective-permute-start(bf16[192,768]{1,0:T(8,128)(2,1)S(1)} %get-tuple-element.120), channel_id=1, source_target_pairs={{0,2},{1,3},{2,0},{3,1},{4,6},{5,7},{6,4},{7,5},{8,10},{9,11},{10,... | collective-permute-start | bytes 884744 | tf_op jit(solution)/shard_map/ppermute | solution.py:578
  7.4 20.5 %collective-permute-start.4 = (bf16[192,768]{1,0:T(8,128)(2,1)S(1)}, bf16[192,768]{1,0:T(8,128)(2,1)}, u32[]{:S(2)}, u32[]{:S(2)}) collective-permute-start(bf16[192,768]{1,0:T(8,128)(2,1)S(1)} %get-tuple-element.121), channel_id=1, source_target_pairs={{0,2},{1,3},{2,0},{3,1},{4,6},{5,7},{6,4},{7,5},{8,10},{9,11},{10,... | collective-permute-start | bytes 884744 | tf_op jit(solution)/shard_map/ppermute | solution.py:578
  28.0 10.9 %copy-start.8 = (bf16[208,768]{1,0:T(8,128)(2,1)}, bf16[208,768]{1,0:T(8,128)(2,1)S(1)}, u32[]{:S(2)}) copy-start(bf16[208,768]{1,0:T(8,128)(2,1)S(1)} %collective-permute-done.5.wo2) | copy-start | bytes 958468
  28.0 11.0 %collective-permute-start.7 = (bf16[192,768]{1,0:T(8,128)(2,1)}, bf16[192,768]{1,0:T(8,128)(2,1)S(1)}, u32[]{:S(2)}, u32[]{:S(2)}) collective-permute-start(bf16[192,768]{1,0:T(8,128)(2,1)} %collective-permute-done.3), channel_id=1, source_target_pairs={{0,8},{4,12},{8,0},{12,4},{16,24},{20,28},{24,16},{28,20},{1,9},{5... | collective-permute-start | bytes 884744 | tf_op jit(solution)/shard_map/ppermute | solution.py:578
  29.3 9.7 %collective-permute-start.8 = (bf16[192,768]{1,0:T(8,128)(2,1)}, bf16[192,768]{1,0:T(8,128)(2,1)}, u32[]{:S(2)}, u32[]{:S(2)}) collective-permute-start(bf16[192,768]{1,0:T(8,128)(2,1)} %collective-permute-done.4), channel_id=1, source_target_pairs={{0,4},{4,0},{8,12},{12,8},{16,20},{20,16},{24,28},{28,24},{1,5},{5... | collective-permute-start | bytes 884744 | tf_op jit(solution)/shard_map/ppermute | solution.py:578
  30.5 11.1 %collective-permute-start.9 = (bf16[512,192]{1,0:T(8,128)(2,1)}, bf16[512,192]{1,0:T(8,128)(2,1)S(1)}, u32[]{:S(2)}, u32[]{:S(2)}) collective-permute-start(bf16[512,192]{1,0:T(8,128)(2,1)} %get-tuple-element.127), channel_id=1, source_target_pairs={{0,2},{1,3},{2,0},{3,1},{4,6},{5,7},{6,4},{7,5},{8,10},{9,11},{10,... | collective-permute-start | bytes 589832 | tf_op jit(solution)/shard_map/ppermute | solution.py:578
  31.8 12.6 %collective-permute-start.10 = (bf16[512,192]{1,0:T(8,128)(2,1)S(1)}, bf16[512,192]{1,0:T(8,128)(2,1)S(1)}, u32[]{:S(2)}, u32[]{:S(2)}) collective-permute-start(bf16[512,192]{1,0:T(8,128)(2,1)S(1)} %get-tuple-element.128), channel_id=1, source_target_pairs={{0,3},{1,2},{2,1},{3,0},{4,7},{5,6},{6,5},{7,4},{8,11},{9,10},{10,... | collective-permute-start | bytes 589832 | tf_op jit(solution)/shard_map/ppermute | solution.py:578
  38.9 8.1 %copy-start.18 = (f32[768]{0:T(1024)S(1)}, f32[768]{0:T(1024)}, u32[]{:S(2)}) copy-start(f32[768]{0:T(1024)} %param.19) | copy-start | bytes 9220
  38.9 8.1 %copy-start.19 = (f32[768]{0:T(1024)S(1)}, f32[768]{0:T(1024)}, u32[]{:S(2)}) copy-start(f32[768]{0:T(1024)} %param.21) | copy-start | bytes 9220
  38.9 8.1 %copy-start.23 = (f32[768]{0:T(1024)S(1)}, f32[768]{0:T(1024)}, u32[]{:S(2)}) copy-start(f32[768]{0:T(1024)} %param.20) | copy-start | bytes 9220
  38.9 7.3 %collective-permute-start.11 = (bf16[208,768]{1,0:T(8,128)(2,1)S(1)}, bf16[208,768]{1,0:T(8,128)(2,1)S(1)}, u32[]{:S(2)}, u32[]{:S(2)}) collective-permute-start(bf16[208,768]{1,0:T(8,128)(2,1)S(1)} %collective-permute-done.5.wo2), channel_id=1, source_target_pairs={{0,1},{1,0},{2,3},{3,2},{4,5},{5,4},{6,7},{7,6},{8,9},{9,8},{10,11... | collective-permute-start | bytes 958472 | tf_op jit(solution)/shard_map/ppermute | solution.py:578
  44.4 15.2 %collective-permute-start.12 = (bf16[384,768]{1,0:T(8,128)(2,1)S(1)}, bf16[384,768]{1,0:T(8,128)(2,1)S(1)}, u32[]{:S(2)}, u32[]{:S(2)}) collective-permute-start(bf16[384,768]{1,0:T(8,128)(2,1)S(1)} %maximum_select_fusion.12), channel_id=1, source_target_pairs={{0,4},{4,0},{8,12},{12,8},{16,20},{20,16},{24,28},{28,24},{1,5},{5... | collective-permute-start | bytes 1769480 | tf_op jit(solution)/shard_map/ppermute | solution.py:578
  44.7 1.5 collective-permute-start.6
  44.7 17.1 %collective-permute-start.14 = (bf16[384,768]{1,0:T(8,128)(2,1)S(1)}, bf16[384,768]{1,0:T(8,128)(2,1)S(1)}, u32[]{:S(2)}, u32[]{:S(2)}) collective-permute-start(bf16[384,768]{1,0:T(8,128)(2,1)S(1)} %maximum_select_fusion.13), channel_id=1, source_target_pairs={{0,8},{4,12},{8,0},{12,4},{16,24},{20,28},{24,16},{28,20},{1,9},{5... | collective-permute-start | bytes 1769480 | tf_op jit(solution)/shard_map/ppermute | solution.py:578
  61.2 3.4 %collective-permute-start.13 = (bf16[768,768]{1,0:T(8,128)(2,1)}, bf16[768,768]{1,0:T(8,128)(2,1)}, u32[]{:S(2)}, u32[]{:S(2)}) collective-permute-start(bf16[768,768]{1,0:T(8,128)(2,1)} %maximum_select_fusion.6.wi2), channel_id=1, source_target_pairs={{0,1},{1,0},{2,3},{3,2},{4,5},{5,4},{6,7},{7,6},{8,9},{9,8},{10,11... | collective-permute-start | bytes 3538952 | tf_op jit(solution)/shard_map/ppermute | solution.py:578
  63.2 3.2 %collective-permute-start.15 = (bf16[768,768]{1,0:T(8,128)(2,1)}, bf16[768,768]{1,0:T(8,128)(2,1)}, u32[]{:S(2)}, u32[]{:S(2)}) collective-permute-start(bf16[768,768]{1,0:T(8,128)(2,1)} %maximum_select_fusion.7.wb2), channel_id=1, source_target_pairs={{0,1},{1,0},{2,3},{3,2},{4,5},{5,4},{6,7},{7,6},{8,9},{9,8},{10,11... | collective-permute-start | bytes 3538952 | tf_op jit(solution)/shard_map/ppermute | solution.py:578
  79.2 4.5 %collective-permute-start.18 = (bf16[1,8,1664]{2,1,0:T(8,128)(2,1)S(1)}, bf16[1,8,1664]{2,1,0:T(8,128)(2,1)S(1)}, u32[]{:S(2)}, u32[]{:S(2)}) collective-permute-start(bf16[1,8,1664]{2,1,0:T(8,128)(2,1)S(1)} %bitcast.69), channel_id=1, source_target_pairs={{0,24},{1,25},{2,26},{3,27},{4,28},{5,29},{6,30},{7,31},{8,16},{9,... | collective-permute-start | bytes 79880 | tf_op jit(solution)/shard_map/ppermute | solution.py:1065
  81.4 3.9 %collective-permute-start.17 = (bf16[1,8,1664]{2,1,0:T(8,128)(2,1)S(1)}, bf16[1,8,1664]{2,1,0:T(8,128)(2,1)S(1)}, u32[]{:S(2)}, u32[]{:S(2)}) collective-permute-start(bf16[1,8,1664]{2,1,0:T(8,128)(2,1)S(1)} %bitcast.70), channel_id=1, source_target_pairs={{0,16},{1,17},{2,18},{3,19},{4,20},{5,21},{6,22},{7,23},{8,24},{9,... | collective-permute-start | bytes 79880 | tf_op jit(solution)/shard_map/ppermute | solution.py:1065
  81.5 3.9 %collective-permute-start.16 = (bf16[1,8,1664]{2,1,0:T(8,128)(2,1)S(1)}, bf16[1,8,1664]{2,1,0:T(8,128)(2,1)S(1)}, u32[]{:S(2)}, u32[]{:S(2)}) collective-permute-start(bf16[1,8,1664]{2,1,0:T(8,128)(2,1)S(1)} %bitcast.71), channel_id=1, source_target_pairs={{0,8},{1,9},{2,10},{3,11},{4,12},{5,13},{6,14},{7,15},{8,0},{9,1},... | collective-permute-start | bytes 79880 | tf_op jit(solution)/shard_map/ppermute | solution.py:1065
  85.4 4.5 %collective-permute-start.21 = (bf16[4,8,1664]{2,1,0:T(8,128)(2,1)S(1)}, bf16[4,8,1664]{2,1,0:T(8,128)(2,1)S(1)}, u32[]{:S(2)}, u32[]{:S(2)}) collective-permute-start(bf16[4,8,1664]{2,1,0:T(8,128)(2,1)S(1)} %bitcast.95), channel_id=1, source_target_pairs={{0,6},{1,7},{2,4},{3,5},{4,2},{5,3},{6,0},{7,1},{8,14},{9,15},{10,... | collective-permute-start | bytes 319496 | tf_op jit(solution)/shard_map/ppermute | solution.py:1065
  87.4 4.0 %collective-permute-start.20 = (bf16[4,8,1664]{2,1,0:T(8,128)(2,1)S(1)}, bf16[4,8,1664]{2,1,0:T(8,128)(2,1)S(1)}, u32[]{:S(2)}, u32[]{:S(2)}) collective-permute-start(bf16[4,8,1664]{2,1,0:T(8,128)(2,1)S(1)} %bitcast.96), channel_id=1, source_target_pairs={{0,4},{1,5},{2,6},{3,7},{4,0},{5,1},{6,2},{7,3},{8,12},{9,13},{10,... | collective-permute-start | bytes 319496 | tf_op jit(solution)/shard_map/ppermute | solution.py:1065
  87.7 5.0 %collective-permute-start.19 = (bf16[4,8,1664]{2,1,0:T(8,128)(2,1)S(1)}, bf16[4,8,1664]{2,1,0:T(8,128)(2,1)S(1)}, u32[]{:S(2)}, u32[]{:S(2)}) collective-permute-start(bf16[4,8,1664]{2,1,0:T(8,128)(2,1)S(1)} %bitcast.97), channel_id=1, source_target_pairs={{0,2},{1,3},{2,0},{3,1},{4,6},{5,7},{6,4},{7,5},{8,10},{9,11},{10,... | collective-permute-start | bytes 319496 | tf_op jit(solution)/shard_map/ppermute | solution.py:1065
  92.9 3.4 %collective-permute-start.22 = (bf16[16,8,1664]{2,1,0:T(8,128)(2,1)S(1)}, bf16[16,8,1664]{2,1,0:T(8,128)(2,1)S(1)}, u32[]{:S(2)}, u32[]{:S(2)}) collective-permute-start(bf16[16,8,1664]{2,1,0:T(8,128)(2,1)S(1)} %bitcast.89), channel_id=1, source_target_pairs={{0,1},{1,0},{2,3},{3,2},{4,5},{5,4},{6,7},{7,6},{8,9},{9,8},{10,11... | collective-permute-start | bytes 1277960 | tf_op jit(solution)/shard_map/ppermute | solution.py:578
  103.0 4.9 %collective-permute-start.23 = (bf16[2,768,768]{2,1,0:T(8,128)(2,1)}, bf16[2,768,768]{2,1,0:T(8,128)(2,1)}, u32[]{:S(2)}, u32[]{:S(2)}) collective-permute-start(bf16[2,768,768]{2,1,0:T(8,128)(2,1)} %get-tuple-element.152), channel_id=1, source_target_pairs={{0,1},{1,0},{2,3},{3,2},{4,5},{5,4},{6,7},{7,6},{8,9},{9,8},{10,11... | collective-permute-start | bytes 7077896 | tf_op jit(solution)/shard_map/ppermute | solution.py:578
  111.0 20.3 %collective-permute-start.25 = (bf16[2,384,768]{2,1,0:T(8,128)(2,1)S(1)}, bf16[2,384,768]{2,1,0:T(8,128)(2,1)S(1)}, u32[]{:S(2)}, u32[]{:S(2)}) collective-permute-start(bf16[2,384,768]{2,1,0:T(8,128)(2,1)S(1)} %constant_dynamic-slice_fusion.7), channel_id=1, source_target_pairs={{0,4},{1,9},{2,6},{3,11},{4,0},{5,13},{6,2},{7,15},{8,12},{9,1},{1... | collective-permute-start | bytes 3538952 | tf_op jit(solution)/shard_map/ppermute | solution.py:633
  112.6 18.8 %collective-permute-start.26 = (bf16[512,768]{1,0:T(8,128)(2,1)S(1)}, bf16[512,768]{1,0:T(8,128)(2,1)S(1)}, u32[]{:S(2)}, u32[]{:S(2)}) collective-permute-start(bf16[512,768]{1,0:T(8,128)(2,1)S(1)} %copy-done.37), channel_id=1, source_target_pairs={{0,2},{1,3},{2,0},{3,1},{4,6},{5,7},{6,4},{7,5},{8,10},{9,11},{10,... | collective-permute-start | bytes 2359304 | tf_op jit(solution)/shard_map/ppermute | solution.py:578
  113.1 18.3 %copy-start.3 = (bf16[512,768]{1,0:T(8,128)(2,1)S(1)}, bf16[512,768]{1,0:T(8,128)(2,1)}, u32[]{:S(2)}) copy-start(bf16[512,768]{1,0:T(8,128)(2,1)} %get-tuple-element.136.low1_ref) | copy-start | bytes 2359300
  128.6 9.1 %copy-start.12 = (bf16[512,192]{1,0:T(8,128)(2,1)}, bf16[512,192]{1,0:T(8,128)(2,1)S(1)}, u32[]{:S(2)}) copy-start(bf16[512,192]{1,0:T(8,128)(2,1)S(1)} %get-tuple-element.185) | copy-start | bytes 589828
  128.6 10.5 %collective-permute-start.24 = (bf16[512,192]{1,0:T(8,128)(2,1)S(1)}, bf16[512,192]{1,0:T(8,128)(2,1)S(1)}, u32[]{:S(2)}, u32[]{:S(2)}) collective-permute-start(bf16[512,192]{1,0:T(8,128)(2,1)S(1)} %get-tuple-element.158), channel_id=1, source_target_pairs={{0,3},{1,2},{2,1},{3,0},{4,7},{5,6},{6,5},{7,4},{8,11},{9,10},{10,... | collective-permute-start | bytes 589832 | tf_op jit(solution)/shard_map/ppermute | solution.py:578
  131.3 6.5 %copy-start.35 = (bf16[2,384,768]{2,1,0:T(8,128)(2,1)}, bf16[2,384,768]{2,1,0:T(8,128)(2,1)S(1)}, u32[]{:S(2)}) copy-start(bf16[2,384,768]{2,1,0:T(8,128)(2,1)S(1)} %collective-permute-done.25) | copy-start | bytes 3538948
  139.2 12.7 %collective-permute-start.27 = (bf16[2,1024,768]{2,1,0:T(8,128)(2,1)}, bf16[2,1024,768]{2,1,0:T(8,128)(2,1)}, u32[]{:S(2)}, u32[]{:S(2)}) collective-permute-start(bf16[2,1024,768]{2,1,0:T(8,128)(2,1)} %weight_grads.2), channel_id=1, source_target_pairs={{0,1},{1,0},{2,3},{3,2},{4,5},{5,4},{6,7},{7,6},{8,9},{9,8},{10,11... | collective-permute-start | bytes 9437192 | tf_op jit(solution)/shard_map/ppermute | solution.py:578
  140.5 11.4 %collective-permute-start.30 = (bf16[2,512,768]{2,1,0:T(8,128)(2,1)}, bf16[2,512,768]{2,1,0:T(8,128)(2,1)}, u32[]{:S(2)}, u32[]{:S(2)}) collective-permute-start(bf16[2,512,768]{2,1,0:T(8,128)(2,1)} %maximum_select_fusion.2), channel_id=1, source_target_pairs={{0,1},{1,0},{2,3},{3,2},{4,5},{5,4},{6,7},{7,6},{8,9},{9,8},{10,11... | collective-permute-start | bytes 4718600 | tf_op jit(solution)/shard_map/ppermute | solution.py:578
  142.6 9.3 %collective-permute-start.29 = (bf16[2,192,768]{2,1,0:T(8,128)(2,1)S(1)}, bf16[2,192,768]{2,1,0:T(8,128)(2,1)}, u32[]{:S(2)}, u32[]{:S(2)}) collective-permute-start(bf16[2,192,768]{2,1,0:T(8,128)(2,1)S(1)} %constant_dynamic-slice_fusion.6), channel_id=1, source_target_pairs={{0,8},{1,5},{2,10},{3,7},{4,12},{5,1},{6,14},{7,3},{8,0},{9,13},{1... | collective-permute-start | bytes 1769480 | tf_op jit(solution)/shard_map/ppermute | solution.py:633
  143.9 8.0 %collective-permute-start.28 = (bf16[512,192]{1,0:T(8,128)(2,1)S(1)}, bf16[512,192]{1,0:T(8,128)(2,1)S(1)}, u32[]{:S(2)}, u32[]{:S(2)}) collective-permute-start(bf16[512,192]{1,0:T(8,128)(2,1)S(1)} %copy-done.15), channel_id=1, source_target_pairs={{0,2},{1,3},{2,0},{3,1},{4,6},{5,7},{6,4},{7,5},{8,10},{9,11},{10,... | collective-permute-start | bytes 589832 | tf_op jit(solution)/shard_map/ppermute | solution.py:578
  155.4 38.2 %collective-permute-start.33 = (bf16[1024,768]{1,0:T(8,128)(2,1)}, bf16[1024,768]{1,0:T(8,128)(2,1)}, u32[]{:S(2)}, u32[]{:S(2)}) collective-permute-start(bf16[1024,768]{1,0:T(8,128)(2,1)} %fusion.1), channel_id=1, source_target_pairs={{0,2},{1,3},{2,0},{3,1},{4,6},{5,7},{6,4},{7,5},{8,10},{9,11},{10,... | collective-permute-start | bytes 4718600 | tf_op jit(solution)/shard_map/ppermute | solution.py:578
  156.9 16.1 %collective-permute-start.31 = (bf16[2,96,768]{2,1,0:T(8,128)(2,1)S(1)}, bf16[2,96,768]{2,1,0:T(8,128)(2,1)S(1)}, u32[]{:S(2)}, u32[]{:S(2)}) collective-permute-start(bf16[2,96,768]{2,1,0:T(8,128)(2,1)S(1)} %constant_dynamic-slice_fusion.5), channel_id=1, source_target_pairs={{0,16},{1,17},{2,18},{3,19},{4,20},{5,21},{6,22},{7,23},{8,24},{9,... | collective-permute-start | bytes 884744 | tf_op jit(solution)/shard_map/ppermute | solution.py:633
  158.4 14.3 %collective-permute-start.32 = (bf16[512,192]{1,0:T(8,128)(2,1)S(1)}, bf16[512,192]{1,0:T(8,128)(2,1)S(1)}, u32[]{:S(2)}, u32[]{:S(2)}) collective-permute-start(bf16[512,192]{1,0:T(8,128)(2,1)S(1)} %copy-done.13), channel_id=1, source_target_pairs={{0,1},{1,0},{2,3},{3,2},{4,5},{5,4},{6,7},{7,6},{8,9},{9,8},{10,11... | collective-permute-start | bytes 589832 | tf_op jit(solution)/shard_map/ppermute | solution.py:578
  173.8 17.7 %collective-permute-start.37 = (bf16[512,768]{1,0:T(8,128)(2,1)}, bf16[512,768]{1,0:T(8,128)(2,1)S(1)}, u32[]{:S(2)}, u32[]{:S(2)}) collective-permute-start(bf16[512,768]{1,0:T(8,128)(2,1)} %get-tuple-element.200), channel_id=1, source_target_pairs={{0,1},{1,0},{2,3},{3,2},{4,5},{5,4},{6,7},{7,6},{8,9},{9,8},{10,11... | collective-permute-start | bytes 2359304 | tf_op jit(solution)/shard_map/ppermute | solution.py:578
  175.3 18.3 %collective-permute-start.34 = (bf16[96,768]{1,0:T(8,128)(2,1)S(1)}, bf16[96,768]{1,0:T(8,128)(2,1)S(1)}, u32[]{:S(2)}, u32[]{:S(2)}) collective-permute-start(bf16[96,768]{1,0:T(8,128)(2,1)S(1)} %slice_bitcast_fusion), channel_id=1, source_target_pairs={{0,2},{1,3},{2,0},{3,1},{4,6},{5,7},{6,4},{7,5},{8,10},{9,11},{10,... | collective-permute-start | bytes 442376 | tf_op jit(solution)/shard_map/ppermute | solution.py:578
  189.7 11.6 %collective-permute-start.36 = (bf16[512,768]{1,0:T(8,128)(2,1)}, bf16[512,768]{1,0:T(8,128)(2,1)S(1)}, u32[]{:S(2)}, u32[]{:S(2)}) collective-permute-start(bf16[512,768]{1,0:T(8,128)(2,1)} %get-tuple-element.198), channel_id=1, source_target_pairs={{0,1},{1,0},{2,3},{3,2},{4,5},{5,4},{6,7},{7,6},{8,9},{9,8},{10,11... | collective-permute-start | bytes 2359304 | tf_op jit(solution)/shard_map/ppermute | solution.py:578
  191.2 8.0 %collective-permute-start.41 = (bf16[320,768]{1,0:T(8,128)(2,1)S(1)}, bf16[320,768]{1,0:T(8,128)(2,1)S(1)}, u32[]{:S(2)}, u32[]{:S(2)}) collective-permute-start(bf16[320,768]{1,0:T(8,128)(2,1)S(1)} %constant_dynamic-slice_fusion.4), channel_id=1, source_target_pairs={{0,4},{1,9},{2,6},{3,11},{4,0},{5,13},{6,2},{7,15},{8,12},{9,1},{1... | collective-permute-start | bytes 1474568 | tf_op jit(solution)/shard_map/ppermute | solution.py:633
  191.6 19.5 %collective-permute-start.38 = (bf16[512,768]{1,0:T(8,128)(2,1)S(1)}, bf16[512,768]{1,0:T(8,128)(2,1)S(1)}, u32[]{:S(2)}, u32[]{:S(2)}) collective-permute-start(bf16[512,768]{1,0:T(8,128)(2,1)S(1)} %add_convert_fusion.5), channel_id=1, source_target_pairs={{0,2},{1,3},{2,0},{3,1},{4,6},{5,7},{6,4},{7,5},{8,10},{9,11},{10,... | collective-permute-start | bytes 2359304 | tf_op jit(solution)/shard_map/ppermute | solution.py:578
  196.2 15.0 %copy-start.32 = (bf16[512,768]{1,0:T(8,128)(2,1)S(1)}, bf16[512,768]{1,0:T(8,128)(2,1)}, u32[]{:S(2)}) copy-start(bf16[512,768]{1,0:T(8,128)(2,1)} %get-tuple-element.171.attn_ref) | copy-start | bytes 2359300
  196.2 17.1 %collective-permute-start.43 = (bf16[512,768]{1,0:T(8,128)(2,1)S(1)}, bf16[512,768]{1,0:T(8,128)(2,1)S(1)}, u32[]{:S(2)}, u32[]{:S(2)}) collective-permute-start(bf16[512,768]{1,0:T(8,128)(2,1)S(1)} %constant_dynamic-slice_fusion.2), channel_id=1, source_target_pairs={{0,4},{1,9},{2,6},{3,11},{4,0},{5,13},{6,2},{7,15},{8,12},{9,1},{1... | collective-permute-start | bytes 2359304 | tf_op jit(solution)/shard_map/ppermute | solution.py:633
  196.3 14.8 %collective-permute-start.35 = (bf16[96,768]{1,0:T(8,128)(2,1)S(1)}, bf16[96,768]{1,0:T(8,128)(2,1)S(1)}, u32[]{:S(2)}, u32[]{:S(2)}) collective-permute-start(bf16[96,768]{1,0:T(8,128)(2,1)S(1)} %fusion.3), channel_id=1, source_target_pairs={{0,16},{1,17},{2,18},{3,19},{4,20},{5,21},{6,22},{7,23},{8,24},{9,... | collective-permute-start | bytes 442376 | tf_op jit(solution)/shard_map/ppermute | solution.py:633
  200.1 15.8 %collective-permute-start.42 = (bf16[160,768]{1,0:T(8,128)(2,1)}, bf16[160,768]{1,0:T(8,128)(2,1)}, u32[]{:S(2)}, u32[]{:S(2)}) collective-permute-start(bf16[160,768]{1,0:T(8,128)(2,1)} %constant_dynamic-slice_fusion.3), channel_id=1, source_target_pairs={{0,8},{1,5},{2,10},{3,7},{4,12},{5,1},{6,14},{7,3},{8,0},{9,13},{1... | collective-permute-start | bytes 737288 | tf_op jit(solution)/shard_map/ppermute | solution.py:633
  211.6 17.8 %collective-permute-start.39 = (bf16[512,768]{1,0:T(8,128)(2,1)S(1)}, bf16[512,768]{1,0:T(8,128)(2,1)S(1)}, u32[]{:S(2)}, u32[]{:S(2)}) collective-permute-start(bf16[512,768]{1,0:T(8,128)(2,1)S(1)} %add_convert_fusion.4), channel_id=1, source_target_pairs={{0,2},{1,3},{2,0},{3,1},{4,6},{5,7},{6,4},{7,5},{8,10},{9,11},{10,... | collective-permute-start | bytes 2359304 | tf_op jit(solution)/shard_map/ppermute | solution.py:578
  214.2 7.1 %collective-permute-start.44 = (bf16[256,768]{1,0:T(8,128)(2,1)}, bf16[256,768]{1,0:T(8,128)(2,1)S(1)}, u32[]{:S(2)}, u32[]{:S(2)}) collective-permute-start(bf16[256,768]{1,0:T(8,128)(2,1)} %constant_dynamic-slice_fusion.1), channel_id=1, source_target_pairs={{0,8},{1,5},{2,10},{3,7},{4,12},{5,1},{6,14},{7,3},{8,0},{9,13},{1... | collective-permute-start | bytes 1179656 | tf_op jit(solution)/shard_map/ppermute | solution.py:633
  221.5 21.1 %collective-permute-start.45 = (bf16[160,768]{1,0:T(8,128)(2,1)S(1)}, bf16[160,768]{1,0:T(8,128)(2,1)S(1)}, u32[]{:S(2)}, u32[]{:S(2)}) collective-permute-start(bf16[160,768]{1,0:T(8,128)(2,1)S(1)} %add_convert_fusion.12), channel_id=1, source_target_pairs={{0,16},{1,17},{2,18},{3,19},{4,20},{5,21},{6,22},{7,23},{8,24},{9,... | collective-permute-start | bytes 737288 | tf_op jit(solution)/shard_map/ppermute | solution.py:633
  223.9 27.1 %collective-permute-start.48 = (bf16[256,768]{1,0:T(8,128)(2,1)S(1)}, bf16[256,768]{1,0:T(8,128)(2,1)S(1)}, u32[]{:S(2)}, u32[]{:S(2)}) collective-permute-start(bf16[256,768]{1,0:T(8,128)(2,1)S(1)} %add_convert_fusion.9), channel_id=1, source_target_pairs={{0,16},{1,17},{2,18},{3,19},{4,20},{5,21},{6,22},{7,23},{8,24},{9,... | collective-permute-start | bytes 1179656 | tf_op jit(solution)/shard_map/ppermute | solution.py:633
  224.0 19.8 %collective-permute-start.51 = (bf16[192,768]{1,0:T(8,128)(2,1)S(1)}, bf16[192,768]{1,0:T(8,128)(2,1)S(1)}, u32[]{:S(2)}, u32[]{:S(2)}) collective-permute-start(bf16[192,768]{1,0:T(8,128)(2,1)S(1)} %maximum_select_fusion.17), channel_id=1, source_target_pairs={{0,8},{1,5},{2,10},{3,7},{4,12},{5,1},{6,14},{7,3},{8,0},{9,13},{1... | collective-permute-start | bytes 884744 | tf_op jit(solution)/shard_map/ppermute | solution.py:633
  229.6 43.7 %collective-permute-start.40 = (bf16[2,512,768]{2,1,0:T(8,128)(2,1)S(1)}, bf16[2,512,768]{2,1,0:T(8,128)(2,1)S(1)}, u32[]{:S(2)}, u32[]{:S(2)}) collective-permute-start(bf16[2,512,768]{2,1,0:T(8,128)(2,1)S(1)} %maximum_select_fusion.4), channel_id=1, source_target_pairs={{0,1},{1,0},{2,3},{3,2},{4,5},{5,4},{6,7},{7,6},{8,9},{9,8},{10,11... | collective-permute-start | bytes 4718600 | tf_op jit(solution)/shard_map/ppermute | solution.py:578
  242.6 9.8 %collective-permute-start.46 = (bf16[160,768]{1,0:T(8,128)(2,1)S(1)}, bf16[160,768]{1,0:T(8,128)(2,1)S(1)}, u32[]{:S(2)}, u32[]{:S(2)}) collective-permute-start(bf16[160,768]{1,0:T(8,128)(2,1)S(1)} %add_convert_fusion.11), channel_id=1, source_target_pairs={{0,8},{1,5},{2,10},{3,7},{4,12},{5,1},{6,14},{7,3},{8,0},{9,13},{1... | collective-permute-start | bytes 737288 | tf_op jit(solution)/shard_map/ppermute | solution.py:633
  244.0 21.0 %collective-permute-start.52 = (bf16[384,768]{1,0:T(8,128)(2,1)S(1)}, bf16[384,768]{1,0:T(8,128)(2,1)S(1)}, u32[]{:S(2)}, u32[]{:S(2)}) collective-permute-start(bf16[384,768]{1,0:T(8,128)(2,1)S(1)} %maximum_select_fusion.14), channel_id=1, source_target_pairs={{0,4},{1,9},{2,6},{3,11},{4,0},{5,13},{6,2},{7,15},{8,12},{9,1},{1... | collective-permute-start | bytes 1769480 | tf_op jit(solution)/shard_map/ppermute | solution.py:633
  251.1 9.1 %collective-permute-start.49 = (bf16[256,768]{1,0:T(8,128)(2,1)S(1)}, bf16[256,768]{1,0:T(8,128)(2,1)S(1)}, u32[]{:S(2)}, u32[]{:S(2)}) collective-permute-start(bf16[256,768]{1,0:T(8,128)(2,1)S(1)} %add_convert_fusion.8), channel_id=1, source_target_pairs={{0,8},{1,5},{2,10},{3,7},{4,12},{5,1},{6,14},{7,3},{8,0},{9,13},{1... | collective-permute-start | bytes 1179656 | tf_op jit(solution)/shard_map/ppermute | solution.py:633
  252.5 18.5 %collective-permute-start.47 = (bf16[320,768]{1,0:T(8,128)(2,1)S(1)}, bf16[320,768]{1,0:T(8,128)(2,1)S(1)}, u32[]{:S(2)}, u32[]{:S(2)}) collective-permute-start(bf16[320,768]{1,0:T(8,128)(2,1)S(1)} %maximum_select_fusion.15), channel_id=1, source_target_pairs={{0,4},{1,9},{2,6},{3,11},{4,0},{5,13},{6,2},{7,15},{8,12},{9,1},{1... | collective-permute-start | bytes 1474568 | tf_op jit(solution)/shard_map/ppermute | solution.py:633
  260.5 18.6 %collective-permute-start.50 = (bf16[512,768]{1,0:T(8,128)(2,1)S(1)}, bf16[512,768]{1,0:T(8,128)(2,1)S(1)}, u32[]{:S(2)}, u32[]{:S(2)}) collective-permute-start(bf16[512,768]{1,0:T(8,128)(2,1)S(1)} %maximum_select_fusion.11), channel_id=1, source_target_pairs={{0,4},{1,9},{2,6},{3,11},{4,0},{5,13},{6,2},{7,15},{8,12},{9,1},{1... | collective-permute-start | bytes 2359304 | tf_op jit(solution)/shard_map/ppermute | solution.py:633
  (29 other events, 79.7 us)
